TPU v7x, 512 devices: a whole 4x4x16 slice. The times are simulated.
512 devices in a mesh: member: 8 (over y, x_hi), space: 64 (over x_lo, z, core).
Axes of the slice: x: 4 (x_hi: 2, x_lo: 2; x = x_hi * 2 + x_lo), y: 4, z: 16, core: 2. Of those that a mesh axis runs over, the one named last changes fastest.
Arguments:
- latent: bfloat16 [16, 4096, 1024], P('member', 'space'), may hold values from -6 to 6
- edge_weight: float32 [3, 32768], P(None, 'space'), may hold values from 0.1 to 1
- neighbours: int32 [3, 32768], P(None, 'space'), may hold values from 0 to 4095, as said below
- band_rows: int32 [64], P('space'), may hold values from 1 to 512, 24576 in all
- w_in: bfloat16 [1024, 1024], replicated, may hold values from -0.1875 to 0.1875
- w_out: bfloat16 [69, 1024], replicated, may hold values from -0.1875 to 0.1875
- target: float32 [69, 32768], P(None, 'space'), may hold values from -80 to 80
Outputs:
- score: float32 [], replicated
- grad_latent: bfloat16 [16, 4096, 1024], P('member', 'space')
- grad_w_out: float32 [69, 1024], P(None, 'space')
Inputs may be any that keep to these rules, and one draw needn't show every extreme that they name: `neighbours`: the node of an edge at grid slot g lies in latitude band g // 512 or one of the two bands beside it, node band b holding nodes b * 64 to (b + 1) * 64 - 1. Band b holds real grid points in its first band_rows[b] slots and padding after them; some band is full.
All inputs are finite; a program needn't handle non-finite values. No bound on the sum of `band_rows` on one device may be relied on, other than what follows from the above.
Results may differ from a plain program's by a relative error of at most 0.0075.
Values may be sent and summed in bfloat16 or wider, within the bound.
No kernel may reach another device: no remote copies, remote signals or barrier semaphores. Data moves between devices by JAX's collectives and lax.ppermute only.
A program may use at most 64 MiB of HBM per device.

v0:
```python
import jax
import jax.numpy as jnp
from jax import lax
from jax.sharding import PartitionSpec as P

epsilon = 1e-06


def extended_2(array, sides, width):
    for axis, dim in sides:
        size, length = (lax.axis_size(axis), array.shape[dim])
        up = [(i, (i + 1) % size) for i in range(size - 1)]
        down = [(j, i) for i, j in up]
        last = lax.slice_in_dim(array, length - width, length, axis=dim)
        first = lax.slice_in_dim(array, 0, width, axis=dim)
        before = lax.ppermute(last, axis, up)
        after = lax.ppermute(first, axis, down)
        array = jnp.concatenate([before, array, after], axis=dim)
    return array


def passed_along(array, axis, by):
    length = lax.axis_size(axis)
    pairs = [(i, i + by) for i in range(length) if 0 <= i + by < length]
    return lax.ppermute(array, axis, pairs)


def partials(everyone, target_rows, valid_rows):
    deviation = everyone - target_rows[None]
    target_sums = jnp.sum(valid_rows * deviation * deviation, axis=(1, 2))

    def against(member_field):
        spread = everyone - member_field[None]
        return jnp.sum(valid_rows * spread * spread, axis=(1, 2))

    pair_sums = lax.map(against, everyone)
    return (target_sums, pair_sums, jnp.sum(valid_rows))


def finish(target_sums, pair_sums, cell_count, variables):
    members = target_sums.shape[0]
    cells = variables * cell_count
    target_dist = jnp.sqrt(target_sums / cells + epsilon)
    pair_dist = jnp.sqrt(pair_sums / cells + epsilon)
    apart = 1.0 - jnp.eye(members, dtype=jnp.float32)
    pair_coef = apart / pair_dist
    score = jnp.mean(target_dist) - jnp.sum(apart * pair_dist) / (2.0 * members * (members - 1))
    return (score, pair_coef, target_dist)


def member_grads(chosen, everyone, coef_rows, dist_rows, target_rows, valid_rows):
    members = everyone.shape[0]
    others = jnp.sum(coef_rows[:, :, None, None] * everyone[None], axis=1)
    spread = jnp.sum(coef_rows, axis=1)[:, None, None] * chosen - others
    toward = (chosen - target_rows[None]) / (members * dist_rows[:, None, None])
    return (valid_rows * (toward - spread / (members * (members - 1)))).astype(jnp.bfloat16)


def per_device(latent, edge_weight, neighbours, band_rows, w_in, w_out, target):
    members_dev, nodes_dev, latent_width = latent.shape
    neigh_count, row_count = edge_weight.shape
    variables = w_out.shape[0]
    band_index = lax.axis_index("space")
    extended = extended_2(latent, (("space", 1),), nodes_dev)
    local_index = neighbours - (band_index - 1) * nodes_dev
    picked = jnp.take(extended, local_index.reshape(-1), axis=1).reshape(
        members_dev, neigh_count, row_count, latent_width
    )
    aggregated = edge_weight[0][None, :, None] * picked[:, 0].astype(jnp.float32)
    for neighbour in range(1, neigh_count):
        aggregated = aggregated + edge_weight[neighbour][None, :, None] * picked[
            :, neighbour
        ].astype(jnp.float32)
    latent_mix = aggregated.astype(jnp.bfloat16)
    preact = jnp.einsum("mgd,de->mge", latent_mix, w_in, preferred_element_type=jnp.float32)
    hidden = jax.nn.silu(preact).astype(jnp.bfloat16)
    fields = jnp.einsum("vd,mgd->mvg", w_out, hidden, preferred_element_type=jnp.float32).astype(
        jnp.bfloat16
    )
    valid_rows = (jnp.arange(row_count) < band_rows[0]).astype(jnp.float32)
    everyone = lax.all_gather(fields, "member", axis=0, tiled=True).astype(jnp.float32)
    target_sums, pair_sums, cell_count = partials(everyone, target, valid_rows)
    target_sums, pair_sums, cell_count = lax.psum((target_sums, pair_sums, cell_count), "space")
    score, pair_coef, target_dist = finish(target_sums, pair_sums, cell_count, variables)
    first_member = lax.axis_index("member") * members_dev
    coef_rows = lax.dynamic_slice_in_dim(pair_coef, first_member, members_dev, 0)
    dist_rows = lax.dynamic_slice_in_dim(target_dist, first_member, members_dev, 0)
    grad_fields = member_grads(
        fields.astype(jnp.float32), everyone, coef_rows, dist_rows, target, valid_rows
    )
    partial_weight = jnp.einsum(
        "mvg,mgd->vd", grad_fields, hidden, preferred_element_type=jnp.float32
    )
    summed = lax.psum(partial_weight, ("member", "space"))
    column_count = latent_width // lax.axis_size("space")
    grad_w_out = lax.dynamic_slice_in_dim(summed, band_index * column_count, column_count, 1)
    back = jnp.einsum("vd,mvg->mgd", w_out, grad_fields, preferred_element_type=jnp.float32)
    sigmoid_part = jax.nn.sigmoid(preact)
    grad_pre = (back * sigmoid_part * (1.0 + preact * (1.0 - sigmoid_part))).astype(jnp.bfloat16)
    grad_mixed = jnp.einsum("mge,de->mgd", grad_pre, w_in, preferred_element_type=jnp.float32)
    spread_terms = (edge_weight[None, :, :, None] * grad_mixed[:, None]).reshape(
        members_dev, -1, latent_width
    )
    flat_index = local_index.reshape(-1)
    collected = jax.vmap(
        lambda edge_terms: jax.ops.segment_sum(edge_terms, flat_index, num_segments=3 * nodes_dev)
    )(spread_terms)
    lower_rim = collected[:, :nodes_dev].astype(jnp.bfloat16)
    middle_rows = collected[:, nodes_dev : 2 * nodes_dev]
    upper_rim = collected[:, 2 * nodes_dev :].astype(jnp.bfloat16)
    from_above = passed_along(lower_rim, "space", -1)
    from_below = passed_along(upper_rim, "space", 1)
    grad_latent = (
        middle_rows + from_above.astype(jnp.float32) + from_below.astype(jnp.float32)
    ).astype(jnp.bfloat16)
    return (score, grad_latent, grad_w_out)


def solution(mesh):
    return jax.shard_map(
        per_device,
        mesh=mesh,
        in_specs=(
            P("member", "space", None),
            P(None, "space"),
            P(None, "space"),
            P("space"),
            P(),
            P(),
            P(None, "space"),
        ),
        out_specs=(P(), P("member", "space", None), P(None, "space")),
        check_vma=False,
    )
```

profile of v0, /device:TPU:1, one launch (start us, length us, event | category | flops | bytes accessed | tf_op | source)
XLA Modules:
  0.0 1031.5 jit_solution(2826235210925329485)
XLA Ops:
  7.2 1.4 copy.28
  8.6 4.9 collective-permute-start
  13.5 5.2 collective-permute-start.1
  20.3 1.0 collective-permute-done.1
  21.3 2.0 pad_maximum_fusion
  23.4 41.8 %gather_fusion = bf16[1536,2,1024]{2,1,0:T(2,128)(2,1)} fusion(bf16[2,192,1024]{2,0,1:T(2,128)(2,1)S(1)} %pad_maximum_fusion, s32[2048]{0:T(1024)S(1)} %pad_clamp_fusion), kind=kCustom, calls=%fused_computation | custom fusion | bytes 12589056 | tf_op jit(solution)/shard_map/jit(_take)/gather | solution.py:66
  65.2 6.4 copy_select_fusion
  71.6 4.7 multiply_convert_fusion.1
  76.4 1.4 copy-done.2
  77.7 1.4 fusion.16
  80.7 63.6 %all-gather.2.cloned.1.call-done = bf16[16,69,512]{2,1,0:T(8,128)(2,1)} async-done(((bf16[2,69,512]{2,1,0:T(8,128)(2,1)}), bf16[16,69,512]{2,1,0:T(8,128)(2,1)}) %all-gather.2.cloned.1.call-update) | async-done | bytes 1130512 | tf_op jit(solution)/shard_map/all_gather | solution.py:81
  144.3 3.0 convert_element_type.76
  147.4 59.9 %while.11 = (s32[]{:T(128)}, f32[16,16]{1,0:T(8,128)S(1)}, f32[16,69,512]{2,1,0:T(8,128)}, s32[]{:T(128)}, s32[]{:T(128)}, /*index=5*/s32[]{:T(128)}) while((s32[]{:T(128)}, f32[16,16]{1,0:T(8,128)S(1)}, f32[16,69,512]{2,1,0:T(8,128)}, s32[]{:T(128)}, s32[]{:T(128)}, /*index=5*/s32[]{:T(128)}) %tuple.38), condition=%wide.region_7.8_spmd.clone, body=%wide.region_5.7_spmd.clone.sunk | while | flops 2262002 | bytes 2689297 | solution.py:36
  147.4 1.0 dynamic-slice_bitcast_fusion.2
  149.0 2.1 fusion.44
  152.8 2.1 fusion.44
  156.5 2.1 fusion.44
  160.2 2.1 fusion.44
  162.4 0.9 dynamic-slice_bitcast_fusion.2
  164.0 2.1 fusion.44
  166.1 0.9 dynamic-slice_bitcast_fusion.2
  167.7 2.1 fusion.44
  171.5 2.1 fusion.44
  175.2 2.1 fusion.44
  178.9 2.1 fusion.44
  182.7 2.1 fusion.44
  186.4 2.1 fusion.44
  190.2 2.1 fusion.44
  193.9 2.1 fusion.44
  197.6 2.1 fusion.44
  201.4 2.1 fusion.44
  205.1 2.1 fusion.44
  207.3 1.5 fusion.7
  208.7 110.8 %all-reduce = (f32[16]{0:T(128)S(1)}, f32[]{:T(128)}, f32[16,16]{1,0:T(8,128)S(1)}) all-reduce(f32[16]{0:T(128)S(1)} %fusion.7, f32[]{:T(128)} %fusion.30, f32[16,16]{1,0:T(8,128)S(1)} %get-tuple-element.25), channel_id=1, replica_groups=mesh['member'=8,'space'=64] {'space'}, use_global_device_ids=true, to_apply=%region_1.2 | all-reduce | flops 273 | bytes 2184 | tf_op jit(solution)/shard_map/psum | solution.py:83
  322.0 1.1 multiply_reduce_fusion
  323.1 7.9 fusion.10
  331.0 5.4 copy.33
  336.4 10.1 bitcast_multiply_fusion
  346.5 1.6 broadcast_in_dim.23
  348.1 211.4 %scatter_fusion = f32[2,192,1024]{2,0,1:T(2,128)} fusion(f32[2,192,1024]{2,0,1:T(2,128)} %broadcast_in_dim.23, s32[1536]{0:T(1024)S(1)} %reshape.87, f32[1536,2,1024]{2,1,0:T(2,128)} %bitcast.66), kind=kCustom, calls=%fused_computation.1 | custom fusion | flops 3145728 | bytes 37754880 | tf_op jit(solution)/shard_map/vmap()/scatter-add | solution.py:106
  559.5 1.9 convert.7
  561.4 1.1 fusion.34
  562.5 4.5 collective-permute-start.2
  567.0 1.9 collective-permute-start.3
  568.9 3.4 convolution_bitcast_fusion
  573.7 446.4 %all-reduce.3.cloned.1.call-done = f32[69,1024]{0,1:T(8,128)} async-done(((f32[69,1024]{0,1:T(8,128)}), f32[69,1024]{0,1:T(8,128)}) %all-reduce.3.cloned.1.call-update) | async-done | bytes 282640 | tf_op jit(solution)/shard_map/psum | solution.py:94
  1020.1 1.3 constant_dynamic-slice_fusion
  1021.4 1.4 fusion.18
  (79 shorter events, 27.9 us)
Async XLA Ops:
  7.2 64.4 %copy-start = (bf16[1024,1024]{1,0:T(8,128)(2,1)S(1)}, bf16[1024,1024]{1,0:T(8,128)(2,1)}, u32[]{:S(2)}) copy-start(bf16[1024,1024]{1,0:T(8,128)(2,1)} %param.13) | copy-start | bytes 6291460
  7.2 137.2 %all-gather.2.cloned.1.call-start = ((), (), s32[]{:S(2)}) async-start(), calls=%async_computation | async-start | bytes 1327104 | tf_op jit(solution)/shard_map/all_gather | solution.py:81
  8.6 11.7 %collective-permute-start = (bf16[2,64,1024]{2,0,1:T(2,128)(2,1)S(1)}, bf16[2,64,1024]{2,0,1:T(2,128)(2,1)S(1)}, u32[]{:S(2)}, u32[]{:S(2)}) collective-permute-start(bf16[2,64,1024]{2,0,1:T(2,128)(2,1)S(1)} %copy.28), channel_id=1, source_target_pairs={{0,1},{1,2},{2,3},{3,4},{4,5},{5,6},{6,7},{7,8},{8,9},{9,10},{10,1... | collective-permute-start | bytes 786440 | tf_op jit(solution)/shard_map/ppermute | solution.py:16
  13.5 7.8 collective-permute-start.1
  71.6 6.1 copy-start.4
  71.6 7.8 copy-start.5
  76.4 1.4 copy-start.2
  79.2 940.9 %all-reduce.3.cloned.1.call-start = ((), (), s32[]{:S(2)}) async-start(), calls=%async_computation.1 | async-start | bytes 1048576 | tf_op jit(solution)/shard_map/psum | solution.py:94
  147.4 59.9 %copy-start.1 = (bf16[16,69,512]{2,1,0:T(8,128)(2,1)S(1)}, bf16[16,69,512]{2,1,0:T(8,128)(2,1)}, u32[]{:S(2)}) copy-start(bf16[16,69,512]{2,1,0:T(8,128)(2,1)} %all-gather.2.cloned.1.call-done) | copy-start | bytes 3391492
  207.3 115.8 %copy-start.3 = (bf16[2,69,512]{2,1,0:T(8,128)(2,1)S(1)}, bf16[2,69,512]{2,1,0:T(8,128)(2,1)}, u32[]{:S(2)}) copy-start(bf16[2,69,512]{2,1,0:T(8,128)(2,1)} %fusion.16) | copy-start | bytes 423940
  562.5 458.9 %collective-permute-start.2 = (bf16[2,64,1024]{2,0,1:T(2,128)(2,1)}, bf16[2,64,1024]{2,0,1:T(2,128)(2,1)S(1)}, u32[]{:S(2)}, u32[]{:S(2)}) collective-permute-start(bf16[2,64,1024]{2,0,1:T(2,128)(2,1)} %get-tuple-element.68), channel_id=1, source_target_pairs={{1,0},{2,1},{3,2},{4,3},{5,4},{6,5},{7,6},{8,7},{9,8},{10,9},{11,1... | collective-permute-start | bytes 786440 | tf_op jit(solution)/shard_map/ppermute | solution.py:25
  567.0 454.4 %collective-permute-start.3 = (bf16[2,64,1024]{2,0,1:T(2,128)(2,1)S(1)}, bf16[2,64,1024]{2,0,1:T(2,128)(2,1)S(1)}, u32[]{:S(2)}, u32[]{:S(2)}) collective-permute-start(bf16[2,64,1024]{2,0,1:T(2,128)(2,1)S(1)} %get-tuple-element.69), channel_id=1, source_target_pairs={{0,1},{1,2},{2,3},{3,4},{4,5},{5,6},{6,7},{7,8},{8,9},{9,10},{10,1... | collective-permute-start | bytes 786440 | tf_op jit(solution)/shard_map/ppermute | solution.py:25
Sparse Core Ops, SparseCore 0:
  79.3 64.9 all-gather.1
  572.5 447.5 all-reduce.2
where the time goes:
time: 1040 us; the launch traced here: 1030 us
  waiting for transfers between devices  511 us (49%)
  other arithmetic  286 us (28%)
  blocking collectives  111 us (11%)
  local copies, waits for them, and re-layouts  71.2 us (7%)
  between operations  18 us (2%)
  matrix products  17.5 us (2%)
  starting transfers between devices  16.8 us (2%)
    psum x1, waiting for transfers between devices, per_device(): summed = lax.psum(partial_weight, ('member', 'space'))  446 us
    scatter-add x1, other arithmetic, per_device(): jax.ops.segment_sum(edge_terms, flat_index, num_segments=3 * nodes_dev)  211 us
    psum x1, blocking collectives, per_device(): lax.psum((target_sums, pair_sums, cell_count), 'space')  111 us
    all_gather x1, waiting for transfers between devices, per_device(): lax.all_gather(fields, 'member', axis=0, tiled=True).astype(jnp.float32)  63.6 us
    gather x1, local copies, waits for them, and re-layouts, per_device(): jnp.take(extended, local_index.reshape(-1), axis=1)  41.8 us
    reduce_sum x16, other arithmetic, against(): return jnp.sum(valid_rows * spread * spread, axis=(1, 2))  33.9 us
  transfers between devices with their start and end apart: 6, of which 3 were waited for; matrix products, arithmetic and copies ran while one was open for 1% of the time, Pallas kernels for 0%

commit v1 on v0

v1 whole, which is shorter than its diff:
```python
import jax
import jax.numpy as jnp
from jax import lax
from jax.experimental import pallas as pl
from jax.experimental.pallas import tpu as pltpu
from jax.sharding import PartitionSpec as P

epsilon = 1e-06
f32 = jnp.float32
bf16 = jnp.bfloat16
VMEM = pl.BlockSpec(memory_space=pltpu.VMEM)
SMEM = pl.BlockSpec(memory_space=pltpu.SMEM)
NT = (((1,), (1,)), ((), ()))
ROWS = 72
ACROSS = 128


def call(body, outs, specs, scratch=(), limit=24, flops=0, moved=0):
    return pl.pallas_call(
        body,
        out_shape=outs,
        in_specs=specs,
        out_specs=jax.tree.map(lambda _: VMEM, outs),
        scratch_shapes=scratch,
        compiler_params=pltpu.CompilerParams(vmem_limit_bytes=limit << 20),
        cost_estimate=pl.CostEstimate(flops=flops, bytes_accessed=moved, transcendentals=0),
    )


def mixing(neighbours, weight, first_node, rows):
    node = lax.broadcasted_iota(jnp.int32, (rows, neighbours.shape[1]), 0) + first_node
    total = jnp.where(node == neighbours[0:1], weight[0:1], 0.0)
    for k in range(1, neighbours.shape[0]):
        total = total + jnp.where(node == neighbours[k : k + 1], weight[k : k + 1], 0.0)
    return total


def forward(
    place, rows_here, before, own, after, w_in, w_out, neighbours, weight,
    sent, fields, hidden, slope, projected,
):
    members, nodes, _ = before.shape
    slots = neighbours.shape[1]
    step = 128
    first = (place[0] - 1) * nodes
    spread = mixing(neighbours[...], weight[...], first, 4 * nodes).T.astype(bf16)
    for m in range(members):
        projected[m, 0:nodes] = jnp.dot(
            before[m], w_in[...], preferred_element_type=f32
        ).astype(bf16)
        projected[m, nodes : 2 * nodes] = own[m]
        projected[m, 2 * nodes : 3 * nodes] = jnp.dot(
            after[m], w_in[...], preferred_element_type=f32
        ).astype(bf16)
        projected[m, 3 * nodes :] = jnp.zeros_like(own[m])
    slot = lax.broadcasted_iota(jnp.int32, (w_out.shape[0], step), 1)
    for m in range(members):
        for start in range(0, slots, step):
            part = slice(start, start + step)
            preact = jnp.dot(spread[part], projected[m], preferred_element_type=f32)
            gate = 0.5 * jnp.tanh(0.5 * preact) + 0.5
            lit = preact * gate
            out = lit.astype(bf16)
            hidden[m, part] = out
            slope[m, part] = (gate + lit * (1.0 - gate)).astype(bf16)
            decoded = lax.dot_general(w_out[...], out, NT, preferred_element_type=f32)
            fields[m, :, part] = jnp.where(slot + start < rows_here[0], decoded, 0.0).astype(bf16)
    for copy in range(sent.shape[0]):
        sent[copy] = fields[...]


def lanes_of(squares):
    rows, slots = squares.shape
    tall = jnp.sum(squares.reshape(rows // 8, 8, slots), axis=0)
    total = tall[:, 0:128]
    for start in range(128, slots, 128):
        total = total + tall[:, start : start + 128]
    return jnp.sum(total, axis=0, keepdims=True)


def distances(rows_here, everyone, mine, target, sums):
    members = everyone.shape[0]
    lines = []
    for a in range(mine.shape[0]):
        own = mine[a].astype(f32)
        for n in range(members):
            gap = own - everyone[n].astype(f32)
            lines.append(lanes_of(gap * gap))
    for a in range(mine.shape[0]):
        gap = mine[a].astype(f32) - target[...]
        lines.append(lanes_of(gap * gap))
    lines.append(jnp.zeros((128 - len(lines), 128), f32))
    table = jnp.concatenate(lines, axis=0).T
    line = jnp.sum(table, axis=0, keepdims=True)
    lane = lax.broadcasted_iota(jnp.int32, (1, 128), 1)
    line = jnp.where(lane == 127, rows_here[0].astype(f32), line)
    sums[...] = jnp.broadcast_to(line, sums.shape)


def output_grads(variables, place, sums, everyone, mine, target, hidden, grads, weight_grad, share):
    members = everyone.shape[0]
    held = mine.shape[0]
    line = jnp.sum(sums[...], axis=0, keepdims=True)
    lane = lax.broadcasted_iota(jnp.int32, (1, 128), 1)
    cells = variables * line[:, 127:128]
    dist = jnp.sqrt(line / cells + epsilon)
    pairs = held * members
    apart = lane < pairs
    for a in range(held):
        apart = apart & (lane != a * members + place[0] + a)
    coef = jnp.where(apart, 1.0 / dist, 0.0)
    per_target = (lane >= pairs) & (lane < pairs + held)
    share[...] = jnp.sum(
        jnp.where(per_target, dist / members, 0.0)
        - jnp.where(apart, dist / (2.0 * members * (members - 1)), 0.0),
        axis=1, keepdims=True,
    ) + jnp.zeros(share.shape, f32)
    total = None
    for a in range(held):
        chosen = mine[a].astype(f32)
        first = a * members
        reach = jnp.sum(jnp.where((lane >= first) & (lane < first + members), coef, 0.0), axis=1, keepdims=True)
        others = coef[:, first : first + 1] * everyone[0].astype(f32)
        for n in range(1, members):
            others = others + coef[:, first + n : first + n + 1] * everyone[n].astype(f32)
        toward = (chosen - target[...]) * (1.0 / (members * dist[:, pairs + a : pairs + a + 1]))
        grad = (toward - (reach * chosen - others) * (1.0 / (members * (members - 1)))).astype(bf16)
        grads[a] = grad
        part = jnp.dot(grad, hidden[a], preferred_element_type=f32)
        total = part if total is None else total + part
    tall = jnp.concatenate([total, jnp.zeros((ACROSS - total.shape[0], total.shape[1]), f32)], axis=0)
    weight_grad[...] = tall.T.astype(bf16).reshape(weight_grad.shape)


def backward(place, grads, w_out, slope, neighbours, weight, below, middle, above):
    held, nodes, _ = middle.shape
    first = (place[0] - 1) * nodes
    slots = neighbours.shape[1]
    step = 128
    spread = mixing(neighbours[...], weight[...], first, 3 * nodes).astype(bf16)
    for m in range(held):
        total = None
        lines = grads[m].astype(f32).T.astype(bf16)
        for start in range(0, slots, step):
            part = slice(start, start + step)
            back = jnp.dot(lines[part], w_out[...], preferred_element_type=f32)
            grad_pre = (back * slope[m, part].astype(f32)).astype(bf16)
            term = jnp.dot(spread[:, part], grad_pre, preferred_element_type=f32)
            total = term if total is None else total + term
        below[m] = total[:nodes].astype(bf16)
        middle[m] = total[nodes : 2 * nodes]
        above[m] = total[2 * nodes :].astype(bf16)


def node_grads(middle, from_above, from_below, w_in, out):
    for m in range(out.shape[0]):
        total = middle[m] + from_above[m].astype(f32) + from_below[m].astype(f32)
        out[m] = lax.dot_general(
            total.astype(bf16), w_in[...], NT, preferred_element_type=f32
        ).astype(bf16)


def gathered_sum(parts, share, out):
    total = jnp.sum(parts[...].astype(f32), axis=0)
    lane = lax.broadcasted_iota(jnp.int32, total.shape, 1)
    total = jnp.where(lane == ACROSS - 1, share[0:1, 0:1], total)
    out[...] = jnp.broadcast_to(total[None], out.shape)


def last_sum(parts, weight_grad, score):
    total = parts[0]
    for k in range(1, parts.shape[0]):
        total = total + parts[k]
    short = max(128 - total.shape[0], 0)
    tall = jnp.pad(total, ((0, short), (0, 0)))
    weight_grad[...] = tall.T[: weight_grad.shape[0], : weight_grad.shape[1]]
    score[...] = total[0:1, ACROSS - 1 :]


def per_device(latent, edge_weight, neighbours, band_rows, w_in, w_out, target):
    members_dev, nodes, width = latent.shape
    slots = edge_weight.shape[1]
    variables = w_out.shape[0]
    groups, bands = lax.axis_size("member"), lax.axis_size("space")
    members = groups * members_dev
    band = lax.axis_index("space").astype(jnp.int32)
    group = lax.axis_index("member").astype(jnp.int32)
    up = [(i, i + 1) for i in range(bands - 1)]
    down = [(i + 1, i) for i in range(bands - 1)]
    before = lax.ppermute(latent, "space", up)
    after = lax.ppermute(latent, "space", down)
    own = jnp.dot(
        latent.reshape(members_dev * nodes, width), w_in, preferred_element_type=f32
    ).astype(bf16).reshape(latent.shape)
    w_rows = jnp.pad(w_out, ((0, ROWS - variables), (0, 0)))
    real = jnp.arange(slots) < band_rows[0]
    masked = jnp.where(real[None], jnp.pad(target, ((0, ROWS - variables), (0, 0))), 0.0)
    where = band.reshape(1)

    shape = jax.ShapeDtypeStruct
    big = (members_dev, slots, width)
    decoded = (members_dev, ROWS, slots)
    sent, fields, hidden, slope = call(
        forward,
        (shape((groups, *decoded), bf16), shape(decoded, bf16), shape(big, bf16), shape(big, bf16)),
        [SMEM, SMEM] + [VMEM] * 7,
        [pltpu.VMEM((members_dev, 4 * nodes, width), bf16)],
        limit=32, flops=1 << 30, moved=8 << 20,
    )(where, band_rows, before, own, after, w_in, w_rows, neighbours, edge_weight)

    everyone = lax.all_to_all(sent, "member", 0, 0, tiled=True).reshape(members, ROWS, slots)
    mine_at = group * members_dev

    sums = call(
        distances, shape((bands, 128), f32), [SMEM] + [VMEM] * 3, flops=1 << 22, moved=2 << 20
    )(band_rows, everyone, fields, masked)
    sums = lax.all_to_all(sums, "space", 0, 0, tiled=True)

    columns = width // bands

    def grads_body(*refs):
        output_grads(variables, *refs)

    grads, weight_parts, share = call(
        grads_body,
        (shape(decoded, bf16), shape((bands, columns, ACROSS), bf16), shape((8, 128), f32)),
        [SMEM] + [VMEM] * 5, flops=1 << 28, moved=4 << 20,
    )(mine_at.reshape(1), sums, everyone, fields, masked, hidden)
    weight_parts = lax.all_to_all(weight_parts, "space", 0, 0, tiled=True)

    small = (members_dev, nodes, width)
    lower, middle, upper = call(
        backward,
        (shape(small, bf16), shape(small, f32), shape(small, bf16)),
        [SMEM] + [VMEM] * 5, flops=1 << 29, moved=4 << 20,
    )(where, grads, w_rows, slope, neighbours, edge_weight)
    from_above = lax.ppermute(lower, "space", down)
    from_below = lax.ppermute(upper, "space", up)
    grad_latent = call(
        node_grads, shape(small, bf16), [VMEM] * 4, flops=1 << 28, moved=4 << 20
    )(middle, from_above, from_below, w_in)

    total = call(
        gathered_sum, shape((groups, columns, ACROSS), f32), [VMEM] * 2, flops=1 << 18, moved=1 << 18
    )(weight_parts, share)
    total = lax.all_to_all(total, "member", 0, 0, tiled=True)
    grad_w_out, score = call(
        last_sum, (shape((variables, columns), f32), shape((1, 1), f32)), [VMEM], flops=1 << 16, moved=1 << 16
    )(total)
    return (score.reshape(()), grad_latent, grad_w_out)


def solution(mesh):
    return jax.shard_map(
        per_device,
        mesh=mesh,
        in_specs=(
            P("member", "space", None),
            P(None, "space"),
            P(None, "space"),
            P("space"),
            P(),
            P(),
            P(None, "space"),
        ),
        out_specs=(P(), P("member", "space", None), P(None, "space")),
        check_vma=False,
    )
```

time: 1040 us -> 123 us (0.12)
  waiting for transfers between devices: 511 us -> 44.4 us
  other arithmetic: 286 us -> 0.93 us
  blocking collectives: 111 us -> 0 us
  local copies, waits for them, and re-layouts: 71.2 us -> 14.1 us
  starting transfers between devices: 16.8 us -> 47.1 us
  between operations: 18 us -> 1.51 us
  matrix products: 17.5 us -> 2.18 us
  Pallas kernels: 0 us -> 12.2 us
    psum x1 -> x0, waiting for transfers between devices: 446 us -> none  [per_device(): summed = lax.psum(partial_weight, ('member', 'space'))]
    scatter-add x1 -> x0, other arithmetic: 211 us -> none  [per_device(): jax.ops.segment_sum(edge_terms, flat_index, num_segments=3 * nodes_dev)]
    psum x1 -> x0, blocking collectives: 111 us -> none  [per_device(): lax.psum((target_sums, pair_sums, cell_count), 'space')]
    all_gather x1 -> x0, waiting for transfers between devices: 63.6 us -> none  [per_device(): lax.all_gather(fields, 'member', axis=0, tiled=True).astype(jnp.float32)]
    all_to_all x0 -> x4, waiting for transfers between devices: none -> 44.4 us  [the longest x1 15.7 us: per_device(): lax.all_to_all(sent, 'member', 0, 0, tiled=True)]
    gather x1 -> x0, local copies, waits for them, and re-layouts: 41.8 us -> none  [per_device(): jnp.take(extended, local_index.reshape(-1), axis=1)]
    reduce_sum x22 -> x0, other arithmetic: 38.4 us -> none  [the longest x16 33.9 us: against(): return jnp.sum(valid_rows * spread * spread, axis=(1, 2))]
    all_to_all x0 -> x4, starting transfers between devices: none -> 31.3 us  [the longest x1 17.7 us: per_device(): sums = lax.all_to_all(sums, 'space', 0, 0, tiled=True)]
  transfers between devices with their start and end apart: 6 -> 8, of which waited for: 3 -> 4; matrix products, arithmetic and copies ran while one was open for 1% -> 3% of each run, Pallas kernels for 0% -> 5%
where the time goes in v1:
time: 123 us; the launch traced here: 122 us
  starting transfers between devices  47.1 us (38%)
  waiting for transfers between devices  44.4 us (36%)
  local copies, waits for them, and re-layouts  14.1 us (11%)
  Pallas kernels  12.2 us (10%)
  matrix products  2.18 us (2%)
  between operations  1.51 us (1%)
    all_to_all x1, starting transfers between devices, per_device(): sums = lax.all_to_all(sums, 'space', 0, 0, tiled=True)  17.7 us
    all_to_all x1, waiting for transfers between devices, per_device(): lax.all_to_all(sent, 'member', 0, 0, tiled=True)  15.7 us
    all_to_all x1, waiting for transfers between devices, per_device(): sums = lax.all_to_all(sums, 'space', 0, 0, tiled=True)  13.3 us
    unnamed x33, local copies, waits for them, and re-layouts  13.2 us
    all_to_all x1, waiting for transfers between devices, per_device(): weight_parts = lax.all_to_all(weight_parts, 'space', 0, 0, tiled=True)  10.4 us
    all_to_all x1, starting transfers between devices, per_device(): lax.all_to_all(sent, 'member', 0, 0, tiled=True)  5.58 us
    ppermute x1, starting transfers between devices, per_device(): after = lax.ppermute(latent, 'space', down)  5.16 us
    ppermute x1, starting transfers between devices, per_device(): before = lax.ppermute(latent, 'space', up)  5.07 us
  transfers between devices with their start and end apart: 8, of which 4 were waited for; matrix products, arithmetic and copies ran while one was open for 3% of the time, Pallas kernels for 5%

profile of v1, /device:TPU:1, one launch (start us, length us, event | category | flops | bytes accessed | tf_op | source)
XLA Modules:
  0.0 122.5 jit_solution(17373295562697887938)
XLA Ops:
  0.6 0.0 copy-start
  0.6 0.0 copy-start.15
  0.7 0.0 copy-start.14
  0.7 5.1 %collective-permute-start = (bf16[2,64,1024]{2,1,0:T(8,128)(2,1)}, bf16[2,64,1024]{2,1,0:T(8,128)(2,1)S(1)}, u32[]{:S(2)}, u32[]{:S(2)}) collective-permute-start(bf16[2,64,1024]{2,1,0:T(8,128)(2,1)} %param.7), channel_id=1, source_target_pairs={{0,1},{1,2},{2,3},{3,4},{4,5},{5,6},{6,7},{7,8},{8,9},{9,10},{10,1... | collective-permute-start | bytes 786440 | tf_op jit(solution)/shard_map/ppermute | solution.py:190
  5.7 5.2 %collective-permute-start.1 = (bf16[2,64,1024]{2,1,0:T(8,128)(2,1)}, bf16[2,64,1024]{2,1,0:T(8,128)(2,1)S(1)}, u32[]{:S(2)}, u32[]{:S(2)}) collective-permute-start(bf16[2,64,1024]{2,1,0:T(8,128)(2,1)} %param.7), channel_id=1, source_target_pairs={{1,0},{2,1},{3,2},{4,3},{5,4},{6,5},{7,6},{8,7},{9,8},{10,9},{11,1... | collective-permute-start | bytes 786440 | tf_op jit(solution)/shard_map/ppermute | solution.py:191
  11.6 0.9 pad.8.w_out
  12.5 0.0 copy-start.6
  12.5 2.2 %convolution_convert_fusion = bf16[128,1024]{1,0:T(8,128)(2,1)S(1)} fusion(bf16[128,1024]{1,0:T(8,128)(2,1)} %bitcast.18, bf16[1024,1024]{1,0:T(8,128)(2,1)} %w_in.3), kind=kOutput, calls=%fused_computation | convolution fusion | flops 268566528 | bytes 2621440 | tf_op jit(solution)/shard_map/dot_general | solution.py:192
  14.7 0.0 collective-permute-done.before
  14.7 0.0 collective-permute-done.1.after
  14.7 0.0 copy-done
  14.7 0.0 copy-done.15
  14.7 0.0 copy-done.14
  14.7 3.4 %shard_map.94 = (bf16[8,2,72,512]{3,2,1,0:T(8,128)(2,1)S(1)}, bf16[2,72,512]{2,1,0:T(8,128)(2,1)S(1)}, bf16[2,512,1024]{2,1,0:T(8,128)(2,1)S(1)}, bf16[2,512,1024]{2,1,0:T(8,128)(2,1)S(1)}) custom-call(s32[1]{0:T(128)} %bitcast.1.place, s32[1]{0:T(128)} %copy.13.rows_here, bf16[2,64,1024]{2,1,0:T(8,128)(2,1)S(1)} %collective-permute-done.before, ...), custom_call_target="tpu_custom_call" | custom-call | flops 1073741824 | bytes 8388608 | tf_op jit(solution)/shard_map/pallas_call | solution.py:203
  18.1 0.0 copy-done.6
  18.2 1.3 %copy-done.1 = bf16[2,512,1024]{2,1,0:T(8,128)(2,1)} copy-done((bf16[2,512,1024]{2,1,0:T(8,128)(2,1)}, bf16[2,512,1024]{2,1,0:T(8,128)(2,1)S(1)}, u32[]{:S(2)}) %copy-start.1) | copy-done | bytes 2097176
  19.5 1.3 %copy-done.3 = bf16[2,512,1024]{2,1,0:T(8,128)(2,1)} copy-done((bf16[2,512,1024]{2,1,0:T(8,128)(2,1)}, bf16[2,512,1024]{2,1,0:T(8,128)(2,1)S(1)}, u32[]{:S(2)}) %copy-start.3) | copy-done | bytes 2097176
  20.8 1.1 copy-done.5
  21.9 0.7 copy-done.8
  22.5 5.6 %all-to-all-start = ((bf16[8,2,72,512]{3,2,1,0:T(8,128)(2,1)}), bf16[8,2,72,512]{3,2,1,0:T(8,128)(2,1)S(1)}, u32[]{:S(2)}, u32[]{:S(2)}) async-start(bf16[8,2,72,512]{3,2,1,0:T(8,128)(2,1)} %copy-done.5), calls=%async_computation | async-start | bytes 2359296 | tf_op jit(solution)/shard_map/all_to_all | solution.py:211
  28.1 0.9 pad_select_fusion.target.refs_4_
  29.0 15.7 %all-to-all-done = bf16[8,2,72,512]{3,2,1,0:T(8,128)(2,1)S(1)} async-done(((bf16[8,2,72,512]{3,2,1,0:T(8,128)(2,1)}), bf16[8,2,72,512]{3,2,1,0:T(8,128)(2,1)S(1)}, u32[]{:S(2)}, u32[]{:S(2)}) %all-to-all-start) | async-done | bytes 1179680 | tf_op jit(solution)/shard_map/all_to_all | solution.py:211
  44.7 0.9 copy-done.9
  45.7 1.4 %shard_map.95 = f32[64,128]{1,0:T(8,128)} custom-call(s32[1]{0:T(128)} %copy.13.rows_here, bf16[16,72,512]{2,1,0:T(8,128)(2,1)S(1)} %bitcast.14, bf16[2,72,512]{2,1,0:T(8,128)(2,1)S(1)} %copy-done.9, f32[72,512]{1,0:T(8,128)S(1)} %pad_select_fusion.target.refs_4_), custom_call_target="tpu_custom_call" | custom-call | flops 4194304 | bytes 2097152 | tf_op jit(solution)/shard_map/pallas_call | solution.py:214
  47.0 17.7 %all-to-all-start.1 = ((f32[64,1,128]{2,1,0:T(1,128)}), f32[64,1,128]{2,1,0:T(1,128)S(1)}, u32[]{:S(2)}, u32[]{:S(2)}) async-start(f32[64,1,128]{2,1,0:T(1,128)} %bitcast.7), calls=%async_computation.1 | async-start | bytes 65536 | tf_op jit(solution)/shard_map/all_to_all | solution.py:217
  64.8 13.3 %all-to-all-done.1 = f32[64,1,128]{2,1,0:T(1,128)S(1)} async-done(((f32[64,1,128]{2,1,0:T(1,128)}), f32[64,1,128]{2,1,0:T(1,128)S(1)}, u32[]{:S(2)}, u32[]{:S(2)}) %all-to-all-start.1) | async-done | bytes 32800 | tf_op jit(solution)/shard_map/all_to_all | solution.py:217
  78.1 1.6 %copy-done.4 = bf16[2,512,1024]{2,1,0:T(8,128)(2,1)S(1)} copy-done((bf16[2,512,1024]{2,1,0:T(8,128)(2,1)S(1)}, bf16[2,512,1024]{2,1,0:T(8,128)(2,1)}, u32[]{:S(2)}) %copy-start.4) | copy-done | bytes 2097176
  79.7 0.9 copy-done.10
  80.6 1.1 shard_map.96
  81.7 0.0 copy-start.11
  81.7 0.7 copy-done.11
  82.4 0.6 copy-done.12
  83.0 4.6 %all-to-all-start.2 = ((bf16[64,16,128]{2,1,0:T(8,128)(2,1)}), bf16[64,16,128]{2,1,0:T(8,128)(2,1)S(1)}, u32[]{:S(2)}, u32[]{:S(2)}) async-start(bf16[64,16,128]{2,1,0:T(8,128)(2,1)} %copy-done.11), calls=%async_computation.2 | async-start | bytes 524288 | tf_op jit(solution)/shard_map/all_to_all | solution.py:229
  87.7 1.6 %copy-done.2 = bf16[2,512,1024]{2,1,0:T(8,128)(2,1)S(1)} copy-done((bf16[2,512,1024]{2,1,0:T(8,128)(2,1)S(1)}, bf16[2,512,1024]{2,1,0:T(8,128)(2,1)}, u32[]{:S(2)}) %copy-start.2) | copy-done | bytes 2097176
  89.3 0.9 copy-done.7
  90.2 0.9 copy-done.13
  91.1 3.0 %shard_map.99 = (bf16[2,64,1024]{2,1,0:T(8,128)(2,1)}, f32[2,64,1024]{2,1,0:T(8,128)S(1)}, bf16[2,64,1024]{2,1,0:T(8,128)(2,1)}) custom-call(s32[1]{0:T(128)} %bitcast.1.place, bf16[2,72,512]{2,1,0:T(8,128)(2,1)S(1)} %copy-done.13, bf16[72,1024]{1,0:T(8,128)(2,1)S(1)} %copy-done.7, bf16[2,512,1024]{2,1,0:T(8,128)(2,1)S(1)} %copy-done.2, ...), custom_call_target="tpu_custom_call" | custom-call | flops 536870912 | bytes 4194304 | tf_op jit(solution)/shard_map/pallas_call | solution.py:232
  94.1 2.5 %collective-permute-start.2 = (bf16[2,64,1024]{2,1,0:T(8,128)(2,1)}, bf16[2,64,1024]{2,1,0:T(8,128)(2,1)S(1)}, u32[]{:S(2)}, u32[]{:S(2)}) collective-permute-start(bf16[2,64,1024]{2,1,0:T(8,128)(2,1)} %get-tuple-element.24), channel_id=1, source_target_pairs={{1,0},{2,1},{3,2},{4,3},{5,4},{6,5},{7,6},{8,7},{9,8},{10,9},{11,1... | collective-permute-start | bytes 786440 | tf_op jit(solution)/shard_map/ppermute | solution.py:237
  96.6 3.1 %collective-permute-start.3 = (bf16[2,64,1024]{2,1,0:T(8,128)(2,1)}, bf16[2,64,1024]{2,1,0:T(8,128)(2,1)S(1)}, u32[]{:S(2)}, u32[]{:S(2)}) collective-permute-start(bf16[2,64,1024]{2,1,0:T(8,128)(2,1)} %get-tuple-element.25), channel_id=1, source_target_pairs={{0,1},{1,2},{2,3},{3,4},{4,5},{5,6},{6,7},{7,8},{8,9},{9,10},{10,1... | collective-permute-start | bytes 786440 | tf_op jit(solution)/shard_map/ppermute | solution.py:238
  99.6 10.4 %all-to-all-done.2.parts = bf16[64,16,128]{2,1,0:T(8,128)(2,1)S(1)} async-done(((bf16[64,16,128]{2,1,0:T(8,128)(2,1)}), bf16[64,16,128]{2,1,0:T(8,128)(2,1)S(1)}, u32[]{:S(2)}, u32[]{:S(2)}) %all-to-all-start.2) | async-done | bytes 262176 | tf_op jit(solution)/shard_map/all_to_all | solution.py:229
  110.0 0.7 shard_map.97
  110.7 3.3 %all-to-all-start.3 = ((f32[8,16,128]{2,1,0:T(8,128)}), f32[8,16,128]{2,1,0:T(8,128)S(1)}, u32[]{:S(2)}, u32[]{:S(2)}) async-start(f32[8,16,128]{2,1,0:T(8,128)} %shard_map.97), calls=%async_computation.3 | async-start | bytes 131072 | tf_op jit(solution)/shard_map/all_to_all | solution.py:246
  114.1 0.0 collective-permute-done.2.from_above
  114.1 0.0 collective-permute-done.3.from_below
  114.1 2.1 %shard_map.100 = bf16[2,64,1024]{2,1,0:T(8,128)(2,1)} custom-call(f32[2,64,1024]{2,1,0:T(8,128)S(1)} %get-tuple-element.23.middle, bf16[2,64,1024]{2,1,0:T(8,128)(2,1)S(1)} %collective-permute-done.2.from_above, bf16[2,64,1024]{2,1,0:T(8,128)(2,1)S(1)} %collective-permute-done.3.from_below, bf16[1024,1024]{1,0:T(8,128)(2,1)S(1)} %copy-done), custom_call_target="tpu_custom_call" | custom-call | flops 268435456 | bytes 4194304 | tf_op jit(solution)/shard_map/pallas_call | solution.py:239
  116.2 5.0 %all-to-all-done.3.parts = f32[8,16,128]{2,1,0:T(8,128)S(1)} async-done(((f32[8,16,128]{2,1,0:T(8,128)}), f32[8,16,128]{2,1,0:T(8,128)S(1)}, u32[]{:S(2)}, u32[]{:S(2)}) %all-to-all-start.3) | async-done | bytes 65568 | tf_op jit(solution)/shard_map/all_to_all | solution.py:246
  121.2 0.6 shard_map.98
  121.8 0.7 copy.12
  (12 shorter events, 0.0 us)
Async XLA Ops:
  0.6 14.1 %copy-start = (bf16[1024,1024]{1,0:T(8,128)(2,1)S(1)}, bf16[1024,1024]{1,0:T(8,128)(2,1)}, u32[]{:S(2)}) copy-start(bf16[1024,1024]{1,0:T(8,128)(2,1)} %w_in.3) | copy-start | bytes 6291460
  0.6 14.1 %copy-start.15 = (f32[3,512]{1,0:T(4,128)S(1)}, f32[3,512]{1,0:T(4,128)}, u32[]{:S(2)}) copy-start(f32[3,512]{1,0:T(4,128)} %weight.3) | copy-start | bytes 18436
  0.7 14.1 %copy-start.14 = (s32[3,512]{1,0:T(4,128)S(1)}, s32[3,512]{1,0:T(4,128)}, u32[]{:S(2)}) copy-start(s32[3,512]{1,0:T(4,128)} %neighbours.3) | copy-start | bytes 18436
  0.7 14.0 %collective-permute-start = (bf16[2,64,1024]{2,1,0:T(8,128)(2,1)}, bf16[2,64,1024]{2,1,0:T(8,128)(2,1)S(1)}, u32[]{:S(2)}, u32[]{:S(2)}) collective-permute-start(bf16[2,64,1024]{2,1,0:T(8,128)(2,1)} %param.7), channel_id=1, source_target_pairs={{0,1},{1,2},{2,3},{3,4},{4,5},{5,6},{6,7},{7,8},{8,9},{9,10},{10,1... | collective-permute-start | bytes 786440 | tf_op jit(solution)/shard_map/ppermute | solution.py:190
  5.7 9.0 %collective-permute-start.1 = (bf16[2,64,1024]{2,1,0:T(8,128)(2,1)}, bf16[2,64,1024]{2,1,0:T(8,128)(2,1)S(1)}, u32[]{:S(2)}, u32[]{:S(2)}) collective-permute-start(bf16[2,64,1024]{2,1,0:T(8,128)(2,1)} %param.7), channel_id=1, source_target_pairs={{1,0},{2,1},{3,2},{4,3},{5,4},{6,5},{7,6},{8,7},{9,8},{10,9},{11,1... | collective-permute-start | bytes 786440 | tf_op jit(solution)/shard_map/ppermute | solution.py:191
  12.5 5.7 %copy-start.6 = (bf16[72,1024]{1,0:T(8,128)(2,1)}, bf16[72,1024]{1,0:T(8,128)(2,1)S(1)}, u32[]{:S(2)}) copy-start(bf16[72,1024]{1,0:T(8,128)(2,1)S(1)} %pad.8.w_out) | copy-start | bytes 442372
  18.1 1.3 %copy-start.1 = (bf16[2,512,1024]{2,1,0:T(8,128)(2,1)}, bf16[2,512,1024]{2,1,0:T(8,128)(2,1)S(1)}, u32[]{:S(2)}) copy-start(bf16[2,512,1024]{2,1,0:T(8,128)(2,1)S(1)} %get-tuple-element.22.slope) | copy-start | bytes 6291460
  19.5 1.3 %copy-start.3 = (bf16[2,512,1024]{2,1,0:T(8,128)(2,1)}, bf16[2,512,1024]{2,1,0:T(8,128)(2,1)S(1)}, u32[]{:S(2)}) copy-start(bf16[2,512,1024]{2,1,0:T(8,128)(2,1)S(1)} %get-tuple-element.17.refs_5_) | copy-start | bytes 6291460
  20.8 1.1 copy-start.5
  21.9 0.7 copy-start.8
  22.5 22.2 %all-to-all-start = ((bf16[8,2,72,512]{3,2,1,0:T(8,128)(2,1)}), bf16[8,2,72,512]{3,2,1,0:T(8,128)(2,1)S(1)}, u32[]{:S(2)}, u32[]{:S(2)}) async-start(bf16[8,2,72,512]{3,2,1,0:T(8,128)(2,1)} %copy-done.5), calls=%async_computation | async-start | bytes 2359296 | tf_op jit(solution)/shard_map/all_to_all | solution.py:211
  44.7 0.9 copy-start.9
  47.0 31.1 %all-to-all-start.1 = ((f32[64,1,128]{2,1,0:T(1,128)}), f32[64,1,128]{2,1,0:T(1,128)S(1)}, u32[]{:S(2)}, u32[]{:S(2)}) async-start(f32[64,1,128]{2,1,0:T(1,128)} %bitcast.7), calls=%async_computation.1 | async-start | bytes 65536 | tf_op jit(solution)/shard_map/all_to_all | solution.py:217
  78.1 1.6 %copy-start.4 = (bf16[2,512,1024]{2,1,0:T(8,128)(2,1)S(1)}, bf16[2,512,1024]{2,1,0:T(8,128)(2,1)}, u32[]{:S(2)}) copy-start(bf16[2,512,1024]{2,1,0:T(8,128)(2,1)} %copy-done.3) | copy-start | bytes 6291460
  79.7 0.9 copy-start.10
  81.7 0.7 copy-start.11
  82.4 0.7 copy-start.12
  83.0 27.0 %all-to-all-start.2 = ((bf16[64,16,128]{2,1,0:T(8,128)(2,1)}), bf16[64,16,128]{2,1,0:T(8,128)(2,1)S(1)}, u32[]{:S(2)}, u32[]{:S(2)}) async-start(bf16[64,16,128]{2,1,0:T(8,128)(2,1)} %copy-done.11), calls=%async_computation.2 | async-start | bytes 524288 | tf_op jit(solution)/shard_map/all_to_all | solution.py:229
  87.7 1.6 %copy-start.2 = (bf16[2,512,1024]{2,1,0:T(8,128)(2,1)S(1)}, bf16[2,512,1024]{2,1,0:T(8,128)(2,1)}, u32[]{:S(2)}) copy-start(bf16[2,512,1024]{2,1,0:T(8,128)(2,1)} %copy-done.1) | copy-start | bytes 6291460
  89.3 0.9 copy-start.7
  90.2 0.9 copy-start.13
  94.1 20.0 %collective-permute-start.2 = (bf16[2,64,1024]{2,1,0:T(8,128)(2,1)}, bf16[2,64,1024]{2,1,0:T(8,128)(2,1)S(1)}, u32[]{:S(2)}, u32[]{:S(2)}) collective-permute-start(bf16[2,64,1024]{2,1,0:T(8,128)(2,1)} %get-tuple-element.24), channel_id=1, source_target_pairs={{1,0},{2,1},{3,2},{4,3},{5,4},{6,5},{7,6},{8,7},{9,8},{10,9},{11,1... | collective-permute-start | bytes 786440 | tf_op jit(solution)/shard_map/ppermute | solution.py:237
  96.6 17.6 %collective-permute-start.3 = (bf16[2,64,1024]{2,1,0:T(8,128)(2,1)}, bf16[2,64,1024]{2,1,0:T(8,128)(2,1)S(1)}, u32[]{:S(2)}, u32[]{:S(2)}) collective-permute-start(bf16[2,64,1024]{2,1,0:T(8,128)(2,1)} %get-tuple-element.25), channel_id=1, source_target_pairs={{0,1},{1,2},{2,3},{3,4},{4,5},{5,6},{6,7},{7,8},{8,9},{9,10},{10,1... | collective-permute-start | bytes 786440 | tf_op jit(solution)/shard_map/ppermute | solution.py:238
  110.7 10.5 %all-to-all-start.3 = ((f32[8,16,128]{2,1,0:T(8,128)}), f32[8,16,128]{2,1,0:T(8,128)S(1)}, u32[]{:S(2)}, u32[]{:S(2)}) async-start(f32[8,16,128]{2,1,0:T(8,128)} %shard_map.97), calls=%async_computation.3 | async-start | bytes 131072 | tf_op jit(solution)/shard_map/all_to_all | solution.py:246

commit v2 on v1

v2 whole, which is shorter than its diff:
```python
import jax
import jax.numpy as jnp
from jax import lax
from jax.experimental import pallas as pl
from jax.experimental.pallas import tpu as pltpu
from jax.sharding import PartitionSpec as P

epsilon = 1e-06
f32 = jnp.float32
bf16 = jnp.bfloat16
VMEM = pl.BlockSpec(memory_space=pltpu.VMEM)
SMEM = pl.BlockSpec(memory_space=pltpu.SMEM)
NT = (((1,), (1,)), ((), ()))
ROWS = 72
ACROSS = 128


HBM = pl.BlockSpec(memory_space=pltpu.HBM)


def call(body, outs, specs, out_specs, scratch=(), room=24 << 10, flops=0, moved=0):
    return pl.pallas_call(
        body,
        out_shape=outs,
        in_specs=specs,
        out_specs=out_specs,
        scratch_shapes=scratch,
        compiler_params=pltpu.CompilerParams(vmem_limit_bytes=room << 10),
        cost_estimate=pl.CostEstimate(flops=flops, bytes_accessed=moved, transcendentals=0),
    )


def mixing(neighbours, weight, first_node, rows):
    node = lax.broadcasted_iota(jnp.int32, (rows, neighbours.shape[1]), 0) + first_node
    total = jnp.where(node == neighbours[0:1], weight[0:1], 0.0)
    for k in range(1, neighbours.shape[0]):
        total = total + jnp.where(node == neighbours[k : k + 1], weight[k : k + 1], 0.0)
    return total


def forward(
    place, rows_here, before, own, after, w_in, w_out, neighbours, weight,
    sent, hidden, slope,
    weights, latents, projected, w_rows, decoded, lit_held, slope_held, w_sems, lit_sems, slope_sems, sent_sems,
):
    members, nodes, width = own.shape
    slots = neighbours.shape[1]
    loads = []
    pieces = w_sems.shape[0]
    for index in range(pieces):
        part = slice(index * (width // pieces), (index + 1) * (width // pieces))
        load = pltpu.make_async_copy(w_in.at[part], weights.at[part], w_sems.at[index])
        load.start()
        loads.append(load)
    step = 128
    first = (place[0] - 1) * nodes
    around = 3 * nodes
    spread = mixing(neighbours[...], weight[...], first, around)
    spread = jnp.concatenate([spread, spread], axis=0).T.astype(bf16)
    for m in range(members):
        for k, source in enumerate((before, own, after)):
            latents[m * around + k * nodes : m * around + (k + 1) * nodes] = source[m]
    for load in loads:
        load.wait()
    whole = jnp.dot(latents[...], weights[...], preferred_element_type=f32)
    high = whole.astype(bf16)
    low = (whole - high.astype(f32)).astype(bf16)
    for m in range(members):
        projected[m, :around] = high[m * around : (m + 1) * around]
        projected[m, around:] = low[m * around : (m + 1) * around]
    variables = w_out.shape[0]
    w_rows[64:ROWS] = jnp.zeros((ROWS - 64, width), f32)
    w_rows[0:variables] = w_out[...].astype(f32)
    rows = w_rows[...].astype(bf16)
    slot = lax.broadcasted_iota(jnp.int32, (ROWS, step), 1)
    copies = []
    for m in range(members):
        for index, start in enumerate(range(0, slots, step)):
            part = slice(start, start + step)
            preact = jnp.dot(spread[part], projected[m], preferred_element_type=f32)
            gate = 0.5 * jnp.tanh(0.5 * preact) + 0.5
            lit = preact * gate
            out = lit.astype(bf16)
            lit_held[m, part] = out
            slope_held[m, part] = (gate + lit * (1.0 - gate)).astype(bf16)
            for held, target, sems in ((lit_held, hidden, lit_sems), (slope_held, slope, slope_sems)):
                copy = pltpu.make_async_copy(held.at[m, part], target.at[m, part], sems.at[m, index])
                copy.start()
                copies.append(copy)
            fields = lax.dot_general(rows, out, NT, preferred_element_type=f32)
            decoded[m, :, part] = jnp.where(slot + start < rows_here[0], fields, 0.0).astype(bf16)
        for k in range(sent.shape[0]):
            copy = pltpu.make_async_copy(decoded.at[m], sent.at[k, m], sent_sems.at[m, k])
            copy.start()
            copies.append(copy)
    for copy in copies:
        copy.wait()


def lanes_of(squares):
    rows, slots = squares.shape
    tall = jnp.sum(squares.reshape(rows // 8, 8, slots), axis=0)
    total = tall[:, 0:128]
    for start in range(128, slots, 128):
        total = total + tall[:, start : start + 128]
    return jnp.sum(total, axis=0, keepdims=True)


def masked_target(rows_here, target, held):
    slot = lax.broadcasted_iota(jnp.int32, target.shape, 1)
    held[64:ROWS] = jnp.zeros((ROWS - 64, target.shape[1]), f32)
    held[0 : target.shape[0]] = jnp.where(slot < rows_here[0], target[...], 0.0)


def distances(owned, place, rows_here, everyone, target, sums, target_held):
    members = everyone.shape[0]
    masked_target(rows_here, target, target_held)
    lines = []
    for a in range(owned):
        own = everyone[place[0] + a].astype(f32)
        for n in range(members):
            gap = own - everyone[n].astype(f32)
            lines.append(lanes_of(gap * gap))
    for a in range(owned):
        gap = everyone[place[0] + a].astype(f32) - target_held[...]
        lines.append(lanes_of(gap * gap))
    lines.append(jnp.zeros((128 - len(lines), 128), f32))
    table = jnp.concatenate(lines, axis=0).T
    line = jnp.sum(table, axis=0, keepdims=True)
    lane = lax.broadcasted_iota(jnp.int32, (1, 128), 1)
    line = jnp.where(lane == 127, rows_here[0].astype(f32), line)
    sums[...] = jnp.broadcast_to(line, sums.shape)


def output_grads(
    variables, place, rows_here, sums, everyone, target, hidden,
    grads, weight_grad, share,
    target_held, lit, parts_held, lit_sems, parts_sems,
):
    members = everyone.shape[0]
    held = grads.shape[0]
    pieces = lit_sems.shape[1]
    step = lit.shape[1] // pieces
    loads = []
    for a in range(held):
        for index in range(pieces):
            part = slice(index * step, (index + 1) * step)
            load = pltpu.make_async_copy(hidden.at[a, part], lit.at[a, part], lit_sems.at[a, index])
            load.start()
            loads.append(load)
    masked_target(rows_here, target, target_held)
    line = jnp.sum(sums[...], axis=0, keepdims=True)
    lane = lax.broadcasted_iota(jnp.int32, (1, 128), 1)
    cells = variables * line[:, 127:128]
    dist = jnp.sqrt(line / cells + epsilon)
    pairs = held * members
    apart = lane < pairs
    for a in range(held):
        apart = apart & (lane != a * members + place[0] + a)
    coef = jnp.where(apart, 1.0 / dist, 0.0)
    per_target = (lane >= pairs) & (lane < pairs + held)
    share[...] = jnp.sum(
        jnp.where(per_target, dist / members, 0.0)
        - jnp.where(apart, dist / (2.0 * members * (members - 1)), 0.0),
        axis=1, keepdims=True,
    ) + jnp.zeros(share.shape, f32)
    shown = []
    for a in range(held):
        chosen = everyone[place[0] + a].astype(f32)
        first = a * members
        reach = jnp.sum(jnp.where((lane >= first) & (lane < first + members), coef, 0.0), axis=1, keepdims=True)
        others = coef[:, first : first + 1] * everyone[0].astype(f32)
        for n in range(1, members):
            others = others + coef[:, first + n : first + n + 1] * everyone[n].astype(f32)
        toward = (chosen - target_held[...]) * (1.0 / (members * dist[:, pairs + a : pairs + a + 1]))
        shown.append((toward - (reach * chosen - others) * (1.0 / (members * (members - 1)))).astype(bf16))
        grads[a] = shown[a]
    for load in loads:
        load.wait()
    total = jnp.dot(shown[0], lit[0], preferred_element_type=f32)
    for a in range(1, held):
        total = total + jnp.dot(shown[a], lit[a], preferred_element_type=f32)
    tall = jnp.concatenate([total, jnp.zeros((ACROSS - total.shape[0], total.shape[1]), f32)], axis=0)
    parts_held[...] = tall.T.astype(bf16).reshape(parts_held.shape)
    pieces = min(parts_sems.shape[0], parts_held.shape[0])
    step = parts_held.shape[0] // pieces
    copies = []
    for index in range(pieces):
        part = slice(index * step, (index + 1) * step)
        copy = pltpu.make_async_copy(parts_held.at[part], weight_grad.at[part], parts_sems.at[index])
        copy.start()
        copies.append(copy)
    for copy in copies:
        copy.wait()


def backward(place, grads, w_out, slope, neighbours, weight, below, middle, above, w_rows):
    held, nodes, width = middle.shape
    variables = w_out.shape[0]
    w_rows[64:ROWS] = jnp.zeros((ROWS - 64, width), f32)
    w_rows[0:variables] = w_out[...].astype(f32)
    rows = w_rows[...].astype(bf16)
    first = (place[0] - 1) * nodes
    slots = neighbours.shape[1]
    step = 128
    spread = mixing(neighbours[...], weight[...], first, 3 * nodes).astype(bf16)
    for m in range(held):
        total = None
        lines = grads[m].astype(f32).T.astype(bf16)
        for start in range(0, slots, step):
            part = slice(start, start + step)
            back = jnp.dot(lines[part], rows, preferred_element_type=f32)
            grad_pre = (back * slope[m, part].astype(f32)).astype(bf16)
            term = jnp.dot(spread[:, part], grad_pre, preferred_element_type=f32)
            total = term if total is None else total + term
        below[m] = total[:nodes].astype(bf16)
        middle[m] = total[nodes : 2 * nodes]
        above[m] = total[2 * nodes :].astype(bf16)


def node_grads(middle, from_above, from_below, w_in, out):
    members, nodes, _ = out.shape
    total = middle[...] + from_above[...].astype(f32) + from_below[...].astype(f32)
    total = total.astype(bf16).reshape(members * nodes, -1)
    done = lax.dot_general(total, w_in[...], NT, preferred_element_type=f32)
    out[...] = done.astype(bf16).reshape(out.shape)


def gathered_sum(parts, share, out):
    total = jnp.sum(parts[...].astype(f32), axis=0)
    lane = lax.broadcasted_iota(jnp.int32, total.shape, 1)
    total = jnp.where(lane == ACROSS - 1, share[0:1, 0:1], total)
    out[...] = jnp.broadcast_to(total[None], out.shape)


def last_sum(parts, weight_grad, score):
    total = parts[0]
    for k in range(1, parts.shape[0]):
        total = total + parts[k]
    weight_grad[...] = total[:, : weight_grad.shape[1]]
    score[...] = total[0:1, ACROSS - 1 :]


def per_device(latent, edge_weight, neighbours, band_rows, w_in, w_out, target):
    members_dev, nodes, width = latent.shape
    slots = edge_weight.shape[1]
    variables = w_out.shape[0]
    groups, bands = lax.axis_size("member"), lax.axis_size("space")
    members = groups * members_dev
    band = lax.axis_index("space").astype(jnp.int32)
    group = lax.axis_index("member").astype(jnp.int32)
    up = [(i, i + 1) for i in range(bands - 1)]
    down = [(i + 1, i) for i in range(bands - 1)]
    before = lax.ppermute(latent, "space", up)
    after = lax.ppermute(latent, "space", down)
    where = band.reshape(1)
    mine_at = (group * members_dev).reshape(1)

    shape = jax.ShapeDtypeStruct
    big = (members_dev, slots, width)
    decoded = (members_dev, ROWS, slots)
    sent, hidden, slope = call(
        forward,
        (shape((groups, *decoded), bf16), shape(big, bf16), shape(big, bf16)),
        [SMEM, SMEM] + [VMEM] * 3 + [HBM] + [VMEM] * 3,
        (HBM, HBM, HBM),
        [
            pltpu.VMEM((width, width), bf16),
            pltpu.VMEM((3 * members_dev * nodes, width), bf16),
            pltpu.VMEM((members_dev, 6 * nodes, width), bf16),
            pltpu.VMEM((ROWS, width), f32),
            pltpu.VMEM(decoded, bf16),
            pltpu.VMEM(big, bf16),
            pltpu.VMEM(big, bf16),
            pltpu.SemaphoreType.DMA((4,)),
            pltpu.SemaphoreType.DMA((members_dev, slots // 128)),
            pltpu.SemaphoreType.DMA((members_dev, slots // 128)),
            pltpu.SemaphoreType.DMA((members_dev, groups)),
        ],
        room=58 << 10, flops=1 << 30, moved=8 << 20,
    )(where, band_rows, before, latent, after, w_in, w_out, neighbours, edge_weight)

    everyone = lax.all_to_all(sent, "member", 0, 0, tiled=True).reshape(members, ROWS, slots)

    def distances_body(*refs):
        distances(members_dev, *refs)

    sums = call(
        distances_body, shape((bands, 128), f32), [SMEM, SMEM, VMEM, VMEM], VMEM,
        [pltpu.VMEM((ROWS, slots), f32)], flops=1 << 22, moved=2 << 20,
    )(mine_at, band_rows, everyone, target)
    sums = lax.all_to_all(sums, "space", 0, 0, tiled=True)

    columns = width // bands
    tiles = (bands, columns, ACROSS)

    def grads_body(*refs):
        output_grads(variables, *refs)

    grads, weight_parts, share = call(
        grads_body,
        (shape(decoded, bf16), shape(tiles, bf16), shape((8, 128), f32)),
        [SMEM, SMEM, VMEM, VMEM, VMEM, HBM],
        (VMEM, HBM, VMEM),
        [
            pltpu.VMEM((ROWS, slots), f32),
            pltpu.VMEM(big, bf16),
            pltpu.VMEM(tiles, bf16),
            pltpu.SemaphoreType.DMA((members_dev, 4)),
            pltpu.SemaphoreType.DMA((4,)),
        ],
        room=60800, flops=1 << 28, moved=4 << 20,
    )(mine_at, band_rows, sums, everyone, target, hidden)
    weight_parts = lax.all_to_all(weight_parts, "space", 0, 0, tiled=True)

    small = (members_dev, nodes, width)
    lower, middle, upper = call(
        backward,
        (shape(small, bf16), shape(small, f32), shape(small, bf16)),
        [SMEM] + [VMEM] * 5,
        (VMEM,) * 3,
        [pltpu.VMEM((ROWS, width), f32)],
        room=60 << 10, flops=1 << 29, moved=4 << 20,
    )(where, grads, w_out, slope, neighbours, edge_weight)
    from_above = lax.ppermute(lower, "space", down)
    from_below = lax.ppermute(upper, "space", up)
    grad_latent = call(
        node_grads, shape(small, bf16), [VMEM] * 4, VMEM, room=58 << 10, flops=1 << 28, moved=4 << 20
    )(middle, from_above, from_below, w_in)

    total = call(
        gathered_sum, shape((groups, columns, ACROSS), f32), [VMEM] * 2, VMEM, flops=1 << 18, moved=1 << 18
    )(weight_parts, share)
    total = lax.all_to_all(total, "member", 0, 0, tiled=True)
    grad_w_out, score = call(
        last_sum, (shape((columns, variables), f32), shape((1, 1), f32)), [VMEM], (VMEM, VMEM),
        flops=1 << 16, moved=1 << 16,
    )(total)
    return (score.reshape(()), grad_latent, grad_w_out.T)


def solution(mesh):
    return jax.shard_map(
        per_device,
        mesh=mesh,
        in_specs=(
            P("member", "space", None),
            P(None, "space"),
            P(None, "space"),
            P("space"),
            P(),
            P(),
            P(None, "space"),
        ),
        out_specs=(P(), P("member", "space", None), P(None, "space")),
        check_vma=False,
    )
```

time: 123 us -> 121 us (0.984)
  blocking collectives: 0 us -> 32.2 us
  starting transfers between devices: 47.1 us -> 30.3 us
  local copies, waits for them, and re-layouts: 14.1 us -> 1.51 us
  waiting for transfers between devices: 44.4 us -> 32.1 us
  Pallas kernels: 12.2 us -> 22.6 us
  matrix products: 2.18 us -> 0 us
    all_to_all x0 -> x1, blocking collectives: none -> 32.2 us  [per_device(): sums = lax.all_to_all(sums, 'space', 0, 0, tiled=True)]
    all_to_all x1 -> x0, starting transfers between devices: 17.7 us -> none  [per_device(): sums = lax.all_to_all(sums, 'space', 0, 0, tiled=True)]
    all_to_all x1 -> x0, waiting for transfers between devices: 13.3 us -> none  [per_device(): sums = lax.all_to_all(sums, 'space', 0, 0, tiled=True)]
    unnamed x33 -> x14, local copies, waits for them, and re-layouts: 13.2 us -> 1.51 us
    pallas_call x6, Pallas kernels: 9.24 us -> 17.6 us  [the longest x1 7.23 us: per_device(): call(forward, (shape((groups, *decoded), bf16), shape(big, bf16), shape(b...]
    dot_general x1 -> x0, matrix products: 2.18 us -> none  [per_device(): jnp.dot(latent.reshape(members_dev * nodes, width), w_in, preferred_eleme...]
    all_to_all x1, waiting for transfers between devices: 4.98 us -> 2.85 us  [per_device(): total = lax.all_to_all(total, 'member', 0, 0, tiled=True)]
    ppermute x1, waiting for transfers between devices: 0.01 us -> 2.07 us  [per_device(): after = lax.ppermute(latent, 'space', down)]
  transfers between devices with their start and end apart: 8 -> 7, of which waited for: 4 -> 4; matrix products, arithmetic and copies ran while one was open for 3% -> 0% of each run, Pallas kernels for 5% -> 8%
where the time goes in v2:
time: 121 us; the launch traced here: 120 us
  blocking collectives  32.2 us (27%)
  waiting for transfers between devices  32.1 us (27%)
  starting transfers between devices  30.3 us (25%)
  Pallas kernels  22.6 us (19%)
  local copies, waits for them, and re-layouts  1.51 us (1%)
  between operations  1.42 us (1%)
    all_to_all x1, blocking collectives, per_device(): sums = lax.all_to_all(sums, 'space', 0, 0, tiled=True)  32.2 us
    all_to_all x1, waiting for transfers between devices, per_device(): lax.all_to_all(sent, 'member', 0, 0, tiled=True)  15.4 us
    all_to_all x1, waiting for transfers between devices, per_device(): weight_parts = lax.all_to_all(weight_parts, 'space', 0, 0, tiled=True)  11.9 us
    pallas_call x1, Pallas kernels, per_device(): call(forward, (shape((groups, *decoded), bf16), shape(big, bf16), shape(b...  7.23 us
    all_to_all x1, starting transfers between devices, per_device(): lax.all_to_all(sent, 'member', 0, 0, tiled=True)  6.8 us
    ppermute x1, starting transfers between devices, per_device(): after = lax.ppermute(latent, 'space', down)  5.16 us
    pallas_call x1, Pallas kernels, per_device(): call(backward, (shape(small, bf16), shape(small, f32), shape(small, bf16)...  4.94 us
    ppermute x1, starting transfers between devices, per_device(): before = lax.ppermute(latent, 'space', up)  4.94 us
  transfers between devices with their start and end apart: 7, of which 4 were waited for; matrix products, arithmetic and copies ran while one was open for 0% of the time, Pallas kernels for 8%

profile of v2, /device:TPU:1, one launch (start us, length us, event | category | flops | bytes accessed | tf_op | source)
XLA Modules:
  0.0 120.1 jit_solution(16243975744875319487)
XLA Ops:
  0.6 4.9 %collective-permute-start = (bf16[2,64,1024]{2,1,0:T(8,128)(2,1)}, bf16[2,64,1024]{2,1,0:T(8,128)(2,1)S(1)}, u32[]{:S(2)}, u32[]{:S(2)}) collective-permute-start(bf16[2,64,1024]{2,1,0:T(8,128)(2,1)} %own.1), channel_id=1, source_target_pairs={{0,1},{1,2},{2,3},{3,4},{4,5},{5,6},{6,7},{7,8},{8,9},{9,10},{10,1... | collective-permute-start | bytes 786440 | tf_op jit(solution)/shard_map/ppermute | solution.py:254
  5.6 5.2 %collective-permute-start.1 = (bf16[2,64,1024]{2,1,0:T(8,128)(2,1)}, bf16[2,64,1024]{2,1,0:T(8,128)(2,1)S(1)}, u32[]{:S(2)}, u32[]{:S(2)}) collective-permute-start(bf16[2,64,1024]{2,1,0:T(8,128)(2,1)} %own.1), channel_id=1, source_target_pairs={{1,0},{2,1},{3,2},{4,3},{5,4},{6,5},{7,6},{8,7},{9,8},{10,9},{11,1... | collective-permute-start | bytes 786440 | tf_op jit(solution)/shard_map/ppermute | solution.py:255
  11.4 0.0 collective-permute-done.before
  11.4 0.0 copy-start.5
  11.4 2.1 %collective-permute-done.1.after = bf16[2,64,1024]{2,1,0:T(8,128)(2,1)S(1)} collective-permute-done((bf16[2,64,1024]{2,1,0:T(8,128)(2,1)}, bf16[2,64,1024]{2,1,0:T(8,128)(2,1)S(1)}, u32[]{:S(2)}, u32[]{:S(2)}) %collective-permute-start.1) | collective-permute-done | bytes 262176 | tf_op jit(solution)/shard_map/ppermute | solution.py:255
  13.5 0.0 copy-start.6
  13.5 0.0 copy-done.5
  13.5 0.7 copy-done.6
  14.2 7.2 %shard_map.94 = (bf16[8,2,72,512]{3,2,1,0:T(8,128)(2,1)}, bf16[2,512,1024]{2,1,0:T(8,128)(2,1)}, bf16[2,512,1024]{2,1,0:T(8,128)(2,1)}) custom-call(s32[1]{0:T(128)} %bitcast.1.place, s32[1]{0:T(128)S(6)} %copy.11.rows_here.refs_1_, bf16[2,64,1024]{2,1,0:T(8,128)(2,1)} %copy-done.5, bf16[2,64,1024]{2,1,0:T(8,128)(2,1)} %own.1, ...), custom_call_target="tpu_custom_call" | custom-call | flops 1073741824 | bytes 8388608 | tf_op jit(solution)/shard_map/pallas_call | solution.py:262
  21.4 0.0 copy-start.1
  21.4 6.8 %all-to-all-start = ((bf16[8,2,72,512]{3,2,1,0:T(8,128)(2,1)}), bf16[8,2,72,512]{3,2,1,0:T(8,128)(2,1)S(1)}, u32[]{:S(2)}, u32[]{:S(2)}) async-start(bf16[8,2,72,512]{3,2,1,0:T(8,128)(2,1)} %get-tuple-element.14), calls=%async_computation | async-start | bytes 2359296 | tf_op jit(solution)/shard_map/all_to_all | solution.py:283
  28.2 15.4 %all-to-all-done = bf16[8,2,72,512]{3,2,1,0:T(8,128)(2,1)S(1)} async-done(((bf16[8,2,72,512]{3,2,1,0:T(8,128)(2,1)}), bf16[8,2,72,512]{3,2,1,0:T(8,128)(2,1)S(1)}, u32[]{:S(2)}, u32[]{:S(2)}) %all-to-all-start) | async-done | bytes 1179680 | tf_op jit(solution)/shard_map/all_to_all | solution.py:283
  43.6 0.0 copy-start
  43.6 0.0 copy-done.1
  43.6 0.8 shard_map.95
  44.4 32.2 %all_to_all.26 = f32[64,1,128]{2,1,0:T(1,128)} all-to-all(f32[64,1,128]{2,1,0:T(1,128)S(1)} %bitcast.11), channel_id=1, replica_groups=mesh['member'=8,'space'=64] {'space'}, dimensions={0} | all-to-all | bytes 65536 | tf_op jit(solution)/shard_map/all_to_all | solution.py:292
  76.6 0.0 copy-done
  76.6 4.8 %shard_map.96 = (bf16[2,72,512]{2,1,0:T(8,128)(2,1)}, bf16[64,16,128]{2,1,0:T(8,128)(2,1)}, f32[8,128]{1,0:T(8,128)}) custom-call(s32[1]{0:T(128)} %bitcast.refs_0_, s32[1]{0:T(128)S(6)} %copy.11.rows_here.refs_1_, f32[64,128]{1,0:T(8,128)} %bitcast.12, bf16[16,72,512]{2,1,0:T(8,128)(2,1)} %bitcast.10, f32[69,512]{1,0:T(8,128)} %refs_4_.1, ...), custom_call_target="tpu_custom_call" | custom-call | flops 268435456 | bytes 4194304 | tf_op jit(solution)/shard_map/pallas_call | solution.py:300
  81.5 0.0 copy-start.2
  81.5 4.5 %all-to-all-start.2 = ((bf16[64,16,128]{2,1,0:T(8,128)(2,1)}), bf16[64,16,128]{2,1,0:T(8,128)(2,1)S(1)}, u32[]{:S(2)}, u32[]{:S(2)}) async-start(bf16[64,16,128]{2,1,0:T(8,128)(2,1)} %get-tuple-element.16), calls=%async_computation.2 | async-start | bytes 524288 | tf_op jit(solution)/shard_map/all_to_all | solution.py:314
  86.0 4.9 %shard_map.99 = (bf16[2,64,1024]{2,1,0:T(8,128)(2,1)}, f32[2,64,1024]{2,1,0:T(8,128)}, bf16[2,64,1024]{2,1,0:T(8,128)(2,1)}) custom-call(s32[1]{0:T(128)} %bitcast.1.place, bf16[2,72,512]{2,1,0:T(8,128)(2,1)} %get-tuple-element.19.grads, bf16[69,1024]{1,0:T(8,128)(2,1)} %w_out.3, bf16[2,512,1024]{2,1,0:T(8,128)(2,1)} %get-tuple-element.20.slope, ...), custom_call_target="tpu_custom_call" | custom-call | flops 536870912 | bytes 4194304 | tf_op jit(solution)/shard_map/pallas_call | solution.py:317
  90.9 2.5 %collective-permute-start.2 = (bf16[2,64,1024]{2,1,0:T(8,128)(2,1)}, bf16[2,64,1024]{2,1,0:T(8,128)(2,1)S(1)}, u32[]{:S(2)}, u32[]{:S(2)}) collective-permute-start(bf16[2,64,1024]{2,1,0:T(8,128)(2,1)} %get-tuple-element.22), channel_id=1, source_target_pairs={{1,0},{2,1},{3,2},{4,3},{5,4},{6,5},{7,6},{8,7},{9,8},{10,9},{11,1... | collective-permute-start | bytes 786440 | tf_op jit(solution)/shard_map/ppermute | solution.py:325
  93.4 3.1 %collective-permute-start.3 = (bf16[2,64,1024]{2,1,0:T(8,128)(2,1)}, bf16[2,64,1024]{2,1,0:T(8,128)(2,1)S(1)}, u32[]{:S(2)}, u32[]{:S(2)}) collective-permute-start(bf16[2,64,1024]{2,1,0:T(8,128)(2,1)} %get-tuple-element.23), channel_id=1, source_target_pairs={{0,1},{1,2},{2,3},{3,4},{4,5},{5,6},{6,7},{7,8},{8,9},{9,10},{10,1... | collective-permute-start | bytes 786440 | tf_op jit(solution)/shard_map/ppermute | solution.py:326
  96.5 11.9 %all-to-all-done.2.parts = bf16[64,16,128]{2,1,0:T(8,128)(2,1)S(1)} async-done(((bf16[64,16,128]{2,1,0:T(8,128)(2,1)}), bf16[64,16,128]{2,1,0:T(8,128)(2,1)S(1)}, u32[]{:S(2)}, u32[]{:S(2)}) %all-to-all-start.2) | async-done | bytes 262176 | tf_op jit(solution)/shard_map/all_to_all | solution.py:314
  108.3 0.0 copy-done.2
  108.3 0.7 shard_map.97
  109.1 3.3 %all-to-all-start.3 = ((f32[8,16,128]{2,1,0:T(8,128)}), f32[8,16,128]{2,1,0:T(8,128)S(1)}, u32[]{:S(2)}, u32[]{:S(2)}) async-start(f32[8,16,128]{2,1,0:T(8,128)} %shard_map.97), calls=%async_computation.3 | async-start | bytes 131072 | tf_op jit(solution)/shard_map/all_to_all | solution.py:334
  112.4 0.0 collective-permute-done.2.from_above
  112.4 0.0 copy-start.3
  112.4 0.0 collective-permute-done.3.from_below
  112.4 0.0 copy-start.4
  112.5 0.7 copy-done.3
  113.1 0.1 copy-done.4
  113.2 3.5 %shard_map.100 = bf16[2,64,1024]{2,1,0:T(8,128)(2,1)} custom-call(f32[2,64,1024]{2,1,0:T(8,128)} %get-tuple-element.21.middle, bf16[2,64,1024]{2,1,0:T(8,128)(2,1)} %copy-done.3, bf16[2,64,1024]{2,1,0:T(8,128)(2,1)} %copy-done.4, bf16[1024,1024]{1,0:T(8,128)(2,1)} %w_in.3), custom_call_target="tpu_custom_call" | custom-call | flops 268435456 | bytes 4194304 | tf_op jit(solution)/shard_map/pallas_call | solution.py:327
  116.7 2.9 %all-to-all-done.3.parts = f32[8,16,128]{2,1,0:T(8,128)S(1)} async-done(((f32[8,16,128]{2,1,0:T(8,128)}), f32[8,16,128]{2,1,0:T(8,128)S(1)}, u32[]{:S(2)}, u32[]{:S(2)}) %all-to-all-start.3) | async-done | bytes 65568 | tf_op jit(solution)/shard_map/all_to_all | solution.py:334
  119.5 0.6 shard_map.98
Async XLA Ops:
  0.6 10.8 %collective-permute-start = (bf16[2,64,1024]{2,1,0:T(8,128)(2,1)}, bf16[2,64,1024]{2,1,0:T(8,128)(2,1)S(1)}, u32[]{:S(2)}, u32[]{:S(2)}) collective-permute-start(bf16[2,64,1024]{2,1,0:T(8,128)(2,1)} %own.1), channel_id=1, source_target_pairs={{0,1},{1,2},{2,3},{3,4},{4,5},{5,6},{6,7},{7,8},{8,9},{9,10},{10,1... | collective-permute-start | bytes 786440 | tf_op jit(solution)/shard_map/ppermute | solution.py:254
  5.6 7.9 %collective-permute-start.1 = (bf16[2,64,1024]{2,1,0:T(8,128)(2,1)}, bf16[2,64,1024]{2,1,0:T(8,128)(2,1)S(1)}, u32[]{:S(2)}, u32[]{:S(2)}) collective-permute-start(bf16[2,64,1024]{2,1,0:T(8,128)(2,1)} %own.1), channel_id=1, source_target_pairs={{1,0},{2,1},{3,2},{4,3},{5,4},{6,5},{7,6},{8,7},{9,8},{10,9},{11,1... | collective-permute-start | bytes 786440 | tf_op jit(solution)/shard_map/ppermute | solution.py:255
  11.4 2.1 %copy-start.5 = (bf16[2,64,1024]{2,1,0:T(8,128)(2,1)}, bf16[2,64,1024]{2,1,0:T(8,128)(2,1)S(1)}, u32[]{:S(2)}) copy-start(bf16[2,64,1024]{2,1,0:T(8,128)(2,1)S(1)} %collective-permute-done.before) | copy-start | bytes 786436
  13.5 0.7 copy-start.6
  21.4 22.2 %copy-start.1 = (f32[69,512]{1,0:T(8,128)S(1)}, f32[69,512]{1,0:T(8,128)}, u32[]{:S(2)}) copy-start(f32[69,512]{1,0:T(8,128)} %refs_4_.1) | copy-start | bytes 423940
  21.4 22.2 %all-to-all-start = ((bf16[8,2,72,512]{3,2,1,0:T(8,128)(2,1)}), bf16[8,2,72,512]{3,2,1,0:T(8,128)(2,1)S(1)}, u32[]{:S(2)}, u32[]{:S(2)}) async-start(bf16[8,2,72,512]{3,2,1,0:T(8,128)(2,1)} %get-tuple-element.14), calls=%async_computation | async-start | bytes 2359296 | tf_op jit(solution)/shard_map/all_to_all | solution.py:283
  43.6 33.0 %copy-start = (bf16[8,2,72,512]{3,2,1,0:T(8,128)(2,1)}, bf16[8,2,72,512]{3,2,1,0:T(8,128)(2,1)S(1)}, u32[]{:S(2)}) copy-start(bf16[8,2,72,512]{3,2,1,0:T(8,128)(2,1)S(1)} %all-to-all-done) | copy-start | bytes 3538948
  81.5 26.9 %copy-start.2 = (f32[8,128]{1,0:T(8,128)S(1)}, f32[8,128]{1,0:T(8,128)}, u32[]{:S(2)}) copy-start(f32[8,128]{1,0:T(8,128)} %get-tuple-element.17.share) | copy-start | bytes 12292
  81.5 26.9 %all-to-all-start.2 = ((bf16[64,16,128]{2,1,0:T(8,128)(2,1)}), bf16[64,16,128]{2,1,0:T(8,128)(2,1)S(1)}, u32[]{:S(2)}, u32[]{:S(2)}) async-start(bf16[64,16,128]{2,1,0:T(8,128)(2,1)} %get-tuple-element.16), calls=%async_computation.2 | async-start | bytes 524288 | tf_op jit(solution)/shard_map/all_to_all | solution.py:314
  90.9 21.5 %collective-permute-start.2 = (bf16[2,64,1024]{2,1,0:T(8,128)(2,1)}, bf16[2,64,1024]{2,1,0:T(8,128)(2,1)S(1)}, u32[]{:S(2)}, u32[]{:S(2)}) collective-permute-start(bf16[2,64,1024]{2,1,0:T(8,128)(2,1)} %get-tuple-element.22), channel_id=1, source_target_pairs={{1,0},{2,1},{3,2},{4,3},{5,4},{6,5},{7,6},{8,7},{9,8},{10,9},{11,1... | collective-permute-start | bytes 786440 | tf_op jit(solution)/shard_map/ppermute | solution.py:325
  93.4 19.0 %collective-permute-start.3 = (bf16[2,64,1024]{2,1,0:T(8,128)(2,1)}, bf16[2,64,1024]{2,1,0:T(8,128)(2,1)S(1)}, u32[]{:S(2)}, u32[]{:S(2)}) collective-permute-start(bf16[2,64,1024]{2,1,0:T(8,128)(2,1)} %get-tuple-element.23), channel_id=1, source_target_pairs={{0,1},{1,2},{2,3},{3,4},{4,5},{5,6},{6,7},{7,8},{8,9},{9,10},{10,1... | collective-permute-start | bytes 786440 | tf_op jit(solution)/shard_map/ppermute | solution.py:326
  109.1 10.5 %all-to-all-start.3 = ((f32[8,16,128]{2,1,0:T(8,128)}), f32[8,16,128]{2,1,0:T(8,128)S(1)}, u32[]{:S(2)}, u32[]{:S(2)}) async-start(f32[8,16,128]{2,1,0:T(8,128)} %shard_map.97), calls=%async_computation.3 | async-start | bytes 131072 | tf_op jit(solution)/shard_map/all_to_all | solution.py:334
  112.4 0.7 copy-start.3
  112.4 0.8 copy-start.4

commit v3 on v2

--- a/solution.py
+++ b/solution.py
@@ -38,41 +38,67 @@
     return total
 
 
-def forward(
-    place, rows_here, before, own, after, w_in, w_out, neighbours, weight,
-    sent, hidden, slope,
-    weights, latents, projected, w_rows, decoded, lit_held, slope_held, w_sems, lit_sems, slope_sems, sent_sems,
-):
-    members, nodes, width = own.shape
-    slots = neighbours.shape[1]
+def prepare(place, w_in, w_out, neighbours, weight, weights, rows, spread, w_held, w_sems):
     loads = []
     pieces = w_sems.shape[0]
+    step = weights.shape[0] // pieces
     for index in range(pieces):
-        part = slice(index * (width // pieces), (index + 1) * (width // pieces))
-        load = pltpu.make_async_copy(w_in.at[part], weights.at[part], w_sems.at[index])
-        load.start()
-        loads.append(load)
+        part = slice(index * step, (index + 1) * step)
+        loads.append(pltpu.make_async_copy(w_in.at[part], weights.at[part], w_sems.at[index]))
+        loads[-1].start()
+    nodes = spread.shape[1] // 6
+    mixed = mixing(neighbours[...], weight[...], (place[0] - 1) * nodes, 3 * nodes)
+    spread[...] = jnp.concatenate([mixed, mixed], axis=0).T.astype(bf16)
+    w_held[64:ROWS] = jnp.zeros((ROWS - 64, w_held.shape[1]), f32)
+    w_held[0 : w_out.shape[0]] = w_out[...].astype(f32)
+    rows[...] = w_held[...].astype(bf16)
+    for load in loads:
+        load.wait()
+
+
+def forward(
+    rows_here, before, own, after, weights, rows, spread,
+    sent, projected,
+    latents, held, decoded, held_sems, sent_sems,
+):
+    members, nodes, _ = own.shape
+    slots = spread.shape[0]
     step = 128
-    first = (place[0] - 1) * nodes
     around = 3 * nodes
-    spread = mixing(neighbours[...], weight[...], first, around)
-    spread = jnp.concatenate([spread, spread], axis=0).T.astype(bf16)
     for m in range(members):
         for k, source in enumerate((before, own, after)):
             latents[m * around + k * nodes : m * around + (k + 1) * nodes] = source[m]
-    for load in loads:
-        load.wait()
     whole = jnp.dot(latents[...], weights[...], preferred_element_type=f32)
     high = whole.astype(bf16)
     low = (whole - high.astype(f32)).astype(bf16)
+    copies = []
     for m in range(members):
-        projected[m, :around] = high[m * around : (m + 1) * around]
-        projected[m, around:] = low[m * around : (m + 1) * around]
-    variables = w_out.shape[0]
-    w_rows[64:ROWS] = jnp.zeros((ROWS - 64, width), f32)
-    w_rows[0:variables] = w_out[...].astype(f32)
-    rows = w_rows[...].astype(bf16)
+        held[m, :around] = high[m * around : (m + 1) * around]
+        held[m, around:] = low[m * around : (m + 1) * around]
+        copies.append(pltpu.make_async_copy(held.at[m], projected.at[m], held_sems.at[m]))
+        copies[-1].start()
     slot = lax.broadcasted_iota(jnp.int32, (ROWS, step), 1)
+    for m in range(members):
+        for start in range(0, slots, step):
+            part = slice(start, start + step)
+            preact = jnp.dot(spread[part], held[m], preferred_element_type=f32)
+            out = (preact * (0.5 * jnp.tanh(0.5 * preact) + 0.5)).astype(bf16)
+            fields = lax.dot_general(rows[...], out, NT, preferred_element_type=f32)
+            decoded[m, :, part] = jnp.where(slot + start < rows_here[0], fields, 0.0).astype(bf16)
+        for k in range(sent.shape[0]):
+            copies.append(pltpu.make_async_copy(decoded.at[m], sent.at[k, m], sent_sems.at[m, k]))
+            copies[-1].start()
+    for copy in copies:
+        copy.wait()
+
+
+def activations(place, projected, neighbours, weight, hidden, slope, held, sems):
+    members = projected.shape[0]
+    slots = neighbours.shape[1]
+    step = 128
+    nodes = projected.shape[1] // 6
+    spread = mixing(neighbours[...], weight[...], (place[0] - 1) * nodes, 3 * nodes)
+    spread = jnp.concatenate([spread, spread], axis=0).T.astype(bf16)
     copies = []
     for m in range(members):
         for index, start in enumerate(range(0, slots, step)):
@@ -80,19 +106,10 @@
             preact = jnp.dot(spread[part], projected[m], preferred_element_type=f32)
             gate = 0.5 * jnp.tanh(0.5 * preact) + 0.5
             lit = preact * gate
-            out = lit.astype(bf16)
-            lit_held[m, part] = out
-            slope_held[m, part] = (gate + lit * (1.0 - gate)).astype(bf16)
-            for held, target, sems in ((lit_held, hidden, lit_sems), (slope_held, slope, slope_sems)):
-                copy = pltpu.make_async_copy(held.at[m, part], target.at[m, part], sems.at[m, index])
-                copy.start()
-                copies.append(copy)
-            fields = lax.dot_general(rows, out, NT, preferred_element_type=f32)
-            decoded[m, :, part] = jnp.where(slot + start < rows_here[0], fields, 0.0).astype(bf16)
-        for k in range(sent.shape[0]):
-            copy = pltpu.make_async_copy(decoded.at[m], sent.at[k, m], sent_sems.at[m, k])
-            copy.start()
-            copies.append(copy)
+            hidden[m, part] = lit.astype(bf16)
+            held[m, part] = (gate + lit * (1.0 - gate)).astype(bf16)
+            copies.append(pltpu.make_async_copy(held.at[m, part], slope.at[m, part], sems.at[m, index]))
+            copies[-1].start()
     for copy in copies:
         copy.wait()
 
@@ -135,19 +152,10 @@
 def output_grads(
     variables, place, rows_here, sums, everyone, target, hidden,
     grads, weight_grad, share,
-    target_held, lit, parts_held, lit_sems, parts_sems,
+    target_held, shown, parts_held, shown_sems, parts_sems,
 ):
     members = everyone.shape[0]
     held = grads.shape[0]
-    pieces = lit_sems.shape[1]
-    step = lit.shape[1] // pieces
-    loads = []
-    for a in range(held):
-        for index in range(pieces):
-            part = slice(index * step, (index + 1) * step)
-            load = pltpu.make_async_copy(hidden.at[a, part], lit.at[a, part], lit_sems.at[a, index])
-            load.start()
-            loads.append(load)
     masked_target(rows_here, target, target_held)
     line = jnp.sum(sums[...], axis=0, keepdims=True)
     lane = lax.broadcasted_iota(jnp.int32, (1, 128), 1)
@@ -164,7 +172,7 @@
         - jnp.where(apart, dist / (2.0 * members * (members - 1)), 0.0),
         axis=1, keepdims=True,
     ) + jnp.zeros(share.shape, f32)
-    shown = []
+    copies = []
     for a in range(held):
         chosen = everyone[place[0] + a].astype(f32)
         first = a * members
@@ -173,18 +181,16 @@
         for n in range(1, members):
             others = others + coef[:, first + n : first + n + 1] * everyone[n].astype(f32)
         toward = (chosen - target_held[...]) * (1.0 / (members * dist[:, pairs + a : pairs + a + 1]))
-        shown.append((toward - (reach * chosen - others) * (1.0 / (members * (members - 1)))).astype(bf16))
-        grads[a] = shown[a]
-    for load in loads:
-        load.wait()
-    total = jnp.dot(shown[0], lit[0], preferred_element_type=f32)
+        shown[a] = (toward - (reach * chosen - others) * (1.0 / (members * (members - 1)))).astype(bf16)
+        copies.append(pltpu.make_async_copy(shown.at[a], grads.at[a], shown_sems.at[a]))
+        copies[-1].start()
+    total = jnp.dot(shown[0], hidden[0], preferred_element_type=f32)
     for a in range(1, held):
-        total = total + jnp.dot(shown[a], lit[a], preferred_element_type=f32)
+        total = total + jnp.dot(shown[a], hidden[a], preferred_element_type=f32)
     tall = jnp.concatenate([total, jnp.zeros((ACROSS - total.shape[0], total.shape[1]), f32)], axis=0)
     parts_held[...] = tall.T.astype(bf16).reshape(parts_held.shape)
     pieces = min(parts_sems.shape[0], parts_held.shape[0])
     step = parts_held.shape[0] // pieces
-    copies = []
     for index in range(pieces):
         part = slice(index * step, (index + 1) * step)
         copy = pltpu.make_async_copy(parts_held.at[part], weight_grad.at[part], parts_sems.at[index])
@@ -259,28 +265,43 @@
     shape = jax.ShapeDtypeStruct
     big = (members_dev, slots, width)
     decoded = (members_dev, ROWS, slots)
-    sent, hidden, slope = call(
+    kept = (members_dev, 6 * nodes, width)
+
+    def stay(array):
+        return pltpu.with_memory_space_constraint(array, pltpu.HBM)
+
+    weights, rows, spread = call(
+        prepare,
+        (pltpu.VMEM(w_in.shape, bf16), pltpu.VMEM((ROWS, width), bf16), pltpu.VMEM((slots, 6 * nodes), bf16)),
+        [SMEM, HBM] + [VMEM] * 3,
+        (VMEM,) * 3,
+        [pltpu.VMEM((ROWS, width), f32), pltpu.SemaphoreType.DMA((4,))],
+        flops=1 << 22, moved=4 << 20,
+    )(where, stay(w_in), stay(w_out), stay(neighbours), stay(edge_weight))
+    sent, projected = call(
         forward,
-        (shape((groups, *decoded), bf16), shape(big, bf16), shape(big, bf16)),
-        [SMEM, SMEM] + [VMEM] * 3 + [HBM] + [VMEM] * 3,
-        (HBM, HBM, HBM),
+        (pltpu.HBM((groups, *decoded), bf16), pltpu.HBM(kept, bf16)),
+        [SMEM] + [VMEM] * 6,
+        (HBM, HBM),
         [
-            pltpu.VMEM((width, width), bf16),
             pltpu.VMEM((3 * members_dev * nodes, width), bf16),
-            pltpu.VMEM((members_dev, 6 * nodes, width), bf16),
-            pltpu.VMEM((ROWS, width), f32),
+            pltpu.VMEM(kept, bf16),
             pltpu.VMEM(decoded, bf16),
-            pltpu.VMEM(big, bf16),
-            pltpu.VMEM(big, bf16),
-            pltpu.SemaphoreType.DMA((4,)),
-            pltpu.SemaphoreType.DMA((members_dev, slots // 128)),
-            pltpu.SemaphoreType.DMA((members_dev, slots // 128)),
+            pltpu.SemaphoreType.DMA((members_dev,)),
             pltpu.SemaphoreType.DMA((members_dev, groups)),
         ],
-        room=58 << 10, flops=1 << 30, moved=8 << 20,
-    )(where, band_rows, before, latent, after, w_in, w_out, neighbours, edge_weight)
+        flops=1 << 30, moved=8 << 20,
+    )(band_rows, before, stay(latent), after, weights, rows, spread)
 
     everyone = lax.all_to_all(sent, "member", 0, 0, tiled=True).reshape(members, ROWS, slots)
+    hidden, slope = call(
+        activations,
+        (pltpu.VMEM(big, bf16), pltpu.HBM(big, bf16)),
+        [SMEM] + [VMEM] * 3,
+        (VMEM, HBM),
+        [pltpu.VMEM(big, bf16), pltpu.SemaphoreType.DMA((members_dev, slots // 128))],
+        flops=1 << 30, moved=8 << 20,
+    )(where, stay(projected), stay(neighbours), stay(edge_weight))
 
     def distances_body(*refs):
         distances(members_dev, *refs)
@@ -299,33 +320,33 @@
 
     grads, weight_parts, share = call(
         grads_body,
-        (shape(decoded, bf16), shape(tiles, bf16), shape((8, 128), f32)),
-        [SMEM, SMEM, VMEM, VMEM, VMEM, HBM],
-        (VMEM, HBM, VMEM),
+        (pltpu.HBM(decoded, bf16), pltpu.HBM(tiles, bf16), shape((8, 128), f32)),
+        [SMEM, SMEM, VMEM, VMEM, VMEM, VMEM],
+        (HBM, HBM, VMEM),
         [
             pltpu.VMEM((ROWS, slots), f32),
-            pltpu.VMEM(big, bf16),
+            pltpu.VMEM(decoded, bf16),
             pltpu.VMEM(tiles, bf16),
-            pltpu.SemaphoreType.DMA((members_dev, 4)),
+            pltpu.SemaphoreType.DMA((members_dev,)),
             pltpu.SemaphoreType.DMA((4,)),
         ],
-        room=60800, flops=1 << 28, moved=4 << 20,
+        flops=1 << 28, moved=4 << 20,
     )(mine_at, band_rows, sums, everyone, target, hidden)
     weight_parts = lax.all_to_all(weight_parts, "space", 0, 0, tiled=True)
 
     small = (members_dev, nodes, width)
     lower, middle, upper = call(
         backward,
-        (shape(small, bf16), shape(small, f32), shape(small, bf16)),
+        (pltpu.VMEM(small, bf16), pltpu.VMEM(small, f32), pltpu.VMEM(small, bf16)),
         [SMEM] + [VMEM] * 5,
         (VMEM,) * 3,
         [pltpu.VMEM((ROWS, width), f32)],
-        room=60 << 10, flops=1 << 29, moved=4 << 20,
-    )(where, grads, w_out, slope, neighbours, edge_weight)
+        flops=1 << 29, moved=4 << 20,
+    )(where, stay(grads), stay(w_out), stay(slope), stay(neighbours), stay(edge_weight))
     from_above = lax.ppermute(lower, "space", down)
     from_below = lax.ppermute(upper, "space", up)
     grad_latent = call(
-        node_grads, shape(small, bf16), [VMEM] * 4, VMEM, room=58 << 10, flops=1 << 28, moved=4 << 20
+        node_grads, shape(small, bf16), [VMEM] * 4, VMEM, flops=1 << 28, moved=4 << 20
     )(middle, from_above, from_below, w_in)
 
     total = call(

time: 121 us -> 116 us (0.959)
  blocking collectives: 32.2 us -> 0 us
  starting transfers between devices: 30.3 us -> 48.7 us
  waiting for transfers between devices: 32.1 us -> 42.3 us
  local copies, waits for them, and re-layouts: 1.51 us -> 0.01 us
    all_to_all x1 -> x0, blocking collectives: 32.2 us -> none  [per_device(): sums = lax.all_to_all(sums, 'space', 0, 0, tiled=True)]
    all_to_all x0 -> x1, starting transfers between devices: none -> 18.4 us  [per_device(): sums = lax.all_to_all(sums, 'space', 0, 0, tiled=True)]
    all_to_all x0 -> x1, waiting for transfers between devices: none -> 8.81 us  [per_device(): sums = lax.all_to_all(sums, 'space', 0, 0, tiled=True)]
    all_to_all x1, waiting for transfers between devices: 2.85 us -> 5.55 us  [per_device(): total = lax.all_to_all(total, 'member', 0, 0, tiled=True)]
    ppermute x1, waiting for transfers between devices: 2.07 us -> 0.01 us  [per_device(): after = lax.ppermute(latent, 'space', down)]
    unnamed x14 -> x4, local copies, waits for them, and re-layouts: 1.51 us -> 0.01 us
    pallas_call x4 -> x6, Pallas kernels: 20.5 us -> 20.5 us  [the longest x1 5.36 us: per_device(): call(forward, (pltpu.HBM((groups, *decoded), bf16), pltpu.HBM(kept, bf16)...]
  transfers between devices with their start and end apart: 7 -> 8, of which waited for: 4 -> 4; matrix products, arithmetic and copies ran while one was open for 0% -> 0% of each run, Pallas kernels for 8% -> 12%
where the time goes in v3:
time: 116 us
  starting transfers between devices  48.7 us (42%)
  waiting for transfers between devices  42.3 us (36%)
  Pallas kernels  23.2 us (20%)
  between operations  1.43 us (1%)
    all_to_all x1, starting transfers between devices, per_device(): sums = lax.all_to_all(sums, 'space', 0, 0, tiled=True)  18.4 us
    all_to_all x1, waiting for transfers between devices, per_device(): lax.all_to_all(sent, 'member', 0, 0, tiled=True)  16 us
    all_to_all x1, waiting for transfers between devices, per_device(): weight_parts = lax.all_to_all(weight_parts, 'space', 0, 0, tiled=True)  11.9 us
    all_to_all x1, waiting for transfers between devices, per_device(): sums = lax.all_to_all(sums, 'space', 0, 0, tiled=True)  8.81 us
    all_to_all x1, starting transfers between devices, per_device(): lax.all_to_all(sent, 'member', 0, 0, tiled=True)  6.35 us
    all_to_all x1, waiting for transfers between devices, per_device(): total = lax.all_to_all(total, 'member', 0, 0, tiled=True)  5.55 us
    pallas_call x1, Pallas kernels, per_device(): call(forward, (pltpu.HBM((groups, *decoded), bf16), pltpu.HBM(kept, bf16)...  5.36 us
    ppermute x1, starting transfers between devices, per_device(): after = lax.ppermute(latent, 'space', down)  5.16 us
  transfers between devices with their start and end apart: 8, of which 4 were waited for; matrix products, arithmetic and copies ran while one was open for 0% of the time, Pallas kernels for 12%

profile of v3, /device:TPU:1, one launch (start us, length us, event | category | flops | bytes accessed | tf_op | source)
XLA Modules:
  0.0 115.7 jit_solution(4370541710719796476)
XLA Ops:
  0.6 4.9 %collective-permute-start = (bf16[2,64,1024]{2,1,0:T(8,128)(2,1)}, bf16[2,64,1024]{2,1,0:T(8,128)(2,1)S(1)}, u32[]{:S(2)}, u32[]{:S(2)}) collective-permute-start(bf16[2,64,1024]{2,1,0:T(8,128)(2,1)} %own.1), channel_id=1, source_target_pairs={{0,1},{1,2},{2,3},{3,4},{4,5},{5,6},{6,7},{7,8},{8,9},{9,10},{10,1... | collective-permute-start | bytes 786440 | tf_op jit(solution)/shard_map/ppermute | solution.py:260
  5.6 5.2 %collective-permute-start.1 = (bf16[2,64,1024]{2,1,0:T(8,128)(2,1)}, bf16[2,64,1024]{2,1,0:T(8,128)(2,1)S(1)}, u32[]{:S(2)}, u32[]{:S(2)}) collective-permute-start(bf16[2,64,1024]{2,1,0:T(8,128)(2,1)} %own.1), channel_id=1, source_target_pairs={{1,0},{2,1},{3,2},{4,3},{5,4},{6,5},{7,6},{8,7},{9,8},{10,9},{11,1... | collective-permute-start | bytes 786440 | tf_op jit(solution)/shard_map/ppermute | solution.py:261
  11.4 2.5 %shard_map.94 = (bf16[1024,1024]{1,0:T(8,128)(2,1)S(1)}, bf16[72,1024]{1,0:T(8,128)(2,1)S(1)}, bf16[512,384]{1,0:T(8,128)(2,1)S(1)}) custom-call(s32[1]{0:T(128)} %bitcast.1.place, bf16[1024,1024]{1,0:T(8,128)(2,1)} %w_in.3, bf16[69,1024]{1,0:T(8,128)(2,1)} %w_out.3, s32[3,512]{1,0:T(4,128)} %neighbours.5, f32[3,512]{1,0:T(4,128)} %weight.5), custom_call_target="tpu_custom_call" | custom-call | flops 4194304 | bytes 4194304 | tf_op jit(solution)/shard_map/pallas_call | solution.py:273
  13.9 0.0 collective-permute-done.before
  13.9 0.0 collective-permute-done.1.after
  13.9 5.4 %shard_map.95 = (bf16[8,2,72,512]{3,2,1,0:T(8,128)(2,1)}, bf16[2,384,1024]{2,1,0:T(8,128)(2,1)}) custom-call(s32[1]{0:T(128)S(6)} %copy.11.rows_here.refs_1_, bf16[2,64,1024]{2,1,0:T(8,128)(2,1)S(1)} %collective-permute-done.before, bf16[2,64,1024]{2,1,0:T(8,128)(2,1)} %own.1, bf16[2,64,1024]{2,1,0:T(8,128)(2,1)S(1)} %collective-permute-done.1.after, ...), custom_call_target="tpu_custom_call" | custom-call | flops 1073741824 | bytes 8388608 | tf_op jit(solution)/shard_map/pallas_call | solution.py:281
  19.3 0.0 copy-start.1
  19.3 6.4 %all-to-all-start = ((bf16[8,2,72,512]{3,2,1,0:T(8,128)(2,1)}), bf16[8,2,72,512]{3,2,1,0:T(8,128)(2,1)S(1)}, u32[]{:S(2)}, u32[]{:S(2)}) async-start(bf16[8,2,72,512]{3,2,1,0:T(8,128)(2,1)} %get-tuple-element.21), calls=%async_computation | async-start | bytes 2359296 | tf_op jit(solution)/shard_map/all_to_all | solution.py:296
  25.6 16.0 %all-to-all-done = bf16[8,2,72,512]{3,2,1,0:T(8,128)(2,1)S(1)} async-done(((bf16[8,2,72,512]{3,2,1,0:T(8,128)(2,1)}), bf16[8,2,72,512]{3,2,1,0:T(8,128)(2,1)S(1)}, u32[]{:S(2)}, u32[]{:S(2)}) %all-to-all-start) | async-done | bytes 1179680 | tf_op jit(solution)/shard_map/all_to_all | solution.py:296
  41.7 0.0 copy-done.1
  41.7 1.4 %shard_map.96 = f32[64,128]{1,0:T(8,128)} custom-call(s32[1]{0:T(128)} %bitcast.refs_0_, s32[1]{0:T(128)S(6)} %copy.11.rows_here.refs_1_, bf16[16,72,512]{2,1,0:T(8,128)(2,1)S(1)} %bitcast.9, f32[69,512]{1,0:T(8,128)S(1)} %copy-done.1), custom_call_target="tpu_custom_call" | custom-call | flops 4194304 | bytes 2097152 | tf_op jit(solution)/shard_map/pallas_call | solution.py:309
  43.1 18.4 %all-to-all-start.1 = ((f32[64,1,128]{2,1,0:T(1,128)}), f32[64,1,128]{2,1,0:T(1,128)S(1)}, u32[]{:S(2)}, u32[]{:S(2)}) async-start(f32[64,1,128]{2,1,0:T(1,128)} %bitcast.4), calls=%async_computation.1 | async-start | bytes 65536 | tf_op jit(solution)/shard_map/all_to_all | solution.py:313
  61.4 4.4 %shard_map.97 = (bf16[2,512,1024]{2,1,0:T(8,128)(2,1)S(1)}, bf16[2,512,1024]{2,1,0:T(8,128)(2,1)}) custom-call(s32[1]{0:T(128)} %bitcast.1.place, bf16[2,384,1024]{2,1,0:T(8,128)(2,1)} %get-tuple-element.22.projected, s32[3,512]{1,0:T(4,128)} %neighbours.5, f32[3,512]{1,0:T(4,128)} %weight.5), custom_call_target="tpu_custom_call" | custom-call | flops 1073741824 | bytes 8388608 | tf_op jit(solution)/shard_map/pallas_call | solution.py:297
  65.8 8.8 %all-to-all-done.1 = f32[64,1,128]{2,1,0:T(1,128)S(1)} async-done(((f32[64,1,128]{2,1,0:T(1,128)}), f32[64,1,128]{2,1,0:T(1,128)S(1)}, u32[]{:S(2)}, u32[]{:S(2)}) %all-to-all-start.1) | async-done | bytes 32800 | tf_op jit(solution)/shard_map/all_to_all | solution.py:313
  74.6 2.0 %shard_map.98 = (bf16[2,72,512]{2,1,0:T(8,128)(2,1)}, bf16[64,16,128]{2,1,0:T(8,128)(2,1)}, f32[8,128]{1,0:T(8,128)S(1)}) custom-call(s32[1]{0:T(128)} %bitcast.refs_0_, s32[1]{0:T(128)S(6)} %copy.11.rows_here.refs_1_, f32[64,128]{1,0:T(8,128)S(1)} %bitcast.11, bf16[16,72,512]{2,1,0:T(8,128)(2,1)S(1)} %bitcast.10, f32[69,512]{1,0:T(8,128)S(1)} %copy-done.1, ...), custom_call_target="tpu_custom_call" | custom-call | flops 268435456 | bytes 4194304 | tf_op jit(solution)/shard_map/pallas_call | solution.py:321
  76.6 0.0 copy-start
  76.6 5.0 %all-to-all-start.2 = ((bf16[64,16,128]{2,1,0:T(8,128)(2,1)}), bf16[64,16,128]{2,1,0:T(8,128)(2,1)S(1)}, u32[]{:S(2)}, u32[]{:S(2)}) async-start(bf16[64,16,128]{2,1,0:T(8,128)(2,1)} %get-tuple-element.24), calls=%async_computation.2 | async-start | bytes 524288 | tf_op jit(solution)/shard_map/all_to_all | solution.py:335
  81.6 4.8 %shard_map.101 = (bf16[2,64,1024]{2,1,0:T(8,128)(2,1)}, f32[2,64,1024]{2,1,0:T(8,128)S(1)}, bf16[2,64,1024]{2,1,0:T(8,128)(2,1)}) custom-call(s32[1]{0:T(128)} %bitcast.1.place, bf16[2,72,512]{2,1,0:T(8,128)(2,1)} %get-tuple-element.27.grads, bf16[69,1024]{1,0:T(8,128)(2,1)} %w_out.3, bf16[2,512,1024]{2,1,0:T(8,128)(2,1)} %get-tuple-element.28.slope, ...), custom_call_target="tpu_custom_call" | custom-call | flops 536870912 | bytes 4194304 | tf_op jit(solution)/shard_map/pallas_call | solution.py:338
  86.4 2.3 %collective-permute-start.2 = (bf16[2,64,1024]{2,1,0:T(8,128)(2,1)}, bf16[2,64,1024]{2,1,0:T(8,128)(2,1)S(1)}, u32[]{:S(2)}, u32[]{:S(2)}) collective-permute-start(bf16[2,64,1024]{2,1,0:T(8,128)(2,1)} %get-tuple-element.30), channel_id=1, source_target_pairs={{1,0},{2,1},{3,2},{4,3},{5,4},{6,5},{7,6},{8,7},{9,8},{10,9},{11,1... | collective-permute-start | bytes 786440 | tf_op jit(solution)/shard_map/ppermute | solution.py:346
  88.7 3.2 %collective-permute-start.3 = (bf16[2,64,1024]{2,1,0:T(8,128)(2,1)}, bf16[2,64,1024]{2,1,0:T(8,128)(2,1)S(1)}, u32[]{:S(2)}, u32[]{:S(2)}) collective-permute-start(bf16[2,64,1024]{2,1,0:T(8,128)(2,1)} %get-tuple-element.31), channel_id=1, source_target_pairs={{0,1},{1,2},{2,3},{3,4},{4,5},{5,6},{6,7},{7,8},{8,9},{9,10},{10,1... | collective-permute-start | bytes 786440 | tf_op jit(solution)/shard_map/ppermute | solution.py:347
  91.9 11.9 %all-to-all-done.2.parts = bf16[64,16,128]{2,1,0:T(8,128)(2,1)S(1)} async-done(((bf16[64,16,128]{2,1,0:T(8,128)(2,1)}), bf16[64,16,128]{2,1,0:T(8,128)(2,1)S(1)}, u32[]{:S(2)}, u32[]{:S(2)}) %all-to-all-start.2) | async-done | bytes 262176 | tf_op jit(solution)/shard_map/all_to_all | solution.py:335
  103.9 0.7 shard_map.99
  104.6 3.3 %all-to-all-start.3 = ((f32[8,16,128]{2,1,0:T(8,128)}), f32[8,16,128]{2,1,0:T(8,128)S(1)}, u32[]{:S(2)}, u32[]{:S(2)}) async-start(f32[8,16,128]{2,1,0:T(8,128)} %shard_map.99), calls=%async_computation.3 | async-start | bytes 131072 | tf_op jit(solution)/shard_map/all_to_all | solution.py:355
  107.9 0.0 collective-permute-done.2.from_above
  107.9 0.0 collective-permute-done.3.from_below
  108.0 0.0 copy-done
  108.0 1.5 %shard_map.102 = bf16[2,64,1024]{2,1,0:T(8,128)(2,1)} custom-call(f32[2,64,1024]{2,1,0:T(8,128)S(1)} %get-tuple-element.29.middle, bf16[2,64,1024]{2,1,0:T(8,128)(2,1)S(1)} %collective-permute-done.2.from_above, bf16[2,64,1024]{2,1,0:T(8,128)(2,1)S(1)} %collective-permute-done.3.from_below, bf16[1024,1024]{1,0:T(8,128)(2,1)S(1)} %copy-done), custom_call_target="tpu_custom_call" | custom-call | flops 268435456 | bytes 4194304 | tf_op jit(solution)/shard_map/pallas_call | solution.py:348
  109.5 5.5 %all-to-all-done.3.parts = f32[8,16,128]{2,1,0:T(8,128)S(1)} async-done(((f32[8,16,128]{2,1,0:T(8,128)}), f32[8,16,128]{2,1,0:T(8,128)S(1)}, u32[]{:S(2)}, u32[]{:S(2)}) %all-to-all-start.3) | async-done | bytes 65568 | tf_op jit(solution)/shard_map/all_to_all | solution.py:355
  115.1 0.6 shard_map.100
Async XLA Ops:
  0.6 13.3 %collective-permute-start = (bf16[2,64,1024]{2,1,0:T(8,128)(2,1)}, bf16[2,64,1024]{2,1,0:T(8,128)(2,1)S(1)}, u32[]{:S(2)}, u32[]{:S(2)}) collective-permute-start(bf16[2,64,1024]{2,1,0:T(8,128)(2,1)} %own.1), channel_id=1, source_target_pairs={{0,1},{1,2},{2,3},{3,4},{4,5},{5,6},{6,7},{7,8},{8,9},{9,10},{10,1... | collective-permute-start | bytes 786440 | tf_op jit(solution)/shard_map/ppermute | solution.py:260
  5.6 8.3 %collective-permute-start.1 = (bf16[2,64,1024]{2,1,0:T(8,128)(2,1)}, bf16[2,64,1024]{2,1,0:T(8,128)(2,1)S(1)}, u32[]{:S(2)}, u32[]{:S(2)}) collective-permute-start(bf16[2,64,1024]{2,1,0:T(8,128)(2,1)} %own.1), channel_id=1, source_target_pairs={{1,0},{2,1},{3,2},{4,3},{5,4},{6,5},{7,6},{8,7},{9,8},{10,9},{11,1... | collective-permute-start | bytes 786440 | tf_op jit(solution)/shard_map/ppermute | solution.py:261
  19.3 22.4 %copy-start.1 = (f32[69,512]{1,0:T(8,128)S(1)}, f32[69,512]{1,0:T(8,128)}, u32[]{:S(2)}) copy-start(f32[69,512]{1,0:T(8,128)} %refs_4_.1) | copy-start | bytes 423940
  19.3 22.4 %all-to-all-start = ((bf16[8,2,72,512]{3,2,1,0:T(8,128)(2,1)}), bf16[8,2,72,512]{3,2,1,0:T(8,128)(2,1)S(1)}, u32[]{:S(2)}, u32[]{:S(2)}) async-start(bf16[8,2,72,512]{3,2,1,0:T(8,128)(2,1)} %get-tuple-element.21), calls=%async_computation | async-start | bytes 2359296 | tf_op jit(solution)/shard_map/all_to_all | solution.py:296
  43.1 31.5 %all-to-all-start.1 = ((f32[64,1,128]{2,1,0:T(1,128)}), f32[64,1,128]{2,1,0:T(1,128)S(1)}, u32[]{:S(2)}, u32[]{:S(2)}) async-start(f32[64,1,128]{2,1,0:T(1,128)} %bitcast.4), calls=%async_computation.1 | async-start | bytes 65536 | tf_op jit(solution)/shard_map/all_to_all | solution.py:313
  76.6 31.4 %copy-start = (bf16[1024,1024]{1,0:T(8,128)(2,1)S(1)}, bf16[1024,1024]{1,0:T(8,128)(2,1)}, u32[]{:S(2)}) copy-start(bf16[1024,1024]{1,0:T(8,128)(2,1)} %w_in.3) | copy-start | bytes 6291460
  76.6 27.3 %all-to-all-start.2 = ((bf16[64,16,128]{2,1,0:T(8,128)(2,1)}), bf16[64,16,128]{2,1,0:T(8,128)(2,1)S(1)}, u32[]{:S(2)}, u32[]{:S(2)}) async-start(bf16[64,16,128]{2,1,0:T(8,128)(2,1)} %get-tuple-element.24), calls=%async_computation.2 | async-start | bytes 524288 | tf_op jit(solution)/shard_map/all_to_all | solution.py:335
  86.4 21.6 %collective-permute-start.2 = (bf16[2,64,1024]{2,1,0:T(8,128)(2,1)}, bf16[2,64,1024]{2,1,0:T(8,128)(2,1)S(1)}, u32[]{:S(2)}, u32[]{:S(2)}) collective-permute-start(bf16[2,64,1024]{2,1,0:T(8,128)(2,1)} %get-tuple-element.30), channel_id=1, source_target_pairs={{1,0},{2,1},{3,2},{4,3},{5,4},{6,5},{7,6},{8,7},{9,8},{10,9},{11,1... | collective-permute-start | bytes 786440 | tf_op jit(solution)/shard_map/ppermute | solution.py:346
  88.7 19.2 %collective-permute-start.3 = (bf16[2,64,1024]{2,1,0:T(8,128)(2,1)}, bf16[2,64,1024]{2,1,0:T(8,128)(2,1)S(1)}, u32[]{:S(2)}, u32[]{:S(2)}) collective-permute-start(bf16[2,64,1024]{2,1,0:T(8,128)(2,1)} %get-tuple-element.31), channel_id=1, source_target_pairs={{0,1},{1,2},{2,3},{3,4},{4,5},{5,6},{6,7},{7,8},{8,9},{9,10},{10,1... | collective-permute-start | bytes 786440 | tf_op jit(solution)/shard_map/ppermute | solution.py:347
  104.6 10.5 %all-to-all-start.3 = ((f32[8,16,128]{2,1,0:T(8,128)}), f32[8,16,128]{2,1,0:T(8,128)S(1)}, u32[]{:S(2)}, u32[]{:S(2)}) async-start(f32[8,16,128]{2,1,0:T(8,128)} %shard_map.99), calls=%async_computation.3 | async-start | bytes 131072 | tf_op jit(solution)/shard_map/all_to_all | solution.py:355

commit v4 on v3

--- a/solution.py
+++ b/solution.py
@@ -38,7 +38,7 @@
     return total
 
 
-def prepare(place, w_in, w_out, neighbours, weight, weights, rows, spread, w_held, w_sems):
+def prepare(place, own, w_in, w_out, neighbours, weight, weights, rows, spread, mine, w_held, w_sems):
     loads = []
     pieces = w_sems.shape[0]
     step = weights.shape[0] // pieces
@@ -54,27 +54,32 @@
     rows[...] = w_held[...].astype(bf16)
     for load in loads:
         load.wait()
+    here = own[...].reshape(mine.shape)
+    mine[...] = jnp.dot(here, weights[...], preferred_element_type=f32)
 
 
 def forward(
-    rows_here, before, own, after, weights, rows, spread,
+    rows_here, before, mine, after, weights, rows, spread,
     sent, projected,
     latents, held, decoded, held_sems, sent_sems,
 ):
-    members, nodes, _ = own.shape
+    members, nodes, _ = before.shape
     slots = spread.shape[0]
     step = 128
     around = 3 * nodes
-    for m in range(members):
-        for k, source in enumerate((before, own, after)):
-            latents[m * around + k * nodes : m * around + (k + 1) * nodes] = source[m]
+    both = members * nodes
+    latents[:both] = before[...].reshape(both, -1)
+    latents[both:] = after[...].reshape(both, -1)
     whole = jnp.dot(latents[...], weights[...], preferred_element_type=f32)
-    high = whole.astype(bf16)
-    low = (whole - high.astype(f32)).astype(bf16)
+    for k, source in enumerate((whole[:both], mine[...], whole[both:])):
+        high = source.astype(bf16)
+        low = (source - high.astype(f32)).astype(bf16)
+        for m in range(members):
+            first = k * nodes
+            held[m, first : first + nodes] = high[m * nodes : (m + 1) * nodes]
+            held[m, around + first : around + first + nodes] = low[m * nodes : (m + 1) * nodes]
     copies = []
     for m in range(members):
-        held[m, :around] = high[m * around : (m + 1) * around]
-        held[m, around:] = low[m * around : (m + 1) * around]
         copies.append(pltpu.make_async_copy(held.at[m], projected.at[m], held_sems.at[m]))
         copies[-1].start()
     slot = lax.broadcasted_iota(jnp.int32, (ROWS, step), 1)
@@ -92,7 +97,8 @@
         copy.wait()
 
 
-def activations(place, projected, neighbours, weight, hidden, slope, held, sems):
+def activations(place, projected, neighbours, weight, hidden, slope, done, held, sems):
+    done[...] = jnp.zeros_like(done)
     members = projected.shape[0]
     slots = neighbours.shape[1]
     step = 128
@@ -129,7 +135,7 @@
     held[0 : target.shape[0]] = jnp.where(slot < rows_here[0], target[...], 0.0)
 
 
-def distances(owned, place, rows_here, everyone, target, sums, target_held):
+def distances(owned, place, rows_here, everyone, target, done, sums, target_held):
     members = everyone.shape[0]
     masked_target(rows_here, target, target_held)
     lines = []
@@ -270,35 +276,38 @@
     def stay(array):
         return pltpu.with_memory_space_constraint(array, pltpu.HBM)
 
-    weights, rows, spread = call(
+    weights, rows, spread, mine = call(
         prepare,
-        (pltpu.VMEM(w_in.shape, bf16), pltpu.VMEM((ROWS, width), bf16), pltpu.VMEM((slots, 6 * nodes), bf16)),
-        [SMEM, HBM] + [VMEM] * 3,
-        (VMEM,) * 3,
+        (
+            pltpu.VMEM(w_in.shape, bf16), pltpu.VMEM((ROWS, width), bf16),
+            pltpu.VMEM((slots, 6 * nodes), bf16), pltpu.VMEM((members_dev * nodes, width), f32),
+        ),
+        [SMEM, VMEM, HBM] + [VMEM] * 3,
+        (VMEM,) * 4,
         [pltpu.VMEM((ROWS, width), f32), pltpu.SemaphoreType.DMA((4,))],
-        flops=1 << 22, moved=4 << 20,
-    )(where, stay(w_in), stay(w_out), stay(neighbours), stay(edge_weight))
+        flops=1 << 28, moved=4 << 20,
+    )(where, stay(latent), stay(w_in), stay(w_out), stay(neighbours), stay(edge_weight))
     sent, projected = call(
         forward,
         (pltpu.HBM((groups, *decoded), bf16), pltpu.HBM(kept, bf16)),
         [SMEM] + [VMEM] * 6,
         (HBM, HBM),
         [
-            pltpu.VMEM((3 * members_dev * nodes, width), bf16),
+            pltpu.VMEM((2 * members_dev * nodes, width), bf16),
             pltpu.VMEM(kept, bf16),
             pltpu.VMEM(decoded, bf16),
             pltpu.SemaphoreType.DMA((members_dev,)),
             pltpu.SemaphoreType.DMA((members_dev, groups)),
         ],
         flops=1 << 30, moved=8 << 20,
-    )(band_rows, before, stay(latent), after, weights, rows, spread)
+    )(band_rows, before, mine, after, weights, rows, spread)
 
     everyone = lax.all_to_all(sent, "member", 0, 0, tiled=True).reshape(members, ROWS, slots)
-    hidden, slope = call(
+    hidden, slope, done = call(
         activations,
-        (pltpu.VMEM(big, bf16), pltpu.HBM(big, bf16)),
+        (pltpu.VMEM(big, bf16), pltpu.HBM(big, bf16), shape((8, 128), f32)),
         [SMEM] + [VMEM] * 3,
-        (VMEM, HBM),
+        (VMEM, HBM, VMEM),
         [pltpu.VMEM(big, bf16), pltpu.SemaphoreType.DMA((members_dev, slots // 128))],
         flops=1 << 30, moved=8 << 20,
     )(where, stay(projected), stay(neighbours), stay(edge_weight))
@@ -307,9 +316,9 @@
         distances(members_dev, *refs)
 
     sums = call(
-        distances_body, shape((bands, 128), f32), [SMEM, SMEM, VMEM, VMEM], VMEM,
+        distances_body, shape((bands, 128), f32), [SMEM, SMEM, VMEM, VMEM, HBM], VMEM,
         [pltpu.VMEM((ROWS, slots), f32)], flops=1 << 22, moved=2 << 20,
-    )(mine_at, band_rows, everyone, target)
+    )(mine_at, band_rows, everyone, target, done)
     sums = lax.all_to_all(sums, "space", 0, 0, tiled=True)
 
     columns = width // bands

time: 116 us -> 114 us (0.983)
  blocking collectives: 0 us -> 30.9 us
  starting transfers between devices: 48.7 us -> 29.4 us
  waiting for transfers between devices: 42.3 us -> 29.7 us
  Pallas kernels: 23.2 us -> 21.9 us
    all_to_all x0 -> x1, blocking collectives: none -> 30.9 us  [per_device(): sums = lax.all_to_all(sums, 'space', 0, 0, tiled=True)]
    all_to_all x1 -> x0, starting transfers between devices: 18.4 us -> none  [per_device(): sums = lax.all_to_all(sums, 'space', 0, 0, tiled=True)]
    all_to_all x1 -> x0, waiting for transfers between devices: 8.81 us -> none  [per_device(): sums = lax.all_to_all(sums, 'space', 0, 0, tiled=True)]
    all_to_all x1, waiting for transfers between devices: 16 us -> 12.1 us  [per_device(): lax.all_to_all(sent, 'member', 0, 0, tiled=True)]
    pallas_call x1, Pallas kernels: 5.36 us -> 4.1 us  [per_device(): call(forward, (pltpu.HBM((groups, *decoded), bf16), pltpu.HBM(kept, bf16)...]
  transfers between devices with their start and end apart: 8 -> 7, of which waited for: 4 -> 3; matrix products, arithmetic and copies ran while one was open for 0% -> 0% of each run, Pallas kernels for 12% -> 13%
where the time goes in v4:
time: 114 us; the launch traced here: 113 us
  blocking collectives  30.9 us (27%)
  waiting for transfers between devices  29.7 us (26%)
  starting transfers between devices  29.4 us (26%)
  Pallas kernels  21.9 us (19%)
  between operations  1.42 us (1%)
    all_to_all x1, blocking collectives, per_device(): sums = lax.all_to_all(sums, 'space', 0, 0, tiled=True)  30.9 us
    all_to_all x1, waiting for transfers between devices, per_device(): lax.all_to_all(sent, 'member', 0, 0, tiled=True)  12.1 us
    all_to_all x1, waiting for transfers between devices, per_device(): weight_parts = lax.all_to_all(weight_parts, 'space', 0, 0, tiled=True)  12 us
    all_to_all x1, starting transfers between devices, per_device(): lax.all_to_all(sent, 'member', 0, 0, tiled=True)  5.68 us
    all_to_all x1, waiting for transfers between devices, per_device(): total = lax.all_to_all(total, 'member', 0, 0, tiled=True)  5.55 us
    ppermute x1, starting transfers between devices, per_device(): after = lax.ppermute(latent, 'space', down)  5.16 us
    ppermute x1, starting transfers between devices, per_device(): before = lax.ppermute(latent, 'space', up)  4.94 us
    all_to_all x1, starting transfers between devices, per_device(): weight_parts = lax.all_to_all(weight_parts, 'space', 0, 0, tiled=True)  4.78 us
  transfers between devices with their start and end apart: 7, of which 3 were waited for; matrix products, arithmetic and copies ran while one was open for 0% of the time, Pallas kernels for 13%

profile of v4, /device:TPU:1, one launch (start us, length us, event | category | flops | bytes accessed | tf_op | source)
XLA Modules:
  0.0 113.4 jit_solution(4325536954566545726)
XLA Ops:
  0.6 4.9 %collective-permute-start = (bf16[2,64,1024]{2,1,0:T(8,128)(2,1)}, bf16[2,64,1024]{2,1,0:T(8,128)(2,1)S(1)}, u32[]{:S(2)}, u32[]{:S(2)}) collective-permute-start(bf16[2,64,1024]{2,1,0:T(8,128)(2,1)} %own.1), channel_id=1, source_target_pairs={{0,1},{1,2},{2,3},{3,4},{4,5},{5,6},{6,7},{7,8},{8,9},{9,10},{10,1... | collective-permute-start | bytes 786440 | tf_op jit(solution)/shard_map/ppermute | solution.py:266
  5.6 5.2 %collective-permute-start.1 = (bf16[2,64,1024]{2,1,0:T(8,128)(2,1)}, bf16[2,64,1024]{2,1,0:T(8,128)(2,1)S(1)}, u32[]{:S(2)}, u32[]{:S(2)}) collective-permute-start(bf16[2,64,1024]{2,1,0:T(8,128)(2,1)} %own.1), channel_id=1, source_target_pairs={{1,0},{2,1},{3,2},{4,3},{5,4},{6,5},{7,6},{8,7},{9,8},{10,9},{11,1... | collective-permute-start | bytes 786440 | tf_op jit(solution)/shard_map/ppermute | solution.py:267
  11.4 3.0 %shard_map.94 = (bf16[1024,1024]{1,0:T(8,128)(2,1)S(1)}, bf16[72,1024]{1,0:T(8,128)(2,1)S(1)}, bf16[512,384]{1,0:T(8,128)(2,1)S(1)}, f32[128,1024]{1,0:T(8,128)S(1)}) custom-call(s32[1]{0:T(128)} %bitcast.1.place, bf16[2,64,1024]{2,1,0:T(8,128)(2,1)} %own.1, bf16[1024,1024]{1,0:T(8,128)(2,1)} %w_in.3, bf16[69,1024]{1,0:T(8,128)(2,1)} %w_out.3, ...), custom_call_target="tpu_custom_call" | custom-call | flops 268435456 | bytes 4194304 | tf_op jit(solution)/shard_map/pallas_call | solution.py:279
  14.4 0.0 collective-permute-done.before
  14.5 0.0 collective-permute-done.1.after
  14.5 4.1 %shard_map.95 = (bf16[8,2,72,512]{3,2,1,0:T(8,128)(2,1)}, bf16[2,384,1024]{2,1,0:T(8,128)(2,1)}) custom-call(s32[1]{0:T(128)S(6)} %copy.11.rows_here.refs_1_, bf16[2,64,1024]{2,1,0:T(8,128)(2,1)S(1)} %collective-permute-done.before, f32[128,1024]{1,0:T(8,128)S(1)} %get-tuple-element.20.mine, bf16[2,64,1024]{2,1,0:T(8,128)(2,1)S(1)} %collective-permute-done.1.after, ...), custom_call_target="tpu_custom_call" | custom-call | flops 1073741824 | bytes 8388608 | tf_op jit(solution)/shard_map/pallas_call | solution.py:290
  18.6 5.7 %all-to-all-start = ((bf16[8,2,72,512]{3,2,1,0:T(8,128)(2,1)}), bf16[8,2,72,512]{3,2,1,0:T(8,128)(2,1)S(1)}, u32[]{:S(2)}, u32[]{:S(2)}) async-start(bf16[8,2,72,512]{3,2,1,0:T(8,128)(2,1)} %get-tuple-element.24), calls=%async_computation | async-start | bytes 2359296 | tf_op jit(solution)/shard_map/all_to_all | solution.py:305
  24.2 0.0 copy-start.1
  24.3 4.4 %shard_map.96 = (bf16[2,512,1024]{2,1,0:T(8,128)(2,1)S(1)}, bf16[2,512,1024]{2,1,0:T(8,128)(2,1)}, f32[8,128]{1,0:T(8,128)S(1)}) custom-call(s32[1]{0:T(128)} %bitcast.1.place, bf16[2,384,1024]{2,1,0:T(8,128)(2,1)} %get-tuple-element.25.projected, s32[3,512]{1,0:T(4,128)} %neighbours.5, f32[3,512]{1,0:T(4,128)} %weight.5), custom_call_target="tpu_custom_call" | custom-call | flops 1073741824 | bytes 8388608 | tf_op jit(solution)/shard_map/pallas_call | solution.py:306
  28.7 12.1 %all-to-all-done = bf16[8,2,72,512]{3,2,1,0:T(8,128)(2,1)S(1)} async-done(((bf16[8,2,72,512]{3,2,1,0:T(8,128)(2,1)}), bf16[8,2,72,512]{3,2,1,0:T(8,128)(2,1)S(1)}, u32[]{:S(2)}, u32[]{:S(2)}) %all-to-all-start) | async-done | bytes 1179680 | tf_op jit(solution)/shard_map/all_to_all | solution.py:305
  40.8 0.0 copy-done.1
  40.8 0.8 shard_map.97
  41.6 30.9 %all_to_all.26 = f32[64,1,128]{2,1,0:T(1,128)S(1)} all-to-all(f32[64,1,128]{2,1,0:T(1,128)S(1)} %bitcast.12), channel_id=1, replica_groups=mesh['member'=8,'space'=64] {'space'}, dimensions={0} | all-to-all | bytes 65536 | tf_op jit(solution)/shard_map/all_to_all | solution.py:322
  72.5 2.0 %shard_map.98 = (bf16[2,72,512]{2,1,0:T(8,128)(2,1)}, bf16[64,16,128]{2,1,0:T(8,128)(2,1)}, f32[8,128]{1,0:T(8,128)S(1)}) custom-call(s32[1]{0:T(128)} %bitcast.refs_0_, s32[1]{0:T(128)S(6)} %copy.11.rows_here.refs_1_, f32[64,128]{1,0:T(8,128)S(1)} %bitcast.11, bf16[16,72,512]{2,1,0:T(8,128)(2,1)S(1)} %bitcast.10, f32[69,512]{1,0:T(8,128)S(1)} %copy-done.1, ...), custom_call_target="tpu_custom_call" | custom-call | flops 268435456 | bytes 4194304 | tf_op jit(solution)/shard_map/pallas_call | solution.py:330
  74.5 0.0 copy-start
  74.5 4.8 %all-to-all-start.2 = ((bf16[64,16,128]{2,1,0:T(8,128)(2,1)}), bf16[64,16,128]{2,1,0:T(8,128)(2,1)S(1)}, u32[]{:S(2)}, u32[]{:S(2)}) async-start(bf16[64,16,128]{2,1,0:T(8,128)(2,1)} %get-tuple-element.28), calls=%async_computation.2 | async-start | bytes 524288 | tf_op jit(solution)/shard_map/all_to_all | solution.py:344
  79.3 4.8 %shard_map.101 = (bf16[2,64,1024]{2,1,0:T(8,128)(2,1)}, f32[2,64,1024]{2,1,0:T(8,128)S(1)}, bf16[2,64,1024]{2,1,0:T(8,128)(2,1)}) custom-call(s32[1]{0:T(128)} %bitcast.1.place, bf16[2,72,512]{2,1,0:T(8,128)(2,1)} %get-tuple-element.31.grads, bf16[69,1024]{1,0:T(8,128)(2,1)} %w_out.3, bf16[2,512,1024]{2,1,0:T(8,128)(2,1)} %get-tuple-element.32.slope, ...), custom_call_target="tpu_custom_call" | custom-call | flops 536870912 | bytes 4194304 | tf_op jit(solution)/shard_map/pallas_call | solution.py:347
  84.0 2.5 %collective-permute-start.2 = (bf16[2,64,1024]{2,1,0:T(8,128)(2,1)}, bf16[2,64,1024]{2,1,0:T(8,128)(2,1)S(1)}, u32[]{:S(2)}, u32[]{:S(2)}) collective-permute-start(bf16[2,64,1024]{2,1,0:T(8,128)(2,1)} %get-tuple-element.34), channel_id=1, source_target_pairs={{1,0},{2,1},{3,2},{4,3},{5,4},{6,5},{7,6},{8,7},{9,8},{10,9},{11,1... | collective-permute-start | bytes 786440 | tf_op jit(solution)/shard_map/ppermute | solution.py:355
  86.5 3.1 %collective-permute-start.3 = (bf16[2,64,1024]{2,1,0:T(8,128)(2,1)}, bf16[2,64,1024]{2,1,0:T(8,128)(2,1)S(1)}, u32[]{:S(2)}, u32[]{:S(2)}) collective-permute-start(bf16[2,64,1024]{2,1,0:T(8,128)(2,1)} %get-tuple-element.35), channel_id=1, source_target_pairs={{0,1},{1,2},{2,3},{3,4},{4,5},{5,6},{6,7},{7,8},{8,9},{9,10},{10,1... | collective-permute-start | bytes 786440 | tf_op jit(solution)/shard_map/ppermute | solution.py:356
  89.6 12.0 %all-to-all-done.2.parts = bf16[64,16,128]{2,1,0:T(8,128)(2,1)S(1)} async-done(((bf16[64,16,128]{2,1,0:T(8,128)(2,1)}), bf16[64,16,128]{2,1,0:T(8,128)(2,1)S(1)}, u32[]{:S(2)}, u32[]{:S(2)}) %all-to-all-start.2) | async-done | bytes 262176 | tf_op jit(solution)/shard_map/all_to_all | solution.py:344
  101.6 0.7 shard_map.99
  102.3 3.3 %all-to-all-start.3 = ((f32[8,16,128]{2,1,0:T(8,128)}), f32[8,16,128]{2,1,0:T(8,128)S(1)}, u32[]{:S(2)}, u32[]{:S(2)}) async-start(f32[8,16,128]{2,1,0:T(8,128)} %shard_map.99), calls=%async_computation.3 | async-start | bytes 131072 | tf_op jit(solution)/shard_map/all_to_all | solution.py:364
  105.7 0.0 collective-permute-done.2.from_above
  105.7 0.0 collective-permute-done.3.from_below
  105.7 0.0 copy-done
  105.7 1.5 %shard_map.102 = bf16[2,64,1024]{2,1,0:T(8,128)(2,1)} custom-call(f32[2,64,1024]{2,1,0:T(8,128)S(1)} %get-tuple-element.33.middle, bf16[2,64,1024]{2,1,0:T(8,128)(2,1)S(1)} %collective-permute-done.2.from_above, bf16[2,64,1024]{2,1,0:T(8,128)(2,1)S(1)} %collective-permute-done.3.from_below, bf16[1024,1024]{1,0:T(8,128)(2,1)S(1)} %copy-done), custom_call_target="tpu_custom_call" | custom-call | flops 268435456 | bytes 4194304 | tf_op jit(solution)/shard_map/pallas_call | solution.py:357
  107.3 5.5 %all-to-all-done.3.parts = f32[8,16,128]{2,1,0:T(8,128)S(1)} async-done(((f32[8,16,128]{2,1,0:T(8,128)}), f32[8,16,128]{2,1,0:T(8,128)S(1)}, u32[]{:S(2)}, u32[]{:S(2)}) %all-to-all-start.3) | async-done | bytes 65568 | tf_op jit(solution)/shard_map/all_to_all | solution.py:364
  112.8 0.6 shard_map.100
Async XLA Ops:
  0.6 13.8 %collective-permute-start = (bf16[2,64,1024]{2,1,0:T(8,128)(2,1)}, bf16[2,64,1024]{2,1,0:T(8,128)(2,1)S(1)}, u32[]{:S(2)}, u32[]{:S(2)}) collective-permute-start(bf16[2,64,1024]{2,1,0:T(8,128)(2,1)} %own.1), channel_id=1, source_target_pairs={{0,1},{1,2},{2,3},{3,4},{4,5},{5,6},{6,7},{7,8},{8,9},{9,10},{10,1... | collective-permute-start | bytes 786440 | tf_op jit(solution)/shard_map/ppermute | solution.py:266
  5.6 8.9 %collective-permute-start.1 = (bf16[2,64,1024]{2,1,0:T(8,128)(2,1)}, bf16[2,64,1024]{2,1,0:T(8,128)(2,1)S(1)}, u32[]{:S(2)}, u32[]{:S(2)}) collective-permute-start(bf16[2,64,1024]{2,1,0:T(8,128)(2,1)} %own.1), channel_id=1, source_target_pairs={{1,0},{2,1},{3,2},{4,3},{5,4},{6,5},{7,6},{8,7},{9,8},{10,9},{11,1... | collective-permute-start | bytes 786440 | tf_op jit(solution)/shard_map/ppermute | solution.py:267
  18.6 22.2 %all-to-all-start = ((bf16[8,2,72,512]{3,2,1,0:T(8,128)(2,1)}), bf16[8,2,72,512]{3,2,1,0:T(8,128)(2,1)S(1)}, u32[]{:S(2)}, u32[]{:S(2)}) async-start(bf16[8,2,72,512]{3,2,1,0:T(8,128)(2,1)} %get-tuple-element.24), calls=%async_computation | async-start | bytes 2359296 | tf_op jit(solution)/shard_map/all_to_all | solution.py:305
  24.2 16.6 %copy-start.1 = (f32[69,512]{1,0:T(8,128)S(1)}, f32[69,512]{1,0:T(8,128)}, u32[]{:S(2)}) copy-start(f32[69,512]{1,0:T(8,128)} %refs_4_.1) | copy-start | bytes 423940
  74.5 31.3 %copy-start = (bf16[1024,1024]{1,0:T(8,128)(2,1)S(1)}, bf16[1024,1024]{1,0:T(8,128)(2,1)}, u32[]{:S(2)}) copy-start(bf16[1024,1024]{1,0:T(8,128)(2,1)} %w_in.3) | copy-start | bytes 6291460
  74.5 27.2 %all-to-all-start.2 = ((bf16[64,16,128]{2,1,0:T(8,128)(2,1)}), bf16[64,16,128]{2,1,0:T(8,128)(2,1)S(1)}, u32[]{:S(2)}, u32[]{:S(2)}) async-start(bf16[64,16,128]{2,1,0:T(8,128)(2,1)} %get-tuple-element.28), calls=%async_computation.2 | async-start | bytes 524288 | tf_op jit(solution)/shard_map/all_to_all | solution.py:344
  84.0 21.7 %collective-permute-start.2 = (bf16[2,64,1024]{2,1,0:T(8,128)(2,1)}, bf16[2,64,1024]{2,1,0:T(8,128)(2,1)S(1)}, u32[]{:S(2)}, u32[]{:S(2)}) collective-permute-start(bf16[2,64,1024]{2,1,0:T(8,128)(2,1)} %get-tuple-element.34), channel_id=1, source_target_pairs={{1,0},{2,1},{3,2},{4,3},{5,4},{6,5},{7,6},{8,7},{9,8},{10,9},{11,1... | collective-permute-start | bytes 786440 | tf_op jit(solution)/shard_map/ppermute | solution.py:355
  86.5 19.2 %collective-permute-start.3 = (bf16[2,64,1024]{2,1,0:T(8,128)(2,1)}, bf16[2,64,1024]{2,1,0:T(8,128)(2,1)S(1)}, u32[]{:S(2)}, u32[]{:S(2)}) collective-permute-start(bf16[2,64,1024]{2,1,0:T(8,128)(2,1)} %get-tuple-element.35), channel_id=1, source_target_pairs={{0,1},{1,2},{2,3},{3,4},{4,5},{5,6},{6,7},{7,8},{8,9},{9,10},{10,1... | collective-permute-start | bytes 786440 | tf_op jit(solution)/shard_map/ppermute | solution.py:356
  102.3 10.5 %all-to-all-start.3 = ((f32[8,16,128]{2,1,0:T(8,128)}), f32[8,16,128]{2,1,0:T(8,128)S(1)}, u32[]{:S(2)}, u32[]{:S(2)}) async-start(f32[8,16,128]{2,1,0:T(8,128)} %shard_map.99), calls=%async_computation.3 | async-start | bytes 131072 | tf_op jit(solution)/shard_map/all_to_all | solution.py:364

commit v5 on v4

--- a/solution.py
+++ b/solution.py
@@ -13,6 +13,7 @@
 NT = (((1,), (1,)), ((), ()))
 ROWS = 72
 ACROSS = 128
+QUAD = 4
 
 
 HBM = pl.BlockSpec(memory_space=pltpu.HBM)
@@ -155,10 +156,29 @@
     sums[...] = jnp.broadcast_to(line, sums.shape)
 
 
+def packed(tall):
+    rows = tall.shape[0] // QUAD
+    column = [tall[pl.ds(k, rows, stride=QUAD), :] for k in range(QUAD)]
+    lane = lax.broadcasted_iota(jnp.int32, (rows, ACROSS), 1)
+    half = ACROSS // 2
+    over = ROWS - half
+    rest = pltpu.roll(column[0], half, 1)
+    for k in range(1, QUAD):
+        rest = jnp.where(lane < k * over, rest, pltpu.roll(column[k], half + k * over, 1))
+    return jnp.concatenate(
+        [
+            jnp.where(lane < half, column[0], pltpu.roll(column[1], half, 1)),
+            jnp.where(lane < half, column[2], pltpu.roll(column[3], half, 1)),
+            rest,
+        ],
+        axis=1,
+    )
+
+
 def output_grads(
     variables, place, rows_here, sums, everyone, target, hidden,
     grads, weight_grad, share,
-    target_held, shown, parts_held, shown_sems, parts_sems,
+    target_held, shown, tall_held, parts_held, shown_sems, parts_sems,
 ):
     members = everyone.shape[0]
     held = grads.shape[0]
@@ -194,7 +214,8 @@
     for a in range(1, held):
         total = total + jnp.dot(shown[a], hidden[a], preferred_element_type=f32)
     tall = jnp.concatenate([total, jnp.zeros((ACROSS - total.shape[0], total.shape[1]), f32)], axis=0)
-    parts_held[...] = tall.T.astype(bf16).reshape(parts_held.shape)
+    tall_held[...] = tall.T
+    parts_held[...] = packed(tall_held).astype(bf16).reshape(parts_held.shape)
     pieces = min(parts_sems.shape[0], parts_held.shape[0])
     step = parts_held.shape[0] // pieces
     for index in range(pieces):
@@ -241,7 +262,7 @@
 def gathered_sum(parts, share, out):
     total = jnp.sum(parts[...].astype(f32), axis=0)
     lane = lax.broadcasted_iota(jnp.int32, total.shape, 1)
-    total = jnp.where(lane == ACROSS - 1, share[0:1, 0:1], total)
+    total = jnp.where(lane == total.shape[1] - 1, share[0:1, 0:1], total)
     out[...] = jnp.broadcast_to(total[None], out.shape)
 
 
@@ -249,8 +270,14 @@
     total = parts[0]
     for k in range(1, parts.shape[0]):
         total = total + parts[k]
-    weight_grad[...] = total[:, : weight_grad.shape[1]]
-    score[...] = total[0:1, ACROSS - 1 :]
+    half = ACROSS // 2
+    over = weight_grad.shape[1] - half
+    for row in range(total.shape[0]):
+        for k in range(QUAD):
+            first, last = k * half, 2 * ACROSS + k * (ROWS - half)
+            weight_grad[row * QUAD + k : row * QUAD + k + 1, :half] = total[row : row + 1, first : first + half]
+            weight_grad[row * QUAD + k : row * QUAD + k + 1, half:] = total[row : row + 1, last : last + over]
+    score[...] = total[0:1, 3 * ACROSS - 1 :]
 
 
 def per_device(latent, edge_weight, neighbours, band_rows, w_in, w_out, target):
@@ -322,7 +349,7 @@
     sums = lax.all_to_all(sums, "space", 0, 0, tiled=True)
 
     columns = width // bands
-    tiles = (bands, columns, ACROSS)
+    tiles = (bands, columns // QUAD, 3 * ACROSS)
 
     def grads_body(*refs):
         output_grads(variables, *refs)
@@ -335,6 +362,7 @@
         [
             pltpu.VMEM((ROWS, slots), f32),
             pltpu.VMEM(decoded, bf16),
+            pltpu.VMEM((width, ACROSS), f32),
             pltpu.VMEM(tiles, bf16),
             pltpu.SemaphoreType.DMA((members_dev,)),
             pltpu.SemaphoreType.DMA((4,)),
@@ -359,7 +387,7 @@
     )(middle, from_above, from_below, w_in)
 
     total = call(
-        gathered_sum, shape((groups, columns, ACROSS), f32), [VMEM] * 2, VMEM, flops=1 << 18, moved=1 << 18
+        gathered_sum, shape((groups, *tiles[1:]), f32), [VMEM] * 2, VMEM, flops=1 << 18, moved=1 << 18
     )(weight_parts, share)
     total = lax.all_to_all(total, "member", 0, 0, tiled=True)
     grad_w_out, score = call(

time: 114 us -> 111 us (0.974)
  waiting for transfers between devices: 29.7 us -> 26.7 us
    all_to_all x1, waiting for transfers between devices: 12 us -> 9.49 us  [per_device(): weight_parts = lax.all_to_all(weight_parts, 'space', 0, 0, tiled=True)]
where the time goes in v5:
time: 111 us
  blocking collectives  30.9 us (28%)
  starting transfers between devices  29.4 us (26%)
  waiting for transfers between devices  26.7 us (24%)
  Pallas kernels  22.3 us (20%)
  between operations  1.42 us (1%)
    all_to_all x1, blocking collectives, per_device(): sums = lax.all_to_all(sums, 'space', 0, 0, tiled=True)  30.9 us
    all_to_all x1, waiting for transfers between devices, per_device(): lax.all_to_all(sent, 'member', 0, 0, tiled=True)  12.1 us
    all_to_all x1, waiting for transfers between devices, per_device(): weight_parts = lax.all_to_all(weight_parts, 'space', 0, 0, tiled=True)  9.49 us
    all_to_all x1, starting transfers between devices, per_device(): lax.all_to_all(sent, 'member', 0, 0, tiled=True)  5.68 us
    ppermute x1, starting transfers between devices, per_device(): after = lax.ppermute(latent, 'space', down)  5.16 us
    all_to_all x1, waiting for transfers between devices, per_device(): total = lax.all_to_all(total, 'member', 0, 0, tiled=True)  5.02 us
    ppermute x1, starting transfers between devices, per_device(): before = lax.ppermute(latent, 'space', up)  4.94 us
    all_to_all x1, starting transfers between devices, per_device(): weight_parts = lax.all_to_all(weight_parts, 'space', 0, 0, tiled=True)  4.78 us
  transfers between devices with their start and end apart: 7, of which 3 were waited for; matrix products, arithmetic and copies ran while one was open for 0% of the time, Pallas kernels for 13%

profile of v5, /device:TPU:1, one launch (start us, length us, event | category | flops | bytes accessed | tf_op | source)
XLA Modules:
  0.0 110.7 jit_solution(349319376229003470)
XLA Ops:
  0.6 4.9 %collective-permute-start = (bf16[2,64,1024]{2,1,0:T(8,128)(2,1)}, bf16[2,64,1024]{2,1,0:T(8,128)(2,1)S(1)}, u32[]{:S(2)}, u32[]{:S(2)}) collective-permute-start(bf16[2,64,1024]{2,1,0:T(8,128)(2,1)} %own.1), channel_id=1, source_target_pairs={{0,1},{1,2},{2,3},{3,4},{4,5},{5,6},{6,7},{7,8},{8,9},{9,10},{10,1... | collective-permute-start | bytes 786440 | tf_op jit(solution)/shard_map/ppermute | solution.py:293
  5.6 5.2 %collective-permute-start.1 = (bf16[2,64,1024]{2,1,0:T(8,128)(2,1)}, bf16[2,64,1024]{2,1,0:T(8,128)(2,1)S(1)}, u32[]{:S(2)}, u32[]{:S(2)}) collective-permute-start(bf16[2,64,1024]{2,1,0:T(8,128)(2,1)} %own.1), channel_id=1, source_target_pairs={{1,0},{2,1},{3,2},{4,3},{5,4},{6,5},{7,6},{8,7},{9,8},{10,9},{11,1... | collective-permute-start | bytes 786440 | tf_op jit(solution)/shard_map/ppermute | solution.py:294
  11.4 3.0 %shard_map.94 = (bf16[1024,1024]{1,0:T(8,128)(2,1)S(1)}, bf16[72,1024]{1,0:T(8,128)(2,1)S(1)}, bf16[512,384]{1,0:T(8,128)(2,1)S(1)}, f32[128,1024]{1,0:T(8,128)S(1)}) custom-call(s32[1]{0:T(128)} %bitcast.1.place, bf16[2,64,1024]{2,1,0:T(8,128)(2,1)} %own.1, bf16[1024,1024]{1,0:T(8,128)(2,1)} %w_in.3, bf16[69,1024]{1,0:T(8,128)(2,1)} %w_out.3, ...), custom_call_target="tpu_custom_call" | custom-call | flops 268435456 | bytes 4194304 | tf_op jit(solution)/shard_map/pallas_call | solution.py:306
  14.4 0.0 collective-permute-done.before
  14.5 0.0 collective-permute-done.1.after
  14.5 4.1 %shard_map.95 = (bf16[8,2,72,512]{3,2,1,0:T(8,128)(2,1)}, bf16[2,384,1024]{2,1,0:T(8,128)(2,1)}) custom-call(s32[1]{0:T(128)S(6)} %copy.11.rows_here.refs_1_, bf16[2,64,1024]{2,1,0:T(8,128)(2,1)S(1)} %collective-permute-done.before, f32[128,1024]{1,0:T(8,128)S(1)} %get-tuple-element.20.mine, bf16[2,64,1024]{2,1,0:T(8,128)(2,1)S(1)} %collective-permute-done.1.after, ...), custom_call_target="tpu_custom_call" | custom-call | flops 1073741824 | bytes 8388608 | tf_op jit(solution)/shard_map/pallas_call | solution.py:317
  18.6 5.7 %all-to-all-start = ((bf16[8,2,72,512]{3,2,1,0:T(8,128)(2,1)}), bf16[8,2,72,512]{3,2,1,0:T(8,128)(2,1)S(1)}, u32[]{:S(2)}, u32[]{:S(2)}) async-start(bf16[8,2,72,512]{3,2,1,0:T(8,128)(2,1)} %get-tuple-element.24), calls=%async_computation | async-start | bytes 2359296 | tf_op jit(solution)/shard_map/all_to_all | solution.py:332
  24.2 0.0 copy-start.1
  24.3 4.4 %shard_map.96 = (bf16[2,512,1024]{2,1,0:T(8,128)(2,1)S(1)}, bf16[2,512,1024]{2,1,0:T(8,128)(2,1)}, f32[8,128]{1,0:T(8,128)S(1)}) custom-call(s32[1]{0:T(128)} %bitcast.1.place, bf16[2,384,1024]{2,1,0:T(8,128)(2,1)} %get-tuple-element.25.projected, s32[3,512]{1,0:T(4,128)} %neighbours.5, f32[3,512]{1,0:T(4,128)} %weight.5), custom_call_target="tpu_custom_call" | custom-call | flops 1073741824 | bytes 8388608 | tf_op jit(solution)/shard_map/pallas_call | solution.py:333
  28.7 12.1 %all-to-all-done = bf16[8,2,72,512]{3,2,1,0:T(8,128)(2,1)S(1)} async-done(((bf16[8,2,72,512]{3,2,1,0:T(8,128)(2,1)}), bf16[8,2,72,512]{3,2,1,0:T(8,128)(2,1)S(1)}, u32[]{:S(2)}, u32[]{:S(2)}) %all-to-all-start) | async-done | bytes 1179680 | tf_op jit(solution)/shard_map/all_to_all | solution.py:332
  40.8 0.0 copy-done.1
  40.8 0.8 shard_map.97
  41.6 30.9 %all_to_all.26 = f32[64,1,128]{2,1,0:T(1,128)S(1)} all-to-all(f32[64,1,128]{2,1,0:T(1,128)S(1)} %bitcast.12), channel_id=1, replica_groups=mesh['member'=8,'space'=64] {'space'}, dimensions={0} | all-to-all | bytes 65536 | tf_op jit(solution)/shard_map/all_to_all | solution.py:349
  72.5 2.2 %shard_map.98 = (bf16[2,72,512]{2,1,0:T(8,128)(2,1)}, bf16[64,4,384]{2,1,0:T(4,128)(2,1)}, f32[8,128]{1,0:T(8,128)S(1)}) custom-call(s32[1]{0:T(128)} %bitcast.refs_0_, s32[1]{0:T(128)S(6)} %copy.11.rows_here.refs_1_, f32[64,128]{1,0:T(8,128)S(1)} %bitcast.11, bf16[16,72,512]{2,1,0:T(8,128)(2,1)S(1)} %bitcast.10, f32[69,512]{1,0:T(8,128)S(1)} %copy-done.1, ...), custom_call_target="tpu_custom_call" | custom-call | flops 268435456 | bytes 4194304 | tf_op jit(solution)/shard_map/pallas_call | solution.py:357
  74.7 0.0 copy-start
  74.7 4.8 %all-to-all-start.2 = ((bf16[64,4,384]{2,1,0:T(4,128)(2,1)}), bf16[64,4,384]{2,1,0:T(4,128)(2,1)S(1)}, u32[]{:S(2)}, u32[]{:S(2)}) async-start(bf16[64,4,384]{2,1,0:T(4,128)(2,1)} %get-tuple-element.28), calls=%async_computation.2 | async-start | bytes 393216 | tf_op jit(solution)/shard_map/all_to_all | solution.py:372
  79.5 4.8 %shard_map.101 = (bf16[2,64,1024]{2,1,0:T(8,128)(2,1)}, f32[2,64,1024]{2,1,0:T(8,128)S(1)}, bf16[2,64,1024]{2,1,0:T(8,128)(2,1)}) custom-call(s32[1]{0:T(128)} %bitcast.1.place, bf16[2,72,512]{2,1,0:T(8,128)(2,1)} %get-tuple-element.31.grads, bf16[69,1024]{1,0:T(8,128)(2,1)} %w_out.3, bf16[2,512,1024]{2,1,0:T(8,128)(2,1)} %get-tuple-element.32.slope, ...), custom_call_target="tpu_custom_call" | custom-call | flops 536870912 | bytes 4194304 | tf_op jit(solution)/shard_map/pallas_call | solution.py:375
  84.3 2.5 %collective-permute-start.2 = (bf16[2,64,1024]{2,1,0:T(8,128)(2,1)}, bf16[2,64,1024]{2,1,0:T(8,128)(2,1)S(1)}, u32[]{:S(2)}, u32[]{:S(2)}) collective-permute-start(bf16[2,64,1024]{2,1,0:T(8,128)(2,1)} %get-tuple-element.34), channel_id=1, source_target_pairs={{1,0},{2,1},{3,2},{4,3},{5,4},{6,5},{7,6},{8,7},{9,8},{10,9},{11,1... | collective-permute-start | bytes 786440 | tf_op jit(solution)/shard_map/ppermute | solution.py:383
  86.7 3.1 %collective-permute-start.3 = (bf16[2,64,1024]{2,1,0:T(8,128)(2,1)}, bf16[2,64,1024]{2,1,0:T(8,128)(2,1)S(1)}, u32[]{:S(2)}, u32[]{:S(2)}) collective-permute-start(bf16[2,64,1024]{2,1,0:T(8,128)(2,1)} %get-tuple-element.35), channel_id=1, source_target_pairs={{0,1},{1,2},{2,3},{3,4},{4,5},{5,6},{6,7},{7,8},{8,9},{9,10},{10,1... | collective-permute-start | bytes 786440 | tf_op jit(solution)/shard_map/ppermute | solution.py:384
  89.8 9.5 %all-to-all-done.2.parts = bf16[64,4,384]{2,1,0:T(4,128)(2,1)S(1)} async-done(((bf16[64,4,384]{2,1,0:T(4,128)(2,1)}), bf16[64,4,384]{2,1,0:T(4,128)(2,1)S(1)}, u32[]{:S(2)}, u32[]{:S(2)}) %all-to-all-start.2) | async-done | bytes 196640 | tf_op jit(solution)/shard_map/all_to_all | solution.py:372
  99.3 0.7 shard_map.99
  100.0 3.3 %all-to-all-start.3 = ((f32[8,4,384]{2,1,0:T(4,128)}), f32[8,4,384]{2,1,0:T(4,128)S(1)}, u32[]{:S(2)}, u32[]{:S(2)}) async-start(f32[8,4,384]{2,1,0:T(4,128)} %shard_map.99), calls=%async_computation.3 | async-start | bytes 98304 | tf_op jit(solution)/shard_map/all_to_all | solution.py:392
  103.4 0.0 collective-permute-done.2.from_above
  103.4 0.0 collective-permute-done.3.from_below
  103.4 0.0 copy-done
  103.4 1.5 %shard_map.102 = bf16[2,64,1024]{2,1,0:T(8,128)(2,1)} custom-call(f32[2,64,1024]{2,1,0:T(8,128)S(1)} %get-tuple-element.33.middle, bf16[2,64,1024]{2,1,0:T(8,128)(2,1)S(1)} %collective-permute-done.2.from_above, bf16[2,64,1024]{2,1,0:T(8,128)(2,1)S(1)} %collective-permute-done.3.from_below, bf16[1024,1024]{1,0:T(8,128)(2,1)S(1)} %copy-done), custom_call_target="tpu_custom_call" | custom-call | flops 268435456 | bytes 4194304 | tf_op jit(solution)/shard_map/pallas_call | solution.py:385
  105.0 5.0 %all-to-all-done.3.parts = f32[8,4,384]{2,1,0:T(4,128)S(1)} async-done(((f32[8,4,384]{2,1,0:T(4,128)}), f32[8,4,384]{2,1,0:T(4,128)S(1)}, u32[]{:S(2)}, u32[]{:S(2)}) %all-to-all-start.3) | async-done | bytes 49184 | tf_op jit(solution)/shard_map/all_to_all | solution.py:392
  110.0 0.7 shard_map.100
Async XLA Ops:
  0.6 13.8 %collective-permute-start = (bf16[2,64,1024]{2,1,0:T(8,128)(2,1)}, bf16[2,64,1024]{2,1,0:T(8,128)(2,1)S(1)}, u32[]{:S(2)}, u32[]{:S(2)}) collective-permute-start(bf16[2,64,1024]{2,1,0:T(8,128)(2,1)} %own.1), channel_id=1, source_target_pairs={{0,1},{1,2},{2,3},{3,4},{4,5},{5,6},{6,7},{7,8},{8,9},{9,10},{10,1... | collective-permute-start | bytes 786440 | tf_op jit(solution)/shard_map/ppermute | solution.py:293
  5.6 8.9 %collective-permute-start.1 = (bf16[2,64,1024]{2,1,0:T(8,128)(2,1)}, bf16[2,64,1024]{2,1,0:T(8,128)(2,1)S(1)}, u32[]{:S(2)}, u32[]{:S(2)}) collective-permute-start(bf16[2,64,1024]{2,1,0:T(8,128)(2,1)} %own.1), channel_id=1, source_target_pairs={{1,0},{2,1},{3,2},{4,3},{5,4},{6,5},{7,6},{8,7},{9,8},{10,9},{11,1... | collective-permute-start | bytes 786440 | tf_op jit(solution)/shard_map/ppermute | solution.py:294
  18.6 22.2 %all-to-all-start = ((bf16[8,2,72,512]{3,2,1,0:T(8,128)(2,1)}), bf16[8,2,72,512]{3,2,1,0:T(8,128)(2,1)S(1)}, u32[]{:S(2)}, u32[]{:S(2)}) async-start(bf16[8,2,72,512]{3,2,1,0:T(8,128)(2,1)} %get-tuple-element.24), calls=%async_computation | async-start | bytes 2359296 | tf_op jit(solution)/shard_map/all_to_all | solution.py:332
  24.2 16.6 %copy-start.1 = (f32[69,512]{1,0:T(8,128)S(1)}, f32[69,512]{1,0:T(8,128)}, u32[]{:S(2)}) copy-start(f32[69,512]{1,0:T(8,128)} %refs_4_.1) | copy-start | bytes 423940
  74.7 28.7 %copy-start = (bf16[1024,1024]{1,0:T(8,128)(2,1)S(1)}, bf16[1024,1024]{1,0:T(8,128)(2,1)}, u32[]{:S(2)}) copy-start(bf16[1024,1024]{1,0:T(8,128)(2,1)} %w_in.3) | copy-start | bytes 6291460
  74.7 24.6 %all-to-all-start.2 = ((bf16[64,4,384]{2,1,0:T(4,128)(2,1)}), bf16[64,4,384]{2,1,0:T(4,128)(2,1)S(1)}, u32[]{:S(2)}, u32[]{:S(2)}) async-start(bf16[64,4,384]{2,1,0:T(4,128)(2,1)} %get-tuple-element.28), calls=%async_computation.2 | async-start | bytes 393216 | tf_op jit(solution)/shard_map/all_to_all | solution.py:372
  84.3 19.1 %collective-permute-start.2 = (bf16[2,64,1024]{2,1,0:T(8,128)(2,1)}, bf16[2,64,1024]{2,1,0:T(8,128)(2,1)S(1)}, u32[]{:S(2)}, u32[]{:S(2)}) collective-permute-start(bf16[2,64,1024]{2,1,0:T(8,128)(2,1)} %get-tuple-element.34), channel_id=1, source_target_pairs={{1,0},{2,1},{3,2},{4,3},{5,4},{6,5},{7,6},{8,7},{9,8},{10,9},{11,1... | collective-permute-start | bytes 786440 | tf_op jit(solution)/shard_map/ppermute | solution.py:383
  86.7 16.7 %collective-permute-start.3 = (bf16[2,64,1024]{2,1,0:T(8,128)(2,1)}, bf16[2,64,1024]{2,1,0:T(8,128)(2,1)S(1)}, u32[]{:S(2)}, u32[]{:S(2)}) collective-permute-start(bf16[2,64,1024]{2,1,0:T(8,128)(2,1)} %get-tuple-element.35), channel_id=1, source_target_pairs={{0,1},{1,2},{2,3},{3,4},{4,5},{5,6},{6,7},{7,8},{8,9},{9,10},{10,1... | collective-permute-start | bytes 786440 | tf_op jit(solution)/shard_map/ppermute | solution.py:384
  100.0 9.9 %all-to-all-start.3 = ((f32[8,4,384]{2,1,0:T(4,128)}), f32[8,4,384]{2,1,0:T(4,128)S(1)}, u32[]{:S(2)}, u32[]{:S(2)}) async-start(f32[8,4,384]{2,1,0:T(4,128)} %shard_map.99), calls=%async_computation.3 | async-start | bytes 98304 | tf_op jit(solution)/shard_map/all_to_all | solution.py:392

commit v6 on v5

--- a/solution.py
+++ b/solution.py
@@ -66,7 +66,7 @@
 ):
     members, nodes, _ = before.shape
     slots = spread.shape[0]
-    step = 128
+    step = 512
     around = 3 * nodes
     both = members * nodes
     latents[:both] = before[...].reshape(both, -1)

time: 111 us -> 111 us (level)
  no operation moved by 1% of the time
where the time goes in v6:
time: 111 us; the launch traced here: 110 us
  blocking collectives  30.9 us (28%)
  starting transfers between devices  29.4 us (26%)
  waiting for transfers between devices  26.7 us (24%)
  Pallas kernels  21.6 us (19%)
  between operations  1.42 us (1%)
    all_to_all x1, blocking collectives, per_device(): sums = lax.all_to_all(sums, 'space', 0, 0, tiled=True)  30.9 us
    all_to_all x1, waiting for transfers between devices, per_device(): lax.all_to_all(sent, 'member', 0, 0, tiled=True)  12.1 us
    all_to_all x1, waiting for transfers between devices, per_device(): weight_parts = lax.all_to_all(weight_parts, 'space', 0, 0, tiled=True)  9.49 us
    all_to_all x1, starting transfers between devices, per_device(): lax.all_to_all(sent, 'member', 0, 0, tiled=True)  5.67 us
    ppermute x1, starting transfers between devices, per_device(): after = lax.ppermute(latent, 'space', down)  5.16 us
    all_to_all x1, waiting for transfers between devices, per_device(): total = lax.all_to_all(total, 'member', 0, 0, tiled=True)  5.02 us
    ppermute x1, starting transfers between devices, per_device(): before = lax.ppermute(latent, 'space', up)  4.94 us
    all_to_all x1, starting transfers between devices, per_device(): weight_parts = lax.all_to_all(weight_parts, 'space', 0, 0, tiled=True)  4.78 us
  transfers between devices with their start and end apart: 7, of which 3 were waited for; matrix products, arithmetic and copies ran while one was open for 0% of the time, Pallas kernels for 13%

profile of v6, /device:TPU:1, one launch (start us, length us, event | category | flops | bytes accessed | tf_op | source)
XLA Modules:
  0.0 110.0 jit_solution(7842014459030121437)
XLA Ops:
  0.6 4.9 %collective-permute-start = (bf16[2,64,1024]{2,1,0:T(8,128)(2,1)}, bf16[2,64,1024]{2,1,0:T(8,128)(2,1)S(1)}, u32[]{:S(2)}, u32[]{:S(2)}) collective-permute-start(bf16[2,64,1024]{2,1,0:T(8,128)(2,1)} %own.1), channel_id=1, source_target_pairs={{0,1},{1,2},{2,3},{3,4},{4,5},{5,6},{6,7},{7,8},{8,9},{9,10},{10,1... | collective-permute-start | bytes 786440 | tf_op jit(solution)/shard_map/ppermute | solution.py:293
  5.6 5.2 %collective-permute-start.1 = (bf16[2,64,1024]{2,1,0:T(8,128)(2,1)}, bf16[2,64,1024]{2,1,0:T(8,128)(2,1)S(1)}, u32[]{:S(2)}, u32[]{:S(2)}) collective-permute-start(bf16[2,64,1024]{2,1,0:T(8,128)(2,1)} %own.1), channel_id=1, source_target_pairs={{1,0},{2,1},{3,2},{4,3},{5,4},{6,5},{7,6},{8,7},{9,8},{10,9},{11,1... | collective-permute-start | bytes 786440 | tf_op jit(solution)/shard_map/ppermute | solution.py:294
  11.4 3.0 %shard_map.94 = (bf16[1024,1024]{1,0:T(8,128)(2,1)S(1)}, bf16[72,1024]{1,0:T(8,128)(2,1)S(1)}, bf16[512,384]{1,0:T(8,128)(2,1)S(1)}, f32[128,1024]{1,0:T(8,128)S(1)}) custom-call(s32[1]{0:T(128)} %bitcast.1.place, bf16[2,64,1024]{2,1,0:T(8,128)(2,1)} %own.1, bf16[1024,1024]{1,0:T(8,128)(2,1)} %w_in.3, bf16[69,1024]{1,0:T(8,128)(2,1)} %w_out.3, ...), custom_call_target="tpu_custom_call" | custom-call | flops 268435456 | bytes 4194304 | tf_op jit(solution)/shard_map/pallas_call | solution.py:306
  14.4 0.0 collective-permute-done.before
  14.5 0.0 collective-permute-done.1.after
  14.5 3.4 %shard_map.95 = (bf16[8,2,72,512]{3,2,1,0:T(8,128)(2,1)}, bf16[2,384,1024]{2,1,0:T(8,128)(2,1)}) custom-call(s32[1]{0:T(128)S(6)} %copy.11.rows_here.refs_1_, bf16[2,64,1024]{2,1,0:T(8,128)(2,1)S(1)} %collective-permute-done.before, f32[128,1024]{1,0:T(8,128)S(1)} %get-tuple-element.20.mine, bf16[2,64,1024]{2,1,0:T(8,128)(2,1)S(1)} %collective-permute-done.1.after, ...), custom_call_target="tpu_custom_call" | custom-call | flops 1073741824 | bytes 8388608 | tf_op jit(solution)/shard_map/pallas_call | solution.py:317
  17.9 5.7 %all-to-all-start = ((bf16[8,2,72,512]{3,2,1,0:T(8,128)(2,1)}), bf16[8,2,72,512]{3,2,1,0:T(8,128)(2,1)S(1)}, u32[]{:S(2)}, u32[]{:S(2)}) async-start(bf16[8,2,72,512]{3,2,1,0:T(8,128)(2,1)} %get-tuple-element.24), calls=%async_computation | async-start | bytes 2359296 | tf_op jit(solution)/shard_map/all_to_all | solution.py:332
  23.6 0.0 copy-start.1
  23.6 4.4 %shard_map.96 = (bf16[2,512,1024]{2,1,0:T(8,128)(2,1)S(1)}, bf16[2,512,1024]{2,1,0:T(8,128)(2,1)}, f32[8,128]{1,0:T(8,128)S(1)}) custom-call(s32[1]{0:T(128)} %bitcast.1.place, bf16[2,384,1024]{2,1,0:T(8,128)(2,1)} %get-tuple-element.25.projected, s32[3,512]{1,0:T(4,128)} %neighbours.5, f32[3,512]{1,0:T(4,128)} %weight.5), custom_call_target="tpu_custom_call" | custom-call | flops 1073741824 | bytes 8388608 | tf_op jit(solution)/shard_map/pallas_call | solution.py:333
  28.0 12.1 %all-to-all-done = bf16[8,2,72,512]{3,2,1,0:T(8,128)(2,1)S(1)} async-done(((bf16[8,2,72,512]{3,2,1,0:T(8,128)(2,1)}), bf16[8,2,72,512]{3,2,1,0:T(8,128)(2,1)S(1)}, u32[]{:S(2)}, u32[]{:S(2)}) %all-to-all-start) | async-done | bytes 1179680 | tf_op jit(solution)/shard_map/all_to_all | solution.py:332
  40.1 0.0 copy-done.1
  40.1 0.8 shard_map.97
  40.9 30.9 %all_to_all.26 = f32[64,1,128]{2,1,0:T(1,128)S(1)} all-to-all(f32[64,1,128]{2,1,0:T(1,128)S(1)} %bitcast.12), channel_id=1, replica_groups=mesh['member'=8,'space'=64] {'space'}, dimensions={0} | all-to-all | bytes 65536 | tf_op jit(solution)/shard_map/all_to_all | solution.py:349
  71.8 2.2 %shard_map.98 = (bf16[2,72,512]{2,1,0:T(8,128)(2,1)}, bf16[64,4,384]{2,1,0:T(4,128)(2,1)}, f32[8,128]{1,0:T(8,128)S(1)}) custom-call(s32[1]{0:T(128)} %bitcast.refs_0_, s32[1]{0:T(128)S(6)} %copy.11.rows_here.refs_1_, f32[64,128]{1,0:T(8,128)S(1)} %bitcast.11, bf16[16,72,512]{2,1,0:T(8,128)(2,1)S(1)} %bitcast.10, f32[69,512]{1,0:T(8,128)S(1)} %copy-done.1, ...), custom_call_target="tpu_custom_call" | custom-call | flops 268435456 | bytes 4194304 | tf_op jit(solution)/shard_map/pallas_call | solution.py:357
  74.0 0.0 copy-start
  74.1 4.8 %all-to-all-start.2 = ((bf16[64,4,384]{2,1,0:T(4,128)(2,1)}), bf16[64,4,384]{2,1,0:T(4,128)(2,1)S(1)}, u32[]{:S(2)}, u32[]{:S(2)}) async-start(bf16[64,4,384]{2,1,0:T(4,128)(2,1)} %get-tuple-element.28), calls=%async_computation.2 | async-start | bytes 393216 | tf_op jit(solution)/shard_map/all_to_all | solution.py:372
  78.8 4.8 %shard_map.101 = (bf16[2,64,1024]{2,1,0:T(8,128)(2,1)}, f32[2,64,1024]{2,1,0:T(8,128)S(1)}, bf16[2,64,1024]{2,1,0:T(8,128)(2,1)}) custom-call(s32[1]{0:T(128)} %bitcast.1.place, bf16[2,72,512]{2,1,0:T(8,128)(2,1)} %get-tuple-element.31.grads, bf16[69,1024]{1,0:T(8,128)(2,1)} %w_out.3, bf16[2,512,1024]{2,1,0:T(8,128)(2,1)} %get-tuple-element.32.slope, ...), custom_call_target="tpu_custom_call" | custom-call | flops 536870912 | bytes 4194304 | tf_op jit(solution)/shard_map/pallas_call | solution.py:375
  83.6 2.5 %collective-permute-start.2 = (bf16[2,64,1024]{2,1,0:T(8,128)(2,1)}, bf16[2,64,1024]{2,1,0:T(8,128)(2,1)S(1)}, u32[]{:S(2)}, u32[]{:S(2)}) collective-permute-start(bf16[2,64,1024]{2,1,0:T(8,128)(2,1)} %get-tuple-element.34), channel_id=1, source_target_pairs={{1,0},{2,1},{3,2},{4,3},{5,4},{6,5},{7,6},{8,7},{9,8},{10,9},{11,1... | collective-permute-start | bytes 786440 | tf_op jit(solution)/shard_map/ppermute | solution.py:383
  86.1 3.1 %collective-permute-start.3 = (bf16[2,64,1024]{2,1,0:T(8,128)(2,1)}, bf16[2,64,1024]{2,1,0:T(8,128)(2,1)S(1)}, u32[]{:S(2)}, u32[]{:S(2)}) collective-permute-start(bf16[2,64,1024]{2,1,0:T(8,128)(2,1)} %get-tuple-element.35), channel_id=1, source_target_pairs={{0,1},{1,2},{2,3},{3,4},{4,5},{5,6},{6,7},{7,8},{8,9},{9,10},{10,1... | collective-permute-start | bytes 786440 | tf_op jit(solution)/shard_map/ppermute | solution.py:384
  89.2 9.5 %all-to-all-done.2.parts = bf16[64,4,384]{2,1,0:T(4,128)(2,1)S(1)} async-done(((bf16[64,4,384]{2,1,0:T(4,128)(2,1)}), bf16[64,4,384]{2,1,0:T(4,128)(2,1)S(1)}, u32[]{:S(2)}, u32[]{:S(2)}) %all-to-all-start.2) | async-done | bytes 196640 | tf_op jit(solution)/shard_map/all_to_all | solution.py:372
  98.7 0.7 shard_map.99
  99.4 3.3 %all-to-all-start.3 = ((f32[8,4,384]{2,1,0:T(4,128)}), f32[8,4,384]{2,1,0:T(4,128)S(1)}, u32[]{:S(2)}, u32[]{:S(2)}) async-start(f32[8,4,384]{2,1,0:T(4,128)} %shard_map.99), calls=%async_computation.3 | async-start | bytes 98304 | tf_op jit(solution)/shard_map/all_to_all | solution.py:392
  102.7 0.0 collective-permute-done.2.from_above
  102.7 0.0 collective-permute-done.3.from_below
  102.7 0.0 copy-done
  102.7 1.5 %shard_map.102 = bf16[2,64,1024]{2,1,0:T(8,128)(2,1)} custom-call(f32[2,64,1024]{2,1,0:T(8,128)S(1)} %get-tuple-element.33.middle, bf16[2,64,1024]{2,1,0:T(8,128)(2,1)S(1)} %collective-permute-done.2.from_above, bf16[2,64,1024]{2,1,0:T(8,128)(2,1)S(1)} %collective-permute-done.3.from_below, bf16[1024,1024]{1,0:T(8,128)(2,1)S(1)} %copy-done), custom_call_target="tpu_custom_call" | custom-call | flops 268435456 | bytes 4194304 | tf_op jit(solution)/shard_map/pallas_call | solution.py:385
  104.3 5.0 %all-to-all-done.3.parts = f32[8,4,384]{2,1,0:T(4,128)S(1)} async-done(((f32[8,4,384]{2,1,0:T(4,128)}), f32[8,4,384]{2,1,0:T(4,128)S(1)}, u32[]{:S(2)}, u32[]{:S(2)}) %all-to-all-start.3) | async-done | bytes 49184 | tf_op jit(solution)/shard_map/all_to_all | solution.py:392
  109.3 0.7 shard_map.100
Async XLA Ops:
  0.6 13.8 %collective-permute-start = (bf16[2,64,1024]{2,1,0:T(8,128)(2,1)}, bf16[2,64,1024]{2,1,0:T(8,128)(2,1)S(1)}, u32[]{:S(2)}, u32[]{:S(2)}) collective-permute-start(bf16[2,64,1024]{2,1,0:T(8,128)(2,1)} %own.1), channel_id=1, source_target_pairs={{0,1},{1,2},{2,3},{3,4},{4,5},{5,6},{6,7},{7,8},{8,9},{9,10},{10,1... | collective-permute-start | bytes 786440 | tf_op jit(solution)/shard_map/ppermute | solution.py:293
  5.6 8.9 %collective-permute-start.1 = (bf16[2,64,1024]{2,1,0:T(8,128)(2,1)}, bf16[2,64,1024]{2,1,0:T(8,128)(2,1)S(1)}, u32[]{:S(2)}, u32[]{:S(2)}) collective-permute-start(bf16[2,64,1024]{2,1,0:T(8,128)(2,1)} %own.1), channel_id=1, source_target_pairs={{1,0},{2,1},{3,2},{4,3},{5,4},{6,5},{7,6},{8,7},{9,8},{10,9},{11,1... | collective-permute-start | bytes 786440 | tf_op jit(solution)/shard_map/ppermute | solution.py:294
  17.9 22.2 %all-to-all-start = ((bf16[8,2,72,512]{3,2,1,0:T(8,128)(2,1)}), bf16[8,2,72,512]{3,2,1,0:T(8,128)(2,1)S(1)}, u32[]{:S(2)}, u32[]{:S(2)}) async-start(bf16[8,2,72,512]{3,2,1,0:T(8,128)(2,1)} %get-tuple-element.24), calls=%async_computation | async-start | bytes 2359296 | tf_op jit(solution)/shard_map/all_to_all | solution.py:332
  23.6 16.6 %copy-start.1 = (f32[69,512]{1,0:T(8,128)S(1)}, f32[69,512]{1,0:T(8,128)}, u32[]{:S(2)}) copy-start(f32[69,512]{1,0:T(8,128)} %refs_4_.1) | copy-start | bytes 423940
  74.0 28.7 %copy-start = (bf16[1024,1024]{1,0:T(8,128)(2,1)S(1)}, bf16[1024,1024]{1,0:T(8,128)(2,1)}, u32[]{:S(2)}) copy-start(bf16[1024,1024]{1,0:T(8,128)(2,1)} %w_in.3) | copy-start | bytes 6291460
  74.1 24.6 %all-to-all-start.2 = ((bf16[64,4,384]{2,1,0:T(4,128)(2,1)}), bf16[64,4,384]{2,1,0:T(4,128)(2,1)S(1)}, u32[]{:S(2)}, u32[]{:S(2)}) async-start(bf16[64,4,384]{2,1,0:T(4,128)(2,1)} %get-tuple-element.28), calls=%async_computation.2 | async-start | bytes 393216 | tf_op jit(solution)/shard_map/all_to_all | solution.py:372
  83.6 19.1 %collective-permute-start.2 = (bf16[2,64,1024]{2,1,0:T(8,128)(2,1)}, bf16[2,64,1024]{2,1,0:T(8,128)(2,1)S(1)}, u32[]{:S(2)}, u32[]{:S(2)}) collective-permute-start(bf16[2,64,1024]{2,1,0:T(8,128)(2,1)} %get-tuple-element.34), channel_id=1, source_target_pairs={{1,0},{2,1},{3,2},{4,3},{5,4},{6,5},{7,6},{8,7},{9,8},{10,9},{11,1... | collective-permute-start | bytes 786440 | tf_op jit(solution)/shard_map/ppermute | solution.py:383
  86.1 16.7 %collective-permute-start.3 = (bf16[2,64,1024]{2,1,0:T(8,128)(2,1)}, bf16[2,64,1024]{2,1,0:T(8,128)(2,1)S(1)}, u32[]{:S(2)}, u32[]{:S(2)}) collective-permute-start(bf16[2,64,1024]{2,1,0:T(8,128)(2,1)} %get-tuple-element.35), channel_id=1, source_target_pairs={{0,1},{1,2},{2,3},{3,4},{4,5},{5,6},{6,7},{7,8},{8,9},{9,10},{10,1... | collective-permute-start | bytes 786440 | tf_op jit(solution)/shard_map/ppermute | solution.py:384
  99.4 9.9 %all-to-all-start.3 = ((f32[8,4,384]{2,1,0:T(4,128)}), f32[8,4,384]{2,1,0:T(4,128)S(1)}, u32[]{:S(2)}, u32[]{:S(2)}) async-start(f32[8,4,384]{2,1,0:T(4,128)} %shard_map.99), calls=%async_computation.3 | async-start | bytes 98304 | tf_op jit(solution)/shard_map/all_to_all | solution.py:392

commit v7 on v6

--- a/solution.py
+++ b/solution.py
@@ -31,12 +31,20 @@
     )
 
 
-def mixing(neighbours, weight, first_node, rows):
-    node = lax.broadcasted_iota(jnp.int32, (rows, neighbours.shape[1]), 0) + first_node
+def mixing(neighbours, weight, bands, nodes):
+    row = lax.broadcasted_iota(jnp.int32, (len(bands) * nodes, neighbours.shape[1]), 0)
+    node = row + bands[0] * nodes
+    for k in range(1, len(bands)):
+        node = jnp.where(row >= k * nodes, row + (bands[k] - k) * nodes, node)
     total = jnp.where(node == neighbours[0:1], weight[0:1], 0.0)
     for k in range(1, neighbours.shape[0]):
         total = total + jnp.where(node == neighbours[k : k + 1], weight[k : k + 1], 0.0)
     return total
+
+
+def paired(band):
+    side = 1 - 2 * lax.rem(band, 2)
+    return band + side, band, band - side
 
 
 def prepare(place, own, w_in, w_out, neighbours, weight, weights, rows, spread, mine, w_held, w_sems):
@@ -48,7 +56,7 @@
         loads.append(pltpu.make_async_copy(w_in.at[part], weights.at[part], w_sems.at[index]))
         loads[-1].start()
     nodes = spread.shape[1] // 6
-    mixed = mixing(neighbours[...], weight[...], (place[0] - 1) * nodes, 3 * nodes)
+    mixed = mixing(neighbours[...], weight[...], paired(place[0]), nodes)
     spread[...] = jnp.concatenate([mixed, mixed], axis=0).T.astype(bf16)
     w_held[64:ROWS] = jnp.zeros((ROWS - 64, w_held.shape[1]), f32)
     w_held[0 : w_out.shape[0]] = w_out[...].astype(f32)
@@ -60,17 +68,17 @@
 
 
 def forward(
-    rows_here, before, mine, after, weights, rows, spread,
+    rows_here, near, mine, far, weights, rows, spread,
     sent, projected,
     latents, held, decoded, held_sems, sent_sems,
 ):
-    members, nodes, _ = before.shape
+    members, nodes, _ = near.shape
     slots = spread.shape[0]
     step = 512
     around = 3 * nodes
     both = members * nodes
-    latents[:both] = before[...].reshape(both, -1)
-    latents[both:] = after[...].reshape(both, -1)
+    latents[:both] = near[...].reshape(both, -1)
+    latents[both:] = far[...].reshape(both, -1)
     whole = jnp.dot(latents[...], weights[...], preferred_element_type=f32)
     for k, source in enumerate((whole[:both], mine[...], whole[both:])):
         high = source.astype(bf16)
@@ -104,7 +112,7 @@
     slots = neighbours.shape[1]
     step = 128
     nodes = projected.shape[1] // 6
-    spread = mixing(neighbours[...], weight[...], (place[0] - 1) * nodes, 3 * nodes)
+    spread = mixing(neighbours[...], weight[...], paired(place[0]), nodes)
     spread = jnp.concatenate([spread, spread], axis=0).T.astype(bf16)
     copies = []
     for m in range(members):
@@ -233,10 +241,10 @@
     w_rows[64:ROWS] = jnp.zeros((ROWS - 64, width), f32)
     w_rows[0:variables] = w_out[...].astype(f32)
     rows = w_rows[...].astype(bf16)
-    first = (place[0] - 1) * nodes
     slots = neighbours.shape[1]
     step = 128
-    spread = mixing(neighbours[...], weight[...], first, 3 * nodes).astype(bf16)
+    band = place[0]
+    spread = mixing(neighbours[...], weight[...], (band - 1, band, band + 1), nodes).astype(bf16)
     for m in range(held):
         total = None
         lines = grads[m].astype(f32).T.astype(bf16)
@@ -290,8 +298,10 @@
     group = lax.axis_index("member").astype(jnp.int32)
     up = [(i, i + 1) for i in range(bands - 1)]
     down = [(i + 1, i) for i in range(bands - 1)]
-    before = lax.ppermute(latent, "space", up)
-    after = lax.ppermute(latent, "space", down)
+    pairs = [(i, i + 1 - 2 * (i % 2)) for i in range(bands)]
+    across = [(i, i - 1 + 2 * (i % 2)) for i in range(1, bands - 1)]
+    near = lax.ppermute(latent, "space", pairs)
+    far = lax.ppermute(latent, "space", across)
     where = band.reshape(1)
     mine_at = (group * members_dev).reshape(1)
 
@@ -327,7 +337,7 @@
             pltpu.SemaphoreType.DMA((members_dev, groups)),
         ],
         flops=1 << 30, moved=8 << 20,
-    )(band_rows, before, mine, after, weights, rows, spread)
+    )(band_rows, near, mine, far, weights, rows, spread)
 
     everyone = lax.all_to_all(sent, "member", 0, 0, tiled=True).reshape(members, ROWS, slots)
     hidden, slope, done = call(

time: 111 us -> 110 us (level)
  waiting for transfers between devices: 26.7 us -> 28.1 us
  starting transfers between devices: 29.4 us -> 28 us
    ppermute x2, waiting for transfers between devices: 0.01 us -> 2.25 us  [the longest x1 2.25 us: per_device(): far = lax.ppermute(latent, 'space', across)]
    all_to_all x1, starting transfers between devices: 5.67 us -> 3.58 us  [per_device(): lax.all_to_all(sent, 'member', 0, 0, tiled=True)]
  transfers between devices with their start and end apart: 7 -> 7, of which waited for: 3 -> 4; matrix products, arithmetic and copies ran while one was open for 0% -> 0% of each run, Pallas kernels for 13% -> 13%
where the time goes in v7:
time: 110 us
  blocking collectives  30.5 us (28%)
  waiting for transfers between devices  28.1 us (26%)
  starting transfers between devices  28 us (25%)
  Pallas kernels  21.6 us (20%)
  between operations  1.43 us (1%)
    all_to_all x1, blocking collectives, per_device(): sums = lax.all_to_all(sums, 'space', 0, 0, tiled=True)  30.5 us
    all_to_all x1, waiting for transfers between devices, per_device(): lax.all_to_all(sent, 'member', 0, 0, tiled=True)  11.4 us
    all_to_all x1, waiting for transfers between devices, per_device(): weight_parts = lax.all_to_all(weight_parts, 'space', 0, 0, tiled=True)  9.49 us
    ppermute x1, starting transfers between devices, per_device(): near = lax.ppermute(latent, 'space', pairs)  8.79 us
    all_to_all x1, waiting for transfers between devices, per_device(): total = lax.all_to_all(total, 'member', 0, 0, tiled=True)  5.02 us
    all_to_all x1, starting transfers between devices, per_device(): weight_parts = lax.all_to_all(weight_parts, 'space', 0, 0, tiled=True)  4.78 us
    pallas_call x1, Pallas kernels, per_device(): call(backward, (pltpu.VMEM(small, bf16), pltpu.VMEM(small, f32), pltpu.VM...  4.76 us
    pallas_call x1, Pallas kernels, per_device(): call(activations, (pltpu.VMEM(big, bf16), pltpu.HBM(big, bf16), shape((8,...  4.41 us
  transfers between devices with their start and end apart: 7, of which 4 were waited for; matrix products, arithmetic and copies ran while one was open for 0% of the time, Pallas kernels for 13%

profile of v7, /device:TPU:1, one launch (start us, length us, event | category | flops | bytes accessed | tf_op | source)
XLA Modules:
  0.0 109.6 jit_solution(1029701638821774260)
XLA Ops:
  0.6 8.8 %collective-permute-start = (bf16[2,64,1024]{2,1,0:T(8,128)(2,1)}, bf16[2,64,1024]{2,1,0:T(8,128)(2,1)S(1)}, u32[]{:S(2)}, u32[]{:S(2)}) collective-permute-start(bf16[2,64,1024]{2,1,0:T(8,128)(2,1)} %own.1), channel_id=1, source_target_pairs={{0,1},{1,0},{2,3},{3,2},{4,5},{5,4},{6,7},{7,6},{8,9},{9,8},{10,11... | collective-permute-start | bytes 786440 | tf_op jit(solution)/shard_map/ppermute | solution.py:303
  9.4 1.9 %collective-permute-start.1 = (bf16[2,64,1024]{2,1,0:T(8,128)(2,1)}, bf16[2,64,1024]{2,1,0:T(8,128)(2,1)S(1)}, u32[]{:S(2)}, u32[]{:S(2)}) collective-permute-start(bf16[2,64,1024]{2,1,0:T(8,128)(2,1)} %own.1), channel_id=1, source_target_pairs={{1,2},{2,1},{3,4},{4,3},{5,6},{6,5},{7,8},{8,7},{9,10},{10,9},{11,... | collective-permute-start | bytes 786440 | tf_op jit(solution)/shard_map/ppermute | solution.py:304
  12.0 3.1 %shard_map.94 = (bf16[1024,1024]{1,0:T(8,128)(2,1)S(1)}, bf16[72,1024]{1,0:T(8,128)(2,1)S(1)}, bf16[512,384]{1,0:T(8,128)(2,1)S(1)}, f32[128,1024]{1,0:T(8,128)S(1)}) custom-call(s32[1]{0:T(128)} %bitcast.1.place, bf16[2,64,1024]{2,1,0:T(8,128)(2,1)} %own.1, bf16[1024,1024]{1,0:T(8,128)(2,1)} %w_in.3, bf16[69,1024]{1,0:T(8,128)(2,1)} %w_out.3, ...), custom_call_target="tpu_custom_call" | custom-call | flops 268435456 | bytes 4194304 | tf_op jit(solution)/shard_map/pallas_call | solution.py:316
  15.1 0.0 collective-permute-done.near
  15.1 2.3 %collective-permute-done.1.far = bf16[2,64,1024]{2,1,0:T(8,128)(2,1)S(1)} collective-permute-done((bf16[2,64,1024]{2,1,0:T(8,128)(2,1)}, bf16[2,64,1024]{2,1,0:T(8,128)(2,1)S(1)}, u32[]{:S(2)}, u32[]{:S(2)}) %collective-permute-start.1) | collective-permute-done | bytes 262176 | tf_op jit(solution)/shard_map/ppermute | solution.py:304
  17.3 3.4 %shard_map.95 = (bf16[8,2,72,512]{3,2,1,0:T(8,128)(2,1)}, bf16[2,384,1024]{2,1,0:T(8,128)(2,1)}) custom-call(s32[1]{0:T(128)S(6)} %copy.11.rows_here.refs_1_, bf16[2,64,1024]{2,1,0:T(8,128)(2,1)S(1)} %collective-permute-done.near, f32[128,1024]{1,0:T(8,128)S(1)} %get-tuple-element.20.mine, bf16[2,64,1024]{2,1,0:T(8,128)(2,1)S(1)} %collective-permute-done.1.far, ...), custom_call_target="tpu_custom_call" | custom-call | flops 1073741824 | bytes 8388608 | tf_op jit(solution)/shard_map/pallas_call | solution.py:327
  20.8 3.6 %all-to-all-start = ((bf16[8,2,72,512]{3,2,1,0:T(8,128)(2,1)}), bf16[8,2,72,512]{3,2,1,0:T(8,128)(2,1)S(1)}, u32[]{:S(2)}, u32[]{:S(2)}) async-start(bf16[8,2,72,512]{3,2,1,0:T(8,128)(2,1)} %get-tuple-element.24), calls=%async_computation | async-start | bytes 2359296 | tf_op jit(solution)/shard_map/all_to_all | solution.py:342
  24.3 0.0 copy-start.1
  24.4 4.4 %shard_map.96 = (bf16[2,512,1024]{2,1,0:T(8,128)(2,1)S(1)}, bf16[2,512,1024]{2,1,0:T(8,128)(2,1)}, f32[8,128]{1,0:T(8,128)S(1)}) custom-call(s32[1]{0:T(128)} %bitcast.1.place, bf16[2,384,1024]{2,1,0:T(8,128)(2,1)} %get-tuple-element.25.projected, s32[3,512]{1,0:T(4,128)} %neighbours.5, f32[3,512]{1,0:T(4,128)} %weight.5), custom_call_target="tpu_custom_call" | custom-call | flops 1073741824 | bytes 8388608 | tf_op jit(solution)/shard_map/pallas_call | solution.py:343
  28.8 11.4 %all-to-all-done = bf16[8,2,72,512]{3,2,1,0:T(8,128)(2,1)S(1)} async-done(((bf16[8,2,72,512]{3,2,1,0:T(8,128)(2,1)}), bf16[8,2,72,512]{3,2,1,0:T(8,128)(2,1)S(1)}, u32[]{:S(2)}, u32[]{:S(2)}) %all-to-all-start) | async-done | bytes 1179680 | tf_op jit(solution)/shard_map/all_to_all | solution.py:342
  40.1 0.0 copy-done.1
  40.1 0.8 shard_map.97
  40.9 30.5 %all_to_all.26 = f32[64,1,128]{2,1,0:T(1,128)S(1)} all-to-all(f32[64,1,128]{2,1,0:T(1,128)S(1)} %bitcast.12), channel_id=1, replica_groups=mesh['member'=8,'space'=64] {'space'}, dimensions={0} | all-to-all | bytes 65536 | tf_op jit(solution)/shard_map/all_to_all | solution.py:359
  71.4 2.2 %shard_map.98 = (bf16[2,72,512]{2,1,0:T(8,128)(2,1)}, bf16[64,4,384]{2,1,0:T(4,128)(2,1)}, f32[8,128]{1,0:T(8,128)S(1)}) custom-call(s32[1]{0:T(128)} %bitcast.refs_0_, s32[1]{0:T(128)S(6)} %copy.11.rows_here.refs_1_, f32[64,128]{1,0:T(8,128)S(1)} %bitcast.11, bf16[16,72,512]{2,1,0:T(8,128)(2,1)S(1)} %bitcast.10, f32[69,512]{1,0:T(8,128)S(1)} %copy-done.1, ...), custom_call_target="tpu_custom_call" | custom-call | flops 268435456 | bytes 4194304 | tf_op jit(solution)/shard_map/pallas_call | solution.py:367
  73.7 0.0 copy-start
  73.7 4.8 %all-to-all-start.2 = ((bf16[64,4,384]{2,1,0:T(4,128)(2,1)}), bf16[64,4,384]{2,1,0:T(4,128)(2,1)S(1)}, u32[]{:S(2)}, u32[]{:S(2)}) async-start(bf16[64,4,384]{2,1,0:T(4,128)(2,1)} %get-tuple-element.28), calls=%async_computation.2 | async-start | bytes 393216 | tf_op jit(solution)/shard_map/all_to_all | solution.py:382
  78.5 4.8 %shard_map.101 = (bf16[2,64,1024]{2,1,0:T(8,128)(2,1)}, f32[2,64,1024]{2,1,0:T(8,128)S(1)}, bf16[2,64,1024]{2,1,0:T(8,128)(2,1)}) custom-call(s32[1]{0:T(128)} %bitcast.1.place, bf16[2,72,512]{2,1,0:T(8,128)(2,1)} %get-tuple-element.31.grads, bf16[69,1024]{1,0:T(8,128)(2,1)} %w_out.3, bf16[2,512,1024]{2,1,0:T(8,128)(2,1)} %get-tuple-element.32.slope, ...), custom_call_target="tpu_custom_call" | custom-call | flops 536870912 | bytes 4194304 | tf_op jit(solution)/shard_map/pallas_call | solution.py:385
  83.2 2.5 %collective-permute-start.2 = (bf16[2,64,1024]{2,1,0:T(8,128)(2,1)}, bf16[2,64,1024]{2,1,0:T(8,128)(2,1)S(1)}, u32[]{:S(2)}, u32[]{:S(2)}) collective-permute-start(bf16[2,64,1024]{2,1,0:T(8,128)(2,1)} %get-tuple-element.34), channel_id=1, source_target_pairs={{1,0},{2,1},{3,2},{4,3},{5,4},{6,5},{7,6},{8,7},{9,8},{10,9},{11,1... | collective-permute-start | bytes 786440 | tf_op jit(solution)/shard_map/ppermute | solution.py:393
  85.7 3.1 %collective-permute-start.3 = (bf16[2,64,1024]{2,1,0:T(8,128)(2,1)}, bf16[2,64,1024]{2,1,0:T(8,128)(2,1)S(1)}, u32[]{:S(2)}, u32[]{:S(2)}) collective-permute-start(bf16[2,64,1024]{2,1,0:T(8,128)(2,1)} %get-tuple-element.35), channel_id=1, source_target_pairs={{0,1},{1,2},{2,3},{3,4},{4,5},{5,6},{6,7},{7,8},{8,9},{9,10},{10,1... | collective-permute-start | bytes 786440 | tf_op jit(solution)/shard_map/ppermute | solution.py:394
  88.8 9.5 %all-to-all-done.2.parts = bf16[64,4,384]{2,1,0:T(4,128)(2,1)S(1)} async-done(((bf16[64,4,384]{2,1,0:T(4,128)(2,1)}), bf16[64,4,384]{2,1,0:T(4,128)(2,1)S(1)}, u32[]{:S(2)}, u32[]{:S(2)}) %all-to-all-start.2) | async-done | bytes 196640 | tf_op jit(solution)/shard_map/all_to_all | solution.py:382
  98.3 0.7 shard_map.99
  99.0 3.3 %all-to-all-start.3 = ((f32[8,4,384]{2,1,0:T(4,128)}), f32[8,4,384]{2,1,0:T(4,128)S(1)}, u32[]{:S(2)}, u32[]{:S(2)}) async-start(f32[8,4,384]{2,1,0:T(4,128)} %shard_map.99), calls=%async_computation.3 | async-start | bytes 98304 | tf_op jit(solution)/shard_map/all_to_all | solution.py:402
  102.3 0.0 collective-permute-done.2.from_above
  102.4 0.0 collective-permute-done.3.from_below
  102.4 0.0 copy-done
  102.4 1.5 %shard_map.102 = bf16[2,64,1024]{2,1,0:T(8,128)(2,1)} custom-call(f32[2,64,1024]{2,1,0:T(8,128)S(1)} %get-tuple-element.33.middle, bf16[2,64,1024]{2,1,0:T(8,128)(2,1)S(1)} %collective-permute-done.2.from_above, bf16[2,64,1024]{2,1,0:T(8,128)(2,1)S(1)} %collective-permute-done.3.from_below, bf16[1024,1024]{1,0:T(8,128)(2,1)S(1)} %copy-done), custom_call_target="tpu_custom_call" | custom-call | flops 268435456 | bytes 4194304 | tf_op jit(solution)/shard_map/pallas_call | solution.py:395
  103.9 5.0 %all-to-all-done.3.parts = f32[8,4,384]{2,1,0:T(4,128)S(1)} async-done(((f32[8,4,384]{2,1,0:T(4,128)}), f32[8,4,384]{2,1,0:T(4,128)S(1)}, u32[]{:S(2)}, u32[]{:S(2)}) %all-to-all-start.3) | async-done | bytes 49184 | tf_op jit(solution)/shard_map/all_to_all | solution.py:402
  108.9 0.7 shard_map.100
Async XLA Ops:
  0.6 14.4 %collective-permute-start = (bf16[2,64,1024]{2,1,0:T(8,128)(2,1)}, bf16[2,64,1024]{2,1,0:T(8,128)(2,1)S(1)}, u32[]{:S(2)}, u32[]{:S(2)}) collective-permute-start(bf16[2,64,1024]{2,1,0:T(8,128)(2,1)} %own.1), channel_id=1, source_target_pairs={{0,1},{1,0},{2,3},{3,2},{4,5},{5,4},{6,7},{7,6},{8,9},{9,8},{10,11... | collective-permute-start | bytes 786440 | tf_op jit(solution)/shard_map/ppermute | solution.py:303
  9.4 7.9 %collective-permute-start.1 = (bf16[2,64,1024]{2,1,0:T(8,128)(2,1)}, bf16[2,64,1024]{2,1,0:T(8,128)(2,1)S(1)}, u32[]{:S(2)}, u32[]{:S(2)}) collective-permute-start(bf16[2,64,1024]{2,1,0:T(8,128)(2,1)} %own.1), channel_id=1, source_target_pairs={{1,2},{2,1},{3,4},{4,3},{5,6},{6,5},{7,8},{8,7},{9,10},{10,9},{11,... | collective-permute-start | bytes 786440 | tf_op jit(solution)/shard_map/ppermute | solution.py:304
  20.8 19.4 %all-to-all-start = ((bf16[8,2,72,512]{3,2,1,0:T(8,128)(2,1)}), bf16[8,2,72,512]{3,2,1,0:T(8,128)(2,1)S(1)}, u32[]{:S(2)}, u32[]{:S(2)}) async-start(bf16[8,2,72,512]{3,2,1,0:T(8,128)(2,1)} %get-tuple-element.24), calls=%async_computation | async-start | bytes 2359296 | tf_op jit(solution)/shard_map/all_to_all | solution.py:342
  24.3 15.8 %copy-start.1 = (f32[69,512]{1,0:T(8,128)S(1)}, f32[69,512]{1,0:T(8,128)}, u32[]{:S(2)}) copy-start(f32[69,512]{1,0:T(8,128)} %refs_4_.1) | copy-start | bytes 423940
  73.7 28.7 %copy-start = (bf16[1024,1024]{1,0:T(8,128)(2,1)S(1)}, bf16[1024,1024]{1,0:T(8,128)(2,1)}, u32[]{:S(2)}) copy-start(bf16[1024,1024]{1,0:T(8,128)(2,1)} %w_in.3) | copy-start | bytes 6291460
  73.7 24.6 %all-to-all-start.2 = ((bf16[64,4,384]{2,1,0:T(4,128)(2,1)}), bf16[64,4,384]{2,1,0:T(4,128)(2,1)S(1)}, u32[]{:S(2)}, u32[]{:S(2)}) async-start(bf16[64,4,384]{2,1,0:T(4,128)(2,1)} %get-tuple-element.28), calls=%async_computation.2 | async-start | bytes 393216 | tf_op jit(solution)/shard_map/all_to_all | solution.py:382
  83.2 19.1 %collective-permute-start.2 = (bf16[2,64,1024]{2,1,0:T(8,128)(2,1)}, bf16[2,64,1024]{2,1,0:T(8,128)(2,1)S(1)}, u32[]{:S(2)}, u32[]{:S(2)}) collective-permute-start(bf16[2,64,1024]{2,1,0:T(8,128)(2,1)} %get-tuple-element.34), channel_id=1, source_target_pairs={{1,0},{2,1},{3,2},{4,3},{5,4},{6,5},{7,6},{8,7},{9,8},{10,9},{11,1... | collective-permute-start | bytes 786440 | tf_op jit(solution)/shard_map/ppermute | solution.py:393
  85.7 16.7 %collective-permute-start.3 = (bf16[2,64,1024]{2,1,0:T(8,128)(2,1)}, bf16[2,64,1024]{2,1,0:T(8,128)(2,1)S(1)}, u32[]{:S(2)}, u32[]{:S(2)}) collective-permute-start(bf16[2,64,1024]{2,1,0:T(8,128)(2,1)} %get-tuple-element.35), channel_id=1, source_target_pairs={{0,1},{1,2},{2,3},{3,4},{4,5},{5,6},{6,7},{7,8},{8,9},{9,10},{10,1... | collective-permute-start | bytes 786440 | tf_op jit(solution)/shard_map/ppermute | solution.py:394
  99.0 9.9 %all-to-all-start.3 = ((f32[8,4,384]{2,1,0:T(4,128)}), f32[8,4,384]{2,1,0:T(4,128)S(1)}, u32[]{:S(2)}, u32[]{:S(2)}) async-start(f32[8,4,384]{2,1,0:T(4,128)} %shard_map.99), calls=%async_computation.3 | async-start | bytes 98304 | tf_op jit(solution)/shard_map/all_to_all | solution.py:402
